TPU v7x, 256 devices: a whole 4x4x8 slice. The times are simulated.
256 devices in a mesh: fsdp: 32 (over z_hi, x, core), tp: 8 (over y, z_lo).
Axes of the slice: x: 4, y: 4, z: 8 (z_hi: 4, z_lo: 2; z = z_hi * 2 + z_lo), core: 2. Of those that a mesh axis runs over, the one named last changes fastest.
Arguments:
- activations: bfloat16 [8192, 8192], P('fsdp'), may hold values from -6 to 6
- grad_output: bfloat16 [8192, 28672], P('fsdp', 'tp'), may hold values from -0.1875 to 0.1875
- projector: bfloat16 [8192, 1024], P('fsdp'), may hold values from -0.125 to 0.125
- first_moment: float32 [1024, 28672], P('fsdp', 'tp'), may hold values from -0.625 to 0.625
- second_moment: float32 [1024, 28672], P('fsdp', 'tp'), may hold values from 0.01 to 0.5
Outputs:
- new_first: float32 [1024, 28672], P('fsdp', 'tp')
- new_second: float32 [1024, 28672], P('fsdp', 'tp')
- weight_update: bfloat16 [8192, 28672], P('fsdp', 'tp')
All inputs are finite; a program needn't handle non-finite values.
Results may differ from a plain program's by a relative error of at most 0.0059.
Values may be sent and summed in bfloat16 or wider, within the bound.
No kernel may reach another device: no remote copies, remote signals or barrier semaphores. Data moves between devices by JAX's collectives and lax.ppermute only.
A program may use at most 64 MiB of HBM per device.

v0:
```python
import functools

import jax
import jax.numpy as jnp
from jax import lax
from jax.experimental import pallas as pl
from jax.experimental.pallas import tpu as pltpu
from jax.sharding import PartitionSpec as P

first_fix = 0.9999734386011124
second_fix = 0.6339676587267705
BF = jnp.bfloat16
F32 = jnp.float32
MIB = 2**20


def swap(array, axis, masks):
    inner = lax.axis_size("tp")
    count = lax.axis_size("fsdp") * inner
    scale = inner if axis == "fsdp" else 1
    return lax.ppermute(
        array, ("fsdp", "tp"), [(i, i ^ (scale * masks[i // inner % 2])) for i in range(count)]
    )


def swap_core(array):
    return swap(array, "fsdp", (1, 1))


def doubled(masks):
    order = [0]
    for mask in masks:
        order = order + [o ^ mask for o in order]
    return order


def table(core, orders):
    first, second = (jnp.array(order, dtype=jnp.int32) for order in orders)
    return jnp.where(core == 0, first, second)


def by_core(core, own, other, axis):
    return jnp.where(
        core == 0,
        jnp.concatenate([own, other], axis=axis),
        jnp.concatenate([other, own], axis=axis),
    )


def call(kernel, outs, args, flops=0, vmem=8, scratch=(), smem=0, after=()):
    moved = sum(a.size * a.dtype.itemsize for a in args)
    moved += sum(o.size * o.dtype.itemsize for o in outs)
    specs = [
        pl.BlockSpec(memory_space=pltpu.SMEM if i < smem else pltpu.VMEM)
        for i in range(len(args))
    ]
    count = len(args)

    def body(*refs):
        kernel(*refs[:count], *refs[count + len(after) :])

    specs += [pl.BlockSpec(memory_space=pl.ANY) for _ in after]
    return pl.pallas_call(
        body,
        out_shape=list(outs),
        in_specs=specs,
        out_specs=[pl.BlockSpec(memory_space=pltpu.VMEM) for _ in outs],
        scratch_shapes=list(scratch),
        compiler_params=pltpu.CompilerParams(vmem_limit_bytes=vmem * MIB),
        cost_estimate=pl.CostEstimate(flops=flops, bytes_accessed=moved, transcendentals=0),
    )(*args, *after)


def shape(rows, columns, kind):
    return jax.ShapeDtypeStruct((rows, columns), kind)


def with_mark(kernel):
    def body(*refs):
        refs[-1][...] = jnp.zeros(refs[-1].shape, refs[-1].dtype)
        kernel(*refs[:-1])

    return body


def stack_kernel(sizes, *refs):
    outs = refs[sum(sizes) :]
    at = 0
    for size, out_ref in zip(sizes, outs):
        row = 0
        for ref in refs[at : at + size]:
            out_ref[row : row + ref.shape[0], :] = ref[...]
            row += ref.shape[0]
        at += size


def stack(groups):
    outs = [shape(sum(a.shape[0] for a in g), g[0].shape[1], g[0].dtype) for g in groups]
    return call(
        functools.partial(stack_kernel, [len(g) for g in groups]),
        outs,
        [a for g in groups for a in g],
    )


def stack_marked(groups, after):
    outs = [shape(sum(a.shape[0] for a in g), g[0].shape[1], g[0].dtype) for g in groups]
    *result, mark = call(
        with_mark(functools.partial(stack_kernel, [len(g) for g in groups])),
        [*outs, shape(8, 128, F32)],
        [a for g in groups for a in g],
        after=after,
    )
    return result, mark


def reorder_kernel(width, index_ref, in_ref, out_ref):
    for k in range(out_ref.shape[1] // width):
        start = pl.multiple_of(index_ref[k] * width, width)
        out_ref[:, k * width : (k + 1) * width] = in_ref[:, pl.ds(start, width)]


def reorder(array, index, width):
    outs = [shape(array.shape[0], array.shape[1], array.dtype)]
    return call(
        functools.partial(reorder_kernel, width), outs, [index, array], vmem=8, smem=1
    )[0]


def sums_kernel(count, block, index_ref, own_ref, other_ref, grads_ref, *refs):
    outs, chosen = refs[:count], refs[count]
    tokens = own_ref.shape[1]
    at = 0
    for part, out_ref in enumerate(outs):
        blocks = out_ref.shape[0] // block
        for k in range(blocks):
            row = slice(k * block, (k + 1) * block)
            start = pl.multiple_of(index_ref[part * blocks + k] * block, block)
            chosen[row, :tokens] = own_ref[pl.ds(start, block), :]
            chosen[row, tokens:] = other_ref[pl.ds(start, block), :]
        width = out_ref.shape[1]
        out_ref[...] = jnp.dot(
            chosen[...], grads_ref[:, at : at + width], preferred_element_type=F32
        ).astype(out_ref.dtype)
        at += width


def partial_sums(index, own, other, grads, rows, widths, block, kind, after=()):
    return call(
        functools.partial(sums_kernel, len(widths), block),
        [shape(rows, w, kind) for w in widths],
        [index, own, other, grads],
        flops=2 * rows * grads.size,
        vmem=8,
        scratch=[pltpu.VMEM((rows, 2 * own.shape[1]), BF)],
        smem=1,
        after=after,
    )


def halve_kernel(count, *refs):
    kept, got, kept_out, sent = (refs[i * count : (i + 1) * count] for i in range(4))
    for k, g, o, s in zip(kept, got, kept_out, sent):
        rows = o.shape[0]
        s[...] = (k[rows:, :] + g[rows:, :].astype(F32)).astype(s.dtype)
        o[...] = k[:rows, :] + g[:rows, :].astype(F32)


def halve(kept, got, after):
    rows = kept[0].shape[0] // 2
    outs = [shape(rows, k.shape[1], kind) for kind in (F32, BF) for k in kept]
    *result, mark = call(
        with_mark(functools.partial(halve_kernel, len(kept))),
        [*outs, shape(8, 128, F32)],
        [*kept, *got],
        after=after,
    )
    return result[: len(kept)], result[len(kept) :], mark


def adam_kernel(count, *refs):
    kept, got = refs[:count], refs[count : 2 * count]
    first_ref, second_ref = refs[2 * count : 2 * count + 2]
    new_first_ref, new_second_ref = refs[2 * count + 2 : 2 * count + 4]
    directions = refs[2 * count + 4 :]
    at = 0
    for k, g, d in zip(kept, got, directions):
        span = slice(at, at + k.shape[1])
        at += k.shape[1]
        lowrank = k[...] + g[...].astype(F32)
        new_first = 0.9 * first_ref[:, span] + 0.1 * lowrank
        new_second = 0.99 * second_ref[:, span] + 0.01 * lowrank * lowrank
        new_first_ref[:, span] = new_first
        new_second_ref[:, span] = new_second
        d[...] = (new_first / first_fix / (jnp.sqrt(new_second / second_fix) + 1e-08)).astype(
            d.dtype
        )


def adam(kept, got, first, second, after):
    outs = [shape(*first.shape, F32)] * 2 + [shape(*k.shape, BF) for k in kept]
    result = call(
        functools.partial(adam_kernel, len(kept)),
        outs,
        [*kept, *got, first, second],
        after=after,
    )
    return result[0], result[1], result[2:]


def pick_kernel(which_ref, first_ref, second_ref, out_ref):
    rows = out_ref.shape[0] // 2
    start = pl.multiple_of(which_ref[0] * rows, rows)
    out_ref[:rows, :] = first_ref[pl.ds(start, rows), :]
    out_ref[rows:, :] = second_ref[pl.ds(start, rows), :]


def join_kernel(core_ref, first_ref, second_ref, other_ref, out_first_ref, out_second_ref):
    rows, half = out_first_ref.shape[0], first_ref.shape[1]
    core = core_ref[0]
    start = pl.multiple_of(core * rows, rows)
    own = pl.ds(pl.multiple_of(core * half, half), half)
    other = pl.ds(pl.multiple_of((1 - core) * half, half), half)
    out_first_ref[:, own] = first_ref[pl.ds(start, rows), :]
    out_first_ref[:, other] = other_ref[:rows, :]
    out_second_ref[:, own] = second_ref[pl.ds(start, rows), :]
    out_second_ref[:, other] = other_ref[rows:, :]


def early_kernel(count, *refs):
    factors, parts, out_ref = refs[:count], refs[count : 2 * count], refs[2 * count]
    at = 0
    for f, p in zip(factors, parts):
        depth, width = p.shape
        out_ref[:, at : at + width] = jnp.dot(
            f[:, :depth], p[...], preferred_element_type=F32
        )
        at += width


def late_kernel(count, row, at, *refs):
    factors, parts, sum_ref, out_ref = (
        refs[:count],
        refs[count : 2 * count],
        refs[2 * count],
        refs[2 * count + 1],
    )
    rows = out_ref.shape[0]
    to = 0
    for f, p in zip(factors, parts):
        depth, width = p.shape
        product = jnp.dot(f[row : row + rows, depth:], p[...], preferred_element_type=F32)
        out_ref[:, to : to + width] = (
            sum_ref[row : row + rows, at : at + width] + product
        ).astype(out_ref.dtype)
        at += width
        to += width


def body(activations, grad_output, projector, first_moment, second_moment):
    place = lax.axis_index("fsdp").astype(jnp.int32)
    tp_place = lax.axis_index("tp").astype(jnp.int32)
    core = place & 1
    chip = place >> 1
    tokens, width = grad_output.shape
    half = width // 2
    rank = projector.shape[1]
    block = rank // 16
    column_count = rank // 8
    wide = half * 5 // 7
    widths = (wide, half - wide)
    rows = first_moment.shape[0]

    def my_half(array):
        return lax.dynamic_slice_in_dim(array, core * half, half, 1)

    def other_half(array):
        return lax.dynamic_slice_in_dim(array, (1 - core) * half, half, 1)

    columns = lax.dynamic_slice_in_dim(projector, tp_place * column_count, column_count, 1)
    for masks in ((8, 16, 24), (2, 4, 6)):
        columns = stack([[columns] + [swap(columns, "fsdp", (m, m)) for m in masks]])[0]
    columns_other = swap_core(columns)
    order = jnp.array([x + z for x in (0, 2, 4, 6) for z in (0, 8, 16, 24)], jnp.int32)
    index = jnp.concatenate([place ^ order, place ^ 1 ^ order])
    act = reorder(activations, index, projector.shape[0])
    depth = columns.shape[0]
    dims = (((0,), (1,)), ((), ()))
    own = lax.dot_general(columns, act[:, :depth], dims, preferred_element_type=F32)
    own = own + lax.dot_general(columns_other, act[:, depth:], dims, preferred_element_type=F32)
    own = own.astype(BF)

    coords = stack([[own, swap(own, "tp", (1, 1))]])[0]
    coords = stack([[coords] + [swap(coords, "tp", (m, m)) for m in (2, 4, 6)]])[0]
    coords_other = swap_core(coords)

    grads = jnp.concatenate(
        [my_half(grad_output), swap_core(other_half(grad_output))], axis=0
    )
    moments = jnp.concatenate([first_moment, second_moment], axis=0)
    moments_other = swap_core(other_half(moments))
    moments_own = my_half(moments)
    first = by_core(core, moments_own[:rows], moments_other[:rows], 0)
    second = by_core(core, moments_own[rows:], moments_other[rows:], 0)
    both = jnp.concatenate([projector, swap_core(projector)], axis=0)

    sum_orders = (([1, 3, 4, 12], [3, 1, 12, 4]), ([4, 12, 1, 3], [12, 4, 3, 1]))
    back_orders = [[o[::-1] for o in orders] for orders in sum_orders]
    keep_index, send_index = [], []
    for orders in sum_orders:
        wanted = chip ^ table(core, [doubled(o[::-1]) for o in orders])
        position = 2 * (tp_place ^ (wanted >> 1)) + (wanted & 1)
        keep_index.append(position[:8])
        send_index.append(position[8:])
    ranks = jnp.arange(rank, dtype=jnp.int32)
    factors = []
    for orders in back_orders:
        blocks = chip ^ table(core, [doubled(o) for o in orders])
        wanted = (blocks[:, None] * block + ranks[None, :block]).reshape(-1)
        choose = (ranks[:, None] == wanted[None, :]).astype(BF)
        factors.append(jnp.dot(both, choose, preferred_element_type=F32).astype(BF))

    def exchange(arrays, orders_of, stage):
        return [
            swap(a, "fsdp", [2 * o[stage] for o in orders]) for a, orders in zip(arrays, orders_of)
        ]

    arrays = (coords, coords_other, grads, rank // 2, widths, block)
    sent = partial_sums(jnp.concatenate(send_index), *arrays, BF)
    kept = partial_sums(jnp.concatenate(keep_index), *arrays, F32)
    marks = []
    for stage in range(3):
        kept, sent, mark = halve(kept, exchange(sent, sum_orders, stage), marks)
        marks = [swap_core(mark)]
    got = exchange(sent, sum_orders, 3)
    new_first, new_second, parts = adam(kept, got, first, second, [*factors, *marks])

    states_other = swap_core(
        call(
            pick_kernel,
            [shape(2 * rows, half, F32)],
            [(1 - core)[None], new_first, new_second],
            smem=1,
        )[0]
    )
    out_first, out_second, joined = call(
        with_mark(join_kernel),
        [shape(rows, width, F32)] * 2 + [shape(8, 128, F32)],
        [core[None], new_first, new_second, states_other],
        smem=1,
    )
    marks = [states_other]
    for stage in range(4):
        got = exchange(parts, back_orders, stage)
        if stage == 1:
            marks = [*marks, joined]
        if stage < 3:
            parts, mark = stack_marked([[p, g] for p, g in zip(parts, got)], marks)
            marks = [swap_core(mark)]
    count = len(parts)
    flops = rank * half * both.shape[0]
    early = call(
        functools.partial(early_kernel, count),
        [shape(both.shape[0], half, F32)],
        [*factors, *parts],
        flops=flops,
        vmem=8,
        after=marks,
    )[0]

    def late(row, parts, after=()):
        at = sum(widths[: parts.start])
        span = sum(widths[parts])
        return call(
            functools.partial(late_kernel, len(widths[parts]), row, at),
            [shape(tokens, span, BF)],
            [*factors[parts], *got[parts], early],
            flops=rank * tokens * span,
            after=after,
        )[0]

    every = slice(0, count)
    other = swap_core(late(tokens, every))
    update = by_core(core, late(0, every), other, 1)
    return (out_first, out_second, update)


def solution(mesh):
    return jax.shard_map(
        body,
        mesh=mesh,
        in_specs=(
            P("fsdp", None),
            P("fsdp", "tp"),
            P("fsdp", None),
            P("fsdp", "tp"),
            P("fsdp", "tp"),
        ),
        out_specs=(P("fsdp", "tp"), P("fsdp", "tp"), P("fsdp", "tp")),
        check_vma=False,
    )
```

profile of v0, /device:TPU:1, one launch (start us, length us, event | category | flops | bytes accessed | tf_op | source)
XLA Modules:
  0.0 177.1 jit_solution(3360917038554923478)
XLA Ops:
  1.5 3.8 %collective-permute-start = (bf16[256,128]{1,0:T(8,128)(2,1)S(1)}, bf16[256,128]{1,0:T(8,128)(2,1)S(1)}, u32[]{:S(2)}, u32[]{:S(2)}) collective-permute-start(bf16[256,128]{1,0:T(8,128)(2,1)S(1)} %constant_dynamic-slice_fusion.4.refs_0_), channel_id=1, source_target_pairs={{0,64},{1,65},{2,66},{3,67},{4,68},{5,69},{6,70},{7,71},{8,72},{9,... | collective-permute-start | bytes 196616 | tf_op jit(solution)/shard_map/ppermute | solution.py:21
  5.3 5.1 %collective-permute-start.1 = (bf16[256,128]{1,0:T(8,128)(2,1)S(1)}, bf16[256,128]{1,0:T(8,128)(2,1)S(1)}, u32[]{:S(2)}, u32[]{:S(2)}) collective-permute-start(bf16[256,128]{1,0:T(8,128)(2,1)S(1)} %constant_dynamic-slice_fusion.4.refs_0_), channel_id=1, source_target_pairs={{0,128},{1,129},{2,130},{3,131},{4,132},{5,133},{6,134},{7,135},{8... | collective-permute-start | bytes 196616 | tf_op jit(solution)/shard_map/ppermute | solution.py:21
  10.4 2.7 %collective-permute-done.1.refs_2_ = bf16[256,128]{1,0:T(8,128)(2,1)S(1)} collective-permute-done((bf16[256,128]{1,0:T(8,128)(2,1)S(1)}, bf16[256,128]{1,0:T(8,128)(2,1)S(1)}, u32[]{:S(2)}, u32[]{:S(2)}) %collective-permute-start.1) | collective-permute-done | bytes 65568 | tf_op jit(solution)/shard_map/ppermute | solution.py:21
  13.2 2.7 %collective-permute-done.2.refs_3_ = bf16[256,128]{1,0:T(8,128)(2,1)S(1)} collective-permute-done((bf16[256,128]{1,0:T(8,128)(2,1)S(1)}, bf16[256,128]{1,0:T(8,128)(2,1)S(1)}, u32[]{:S(2)}, u32[]{:S(2)}) %collective-permute-start.2) | collective-permute-done | bytes 65568 | tf_op jit(solution)/shard_map/ppermute | solution.py:21
  17.2 2.5 %collective-permute-start.4 = (bf16[1024,128]{1,0:T(8,128)(2,1)S(1)}, bf16[1024,128]{1,0:T(8,128)(2,1)S(1)}, u32[]{:S(2)}, u32[]{:S(2)}) collective-permute-start(bf16[1024,128]{1,0:T(8,128)(2,1)S(1)} %shard_map.157.refs_0_), channel_id=1, source_target_pairs={{0,32},{1,33},{2,34},{3,35},{4,36},{5,37},{6,38},{7,39},{8,40},{9,... | collective-permute-start | bytes 786440 | tf_op jit(solution)/shard_map/ppermute | solution.py:21
  19.9 3.0 %collective-permute-start.24 = (bf16[256,1024]{1,0:T(8,128)(2,1)}, bf16[256,1024]{1,0:T(8,128)(2,1)}, u32[]{:S(2)}, u32[]{:S(2)}) collective-permute-start(bf16[256,1024]{1,0:T(8,128)(2,1)} %param.16), channel_id=1, source_target_pairs={{0,8},{1,9},{2,10},{3,11},{4,12},{5,13},{6,14},{7,15},{8,0},{9,1},... | collective-permute-start | bytes 1572872 | tf_op jit(solution)/shard_map/ppermute | solution.py:21
  22.8 6.7 %collective-permute-done.4.refs_2_ = bf16[1024,128]{1,0:T(8,128)(2,1)S(1)} collective-permute-done((bf16[1024,128]{1,0:T(8,128)(2,1)S(1)}, bf16[1024,128]{1,0:T(8,128)(2,1)S(1)}, u32[]{:S(2)}, u32[]{:S(2)}) %collective-permute-start.4) | collective-permute-done | bytes 262176 | tf_op jit(solution)/shard_map/ppermute | solution.py:21
  29.5 3.5 %collective-permute-done.5.refs_3_ = bf16[1024,128]{1,0:T(8,128)(2,1)S(1)} collective-permute-done((bf16[1024,128]{1,0:T(8,128)(2,1)S(1)}, bf16[1024,128]{1,0:T(8,128)(2,1)S(1)}, u32[]{:S(2)}, u32[]{:S(2)}) %collective-permute-start.5) | collective-permute-done | bytes 262176 | tf_op jit(solution)/shard_map/ppermute | solution.py:21
  33.1 2.3 %collective-permute-start.6 = (bf16[4096,128]{1,0:T(8,128)(2,1)S(1)}, bf16[4096,128]{1,0:T(8,128)(2,1)}, u32[]{:S(2)}, u32[]{:S(2)}) collective-permute-start(bf16[4096,128]{1,0:T(8,128)(2,1)S(1)} %shard_map.158), channel_id=1, source_target_pairs={{0,8},{1,9},{2,10},{3,11},{4,12},{5,13},{6,14},{7,15},{8,0},{9,1},... | collective-permute-start | bytes 3145736 | tf_op jit(solution)/shard_map/ppermute | solution.py:21
  36.6 2.2 %copy-done = bf16[256,8192]{1,0:T(8,128)(2,1)S(1)} copy-done((bf16[256,8192]{1,0:T(8,128)(2,1)S(1)}, bf16[256,8192]{1,0:T(8,128)(2,1)}, u32[]{:S(2)}) %copy-start) | copy-done | bytes 4194328
  40.0 2.1 %fusion.2 = f32[128,256]{1,0:T(8,128)S(1)} fusion(bf16[4096,128]{1,0:T(8,128)(2,1)} %collective-permute-done.6, bf16[256,8192]{1,0:T(8,128)(2,1)S(1)} %shard_map.159), kind=kOutput, calls=%fused_computation.4 | convolution fusion | flops 268435456 | bytes 3276800 | tf_op jit(solution)/shard_map/dot_general | solution.py:290
  43.9 2.3 %collective-permute-done.7.refs_1_ = bf16[128,256]{1,0:T(8,128)(2,1)S(1)} collective-permute-done((bf16[128,256]{1,0:T(8,128)(2,1)S(1)}, bf16[128,256]{1,0:T(8,128)(2,1)S(1)}, u32[]{:S(2)}, u32[]{:S(2)}) %collective-permute-start.7) | collective-permute-done | bytes 65568 | tf_op jit(solution)/shard_map/ppermute | solution.py:21
  46.2 2.8 %collective-permute-start.10 = (bf16[256,256]{1,0:T(8,128)(2,1)S(1)}, bf16[256,256]{1,0:T(8,128)(2,1)S(1)}, u32[]{:S(2)}, u32[]{:S(2)}) collective-permute-start(bf16[256,256]{1,0:T(8,128)(2,1)S(1)} %shard_map.160.refs_0_), channel_id=1, source_target_pairs={{0,6},{1,7},{2,4},{3,5},{4,2},{5,3},{6,0},{7,1},{8,14},{9,15},{10,... | collective-permute-start | bytes 393224 | tf_op jit(solution)/shard_map/ppermute | solution.py:21
  51.4 1.8 collective-permute-done.8.refs_1_
  53.1 2.2 %collective-permute-done.9.refs_2_ = bf16[256,256]{1,0:T(8,128)(2,1)S(1)} collective-permute-done((bf16[256,256]{1,0:T(8,128)(2,1)S(1)}, bf16[256,256]{1,0:T(8,128)(2,1)S(1)}, u32[]{:S(2)}, u32[]{:S(2)}) %collective-permute-start.9) | collective-permute-done | bytes 131104 | tf_op jit(solution)/shard_map/ppermute | solution.py:21
  55.3 2.6 %collective-permute-start.11 = (bf16[1024,256]{1,0:T(8,128)(2,1)S(1)}, bf16[1024,256]{1,0:T(8,128)(2,1)S(1)}, u32[]{:S(2)}, u32[]{:S(2)}) collective-permute-start(bf16[1024,256]{1,0:T(8,128)(2,1)S(1)} %shard_map.161.refs_1_), channel_id=1, source_target_pairs={{0,8},{1,9},{2,10},{3,11},{4,12},{5,13},{6,14},{7,15},{8,0},{9,1},... | collective-permute-start | bytes 1572872 | tf_op jit(solution)/shard_map/ppermute | solution.py:21
  59.5 2.6 %shard_map.163 = (bf16[512,1280]{1,0:T(8,128)(2,1)}, bf16[512,512]{1,0:T(8,128)(2,1)}) custom-call(s32[16]{0:T(128)S(1)} %get-tuple-element.92.refs_0_, bf16[1024,256]{1,0:T(8,128)(2,1)S(1)} %shard_map.161.refs_1_, bf16[1024,256]{1,0:T(8,128)(2,1)S(1)} %collective-permute-done.11.refs_2_, bf16[512,1792]{1,0:T(8,128)(2,1)S(1)} %pad_maximum_fusion.refs_3_), custom_call_target="tpu_custom_call" | custom-call | flops 939524096 | bytes 4718656 | tf_op jit(solution)/shard_map/pallas_call | solution.py:63
  64.3 4.3 %collective-permute-start.14 = (bf16[512,512]{1,0:T(8,128)(2,1)}, bf16[512,512]{1,0:T(8,128)(2,1)}, u32[]{:S(2)}, u32[]{:S(2)}) collective-permute-start(bf16[512,512]{1,0:T(8,128)(2,1)} %get-tuple-element.41), channel_id=1, source_target_pairs={{0,64},{1,65},{2,66},{3,67},{4,68},{5,69},{6,70},{7,71},{8,200},{9... | collective-permute-start | bytes 1572872 | tf_op jit(solution)/shard_map/ppermute | solution.py:21
  73.1 1.7 shard_map.162
  74.8 6.0 %collective-permute-done.14.refs_3_ = bf16[512,512]{1,0:T(8,128)(2,1)} collective-permute-done((bf16[512,512]{1,0:T(8,128)(2,1)}, bf16[512,512]{1,0:T(8,128)(2,1)}, u32[]{:S(2)}, u32[]{:S(2)}) %collective-permute-start.14) | collective-permute-done | bytes 524320 | tf_op jit(solution)/shard_map/ppermute | solution.py:21
  80.8 1.4 shard_map.164
  82.1 1.8 %collective-permute-start.15 = (bf16[256,1280]{1,0:T(8,128)(2,1)S(1)}, bf16[256,1280]{1,0:T(8,128)(2,1)S(1)}, u32[]{:S(2)}, u32[]{:S(2)}) collective-permute-start(bf16[256,1280]{1,0:T(8,128)(2,1)S(1)} %get-tuple-element.44), channel_id=1, source_target_pairs={{0,48},{1,49},{2,50},{3,51},{4,52},{5,53},{6,54},{7,55},{8,24},{9,... | collective-permute-start | bytes 1966088 | tf_op jit(solution)/shard_map/ppermute | solution.py:21
  84.0 1.7 collective-permute-start.16
  86.8 3.8 %collective-permute-start.17 = (f32[8,128]{1,0:T(8,128)S(1)}, f32[8,128]{1,0:T(8,128)S(1)}, u32[]{:S(2)}, u32[]{:S(2)}) collective-permute-start(f32[8,128]{1,0:T(8,128)S(1)} %get-tuple-element.46), channel_id=1, source_target_pairs={{0,8},{1,9},{2,10},{3,11},{4,12},{5,13},{6,14},{7,15},{8,0},{9,1},... | collective-permute-start | bytes 12296 | tf_op jit(solution)/shard_map/ppermute | solution.py:21
  91.5 1.8 collective-permute-done.16.refs_3_
  93.4 3.1 %collective-permute-start.18 = (bf16[128,1280]{1,0:T(8,128)(2,1)S(1)}, bf16[128,1280]{1,0:T(8,128)(2,1)S(1)}, u32[]{:S(2)}, u32[]{:S(2)}) collective-permute-start(bf16[128,1280]{1,0:T(8,128)(2,1)S(1)} %get-tuple-element.49), channel_id=1, source_target_pairs={{0,64},{1,65},{2,66},{3,67},{4,68},{5,69},{6,70},{7,71},{8,200},{9... | collective-permute-start | bytes 983048 | tf_op jit(solution)/shard_map/ppermute | solution.py:21
  97.5 2.2 %collective-permute-start.19 = (bf16[128,512]{1,0:T(8,128)(2,1)S(1)}, bf16[128,512]{1,0:T(8,128)(2,1)S(1)}, u32[]{:S(2)}, u32[]{:S(2)}) collective-permute-start(bf16[128,512]{1,0:T(8,128)(2,1)S(1)} %get-tuple-element.50), channel_id=1, source_target_pairs={{0,16},{1,17},{2,18},{3,19},{4,20},{5,21},{6,22},{7,23},{8,56},{9,... | collective-permute-start | bytes 393224 | tf_op jit(solution)/shard_map/ppermute | solution.py:21
  99.7 1.3 fusion.8.refs_7_.refs_1_
  101.1 1.7 collective-permute-done.19.refs_3_
  104.1 2.7 %collective-permute-start.21 = (bf16[64,1280]{1,0:T(8,128)(2,1)S(1)}, bf16[64,1280]{1,0:T(8,128)(2,1)S(1)}, u32[]{:S(2)}, u32[]{:S(2)}) collective-permute-start(bf16[64,1280]{1,0:T(8,128)(2,1)S(1)} %get-tuple-element.54), channel_id=1, source_target_pairs={{0,192},{1,193},{2,194},{3,195},{4,196},{5,197},{6,198},{7,199},{8... | collective-permute-start | bytes 491528 | tf_op jit(solution)/shard_map/ppermute | solution.py:21
  106.8 6.2 %collective-permute-start.25 = (f32[8,128]{1,0:T(8,128)S(1)}, f32[8,128]{1,0:T(8,128)S(1)}, u32[]{:S(2)}, u32[]{:S(2)}) collective-permute-start(f32[8,128]{1,0:T(8,128)S(1)} %get-tuple-element.56), channel_id=1, source_target_pairs={{0,8},{1,9},{2,10},{3,11},{4,12},{5,13},{6,14},{7,15},{8,0},{9,1},... | collective-permute-start | bytes 12296 | tf_op jit(solution)/shard_map/ppermute | solution.py:21
  113.0 1.3 fusion.9.refs_6_.refs_0_
  114.9 2.8 %collective-permute-start.26 = (f32[64,1792]{1,0:T(8,128)S(1)}, f32[64,1792]{1,0:T(8,128)S(1)}, u32[]{:S(2)}, u32[]{:S(2)}) collective-permute-start(f32[64,1792]{1,0:T(8,128)S(1)} %shard_map.168), channel_id=1, source_target_pairs={{0,8},{1,9},{2,10},{3,11},{4,12},{5,13},{6,14},{7,15},{8,0},{9,1},... | collective-permute-start | bytes 1376264 | tf_op jit(solution)/shard_map/ppermute | solution.py:21
  118.5 3.1 %collective-permute-done.28.refs_3_ = bf16[64,512]{1,0:T(8,128)(2,1)S(1)} collective-permute-done((bf16[64,512]{1,0:T(8,128)(2,1)S(1)}, bf16[64,512]{1,0:T(8,128)(2,1)S(1)}, u32[]{:S(2)}, u32[]{:S(2)}) %collective-permute-start.28) | collective-permute-done | bytes 65568 | tf_op jit(solution)/shard_map/ppermute | solution.py:21
  121.6 2.5 %collective-permute-done.27.refs_1_ = bf16[64,1280]{1,0:T(8,128)(2,1)S(1)} collective-permute-done((bf16[64,1280]{1,0:T(8,128)(2,1)S(1)}, bf16[64,1280]{1,0:T(8,128)(2,1)S(1)}, u32[]{:S(2)}, u32[]{:S(2)}) %collective-permute-start.27) | collective-permute-done | bytes 163872 | tf_op jit(solution)/shard_map/ppermute | solution.py:21
  124.1 1.3 collective-permute-start.29
  125.5 1.7 collective-permute-start.30
  130.6 5.3 %collective-permute-done.29.refs_1_ = bf16[128,1280]{1,0:T(8,128)(2,1)S(1)} collective-permute-done((bf16[128,1280]{1,0:T(8,128)(2,1)S(1)}, bf16[128,1280]{1,0:T(8,128)(2,1)S(1)}, u32[]{:S(2)}, u32[]{:S(2)}) %collective-permute-start.29) | collective-permute-done | bytes 327712 | tf_op jit(solution)/shard_map/ppermute | solution.py:21
  136.1 1.4 collective-permute-start.33
  137.6 4.9 %collective-permute-start.34 = (f32[8,128]{1,0:T(8,128)S(1)}, f32[8,128]{1,0:T(8,128)S(1)}, u32[]{:S(2)}, u32[]{:S(2)}) collective-permute-start(f32[8,128]{1,0:T(8,128)S(1)} %get-tuple-element.69), channel_id=1, source_target_pairs={{0,8},{1,9},{2,10},{3,11},{4,12},{5,13},{6,14},{7,15},{8,0},{9,1},... | collective-permute-start | bytes 12296 | tf_op jit(solution)/shard_map/ppermute | solution.py:21
  143.4 1.5 collective-permute-done.33.refs_3_
  146.1 2.6 %collective-permute-start.36 = (bf16[512,512]{1,0:T(8,128)(2,1)S(1)}, bf16[512,512]{1,0:T(8,128)(2,1)S(1)}, u32[]{:S(2)}, u32[]{:S(2)}) collective-permute-start(bf16[512,512]{1,0:T(8,128)(2,1)S(1)} %get-tuple-element.71.refs_3_), channel_id=1, source_target_pairs={{0,64},{1,65},{2,66},{3,67},{4,68},{5,69},{6,70},{7,71},{8,200},{9... | collective-permute-start | bytes 1572872 | tf_op jit(solution)/shard_map/ppermute | solution.py:21
  148.7 6.5 %collective-permute-start.37 = (f32[8,128]{1,0:T(8,128)S(1)}, f32[8,128]{1,0:T(8,128)S(1)}, u32[]{:S(2)}, u32[]{:S(2)}) collective-permute-start(f32[8,128]{1,0:T(8,128)S(1)} %get-tuple-element.72), channel_id=1, source_target_pairs={{0,8},{1,9},{2,10},{3,11},{4,12},{5,13},{6,14},{7,15},{8,0},{9,1},... | collective-permute-start | bytes 12296 | tf_op jit(solution)/shard_map/ppermute | solution.py:21
  157.2 4.8 %collective-permute-done.36.refs_3_ = bf16[512,512]{1,0:T(8,128)(2,1)S(1)} collective-permute-done((bf16[512,512]{1,0:T(8,128)(2,1)S(1)}, bf16[512,512]{1,0:T(8,128)(2,1)S(1)}, u32[]{:S(2)}, u32[]{:S(2)}) %collective-permute-start.36) | collective-permute-done | bytes 524320 | tf_op jit(solution)/shard_map/ppermute | solution.py:21
  161.9 2.6 %collective-permute-done.35.refs_2_ = bf16[512,1280]{1,0:T(8,128)(2,1)S(1)} collective-permute-done((bf16[512,1280]{1,0:T(8,128)(2,1)S(1)}, bf16[512,1280]{1,0:T(8,128)(2,1)S(1)}, u32[]{:S(2)}, u32[]{:S(2)}) %collective-permute-start.35) | collective-permute-done | bytes 1310752 | tf_op jit(solution)/shard_map/ppermute | solution.py:21
  165.2 8.1 %collective-permute-start.38 = (bf16[256,1792]{1,0:T(8,128)(2,1)S(1)}, bf16[256,1792]{1,0:T(8,128)(2,1)S(1)}, u32[]{:S(2)}, u32[]{:S(2)}) collective-permute-start(bf16[256,1792]{1,0:T(8,128)(2,1)S(1)} %shard_map.175), channel_id=1, source_target_pairs={{0,8},{1,9},{2,10},{3,11},{4,12},{5,13},{6,14},{7,15},{8,0},{9,1},... | collective-permute-start | bytes 2752520 | tf_op jit(solution)/shard_map/ppermute | solution.py:21
  174.1 1.4 collective-permute-done.38
  175.5 1.6 maximum_select_fusion
  (107 shorter events, 31.7 us)
Async XLA Ops:
  1.5 8.9 %collective-permute-start = (bf16[256,128]{1,0:T(8,128)(2,1)S(1)}, bf16[256,128]{1,0:T(8,128)(2,1)S(1)}, u32[]{:S(2)}, u32[]{:S(2)}) collective-permute-start(bf16[256,128]{1,0:T(8,128)(2,1)S(1)} %constant_dynamic-slice_fusion.4.refs_0_), channel_id=1, source_target_pairs={{0,64},{1,65},{2,66},{3,67},{4,68},{5,69},{6,70},{7,71},{8,72},{9,... | collective-permute-start | bytes 196616 | tf_op jit(solution)/shard_map/ppermute | solution.py:21
  5.3 7.9 %collective-permute-start.1 = (bf16[256,128]{1,0:T(8,128)(2,1)S(1)}, bf16[256,128]{1,0:T(8,128)(2,1)S(1)}, u32[]{:S(2)}, u32[]{:S(2)}) collective-permute-start(bf16[256,128]{1,0:T(8,128)(2,1)S(1)} %constant_dynamic-slice_fusion.4.refs_0_), channel_id=1, source_target_pairs={{0,128},{1,129},{2,130},{3,131},{4,132},{5,133},{6,134},{7,135},{8... | collective-permute-start | bytes 196616 | tf_op jit(solution)/shard_map/ppermute | solution.py:21
  10.4 5.5 %collective-permute-start.2 = (bf16[256,128]{1,0:T(8,128)(2,1)S(1)}, bf16[256,128]{1,0:T(8,128)(2,1)S(1)}, u32[]{:S(2)}, u32[]{:S(2)}) collective-permute-start(bf16[256,128]{1,0:T(8,128)(2,1)S(1)} %constant_dynamic-slice_fusion.4.refs_0_), channel_id=1, source_target_pairs={{0,192},{1,193},{2,194},{3,195},{4,196},{5,197},{6,198},{7,199},{8... | collective-permute-start | bytes 196616 | tf_op jit(solution)/shard_map/ppermute | solution.py:21
  15.9 6.9 %collective-permute-start.3 = (bf16[1024,128]{1,0:T(8,128)(2,1)S(1)}, bf16[1024,128]{1,0:T(8,128)(2,1)S(1)}, u32[]{:S(2)}, u32[]{:S(2)}) collective-permute-start(bf16[1024,128]{1,0:T(8,128)(2,1)S(1)} %shard_map.157.refs_0_), channel_id=1, source_target_pairs={{0,16},{1,17},{2,18},{3,19},{4,20},{5,21},{6,22},{7,23},{8,24},{9,... | collective-permute-start | bytes 786440 | tf_op jit(solution)/shard_map/ppermute | solution.py:21
  17.2 12.3 %collective-permute-start.4 = (bf16[1024,128]{1,0:T(8,128)(2,1)S(1)}, bf16[1024,128]{1,0:T(8,128)(2,1)S(1)}, u32[]{:S(2)}, u32[]{:S(2)}) collective-permute-start(bf16[1024,128]{1,0:T(8,128)(2,1)S(1)} %shard_map.157.refs_0_), channel_id=1, source_target_pairs={{0,32},{1,33},{2,34},{3,35},{4,36},{5,37},{6,38},{7,39},{8,40},{9,... | collective-permute-start | bytes 786440 | tf_op jit(solution)/shard_map/ppermute | solution.py:21
  19.7 13.4 %collective-permute-start.5 = (bf16[1024,128]{1,0:T(8,128)(2,1)S(1)}, bf16[1024,128]{1,0:T(8,128)(2,1)S(1)}, u32[]{:S(2)}, u32[]{:S(2)}) collective-permute-start(bf16[1024,128]{1,0:T(8,128)(2,1)S(1)} %shard_map.157.refs_0_), channel_id=1, source_target_pairs={{0,48},{1,49},{2,50},{3,51},{4,52},{5,53},{6,54},{7,55},{8,56},{9,... | collective-permute-start | bytes 786440 | tf_op jit(solution)/shard_map/ppermute | solution.py:21
  19.9 76.6 %collective-permute-start.24 = (bf16[256,1024]{1,0:T(8,128)(2,1)}, bf16[256,1024]{1,0:T(8,128)(2,1)}, u32[]{:S(2)}, u32[]{:S(2)}) collective-permute-start(bf16[256,1024]{1,0:T(8,128)(2,1)} %param.16), channel_id=1, source_target_pairs={{0,8},{1,9},{2,10},{3,11},{4,12},{5,13},{6,14},{7,15},{8,0},{9,1},... | collective-permute-start | bytes 1572872 | tf_op jit(solution)/shard_map/ppermute | solution.py:21
  22.8 12.6 %copy-start.7 = (bf16[256,3584]{1,0:T(8,128)(2,1)S(1)}, bf16[256,3584]{1,0:T(8,128)(2,1)}, u32[]{:S(2)}) copy-start(bf16[256,3584]{1,0:T(8,128)(2,1)} %param.15) | copy-start | bytes 5505028
  33.1 3.4 %copy-start.14 = (s32[16]{0:T(128)S(1)}, s32[16]{0:T(128)}, u32[]{:S(2)}) copy-start(s32[16]{0:T(128)} %constant.36.clone) | copy-start | bytes 196
  33.1 6.9 %collective-permute-start.6 = (bf16[4096,128]{1,0:T(8,128)(2,1)S(1)}, bf16[4096,128]{1,0:T(8,128)(2,1)}, u32[]{:S(2)}, u32[]{:S(2)}) collective-permute-start(bf16[4096,128]{1,0:T(8,128)(2,1)S(1)} %shard_map.158), channel_id=1, source_target_pairs={{0,8},{1,9},{2,10},{3,11},{4,12},{5,13},{6,14},{7,15},{8,0},{9,1},... | collective-permute-start | bytes 3145736 | tf_op jit(solution)/shard_map/ppermute | solution.py:21
  36.4 21.7 %collective-permute-start.12 = (bf16[256,1792]{1,0:T(8,128)(2,1)S(1)}, bf16[256,1792]{1,0:T(8,128)(2,1)S(1)}, u32[]{:S(2)}, u32[]{:S(2)}) collective-permute-start(bf16[256,1792]{1,0:T(8,128)(2,1)S(1)} %get-tuple-element.74), channel_id=1, source_target_pairs={{0,8},{1,9},{2,10},{3,11},{4,12},{5,13},{6,14},{7,15},{8,0},{9,1},... | collective-permute-start | bytes 2752520 | tf_op jit(solution)/shard_map/ppermute | solution.py:21
  36.6 2.2 %copy-start = (bf16[256,8192]{1,0:T(8,128)(2,1)S(1)}, bf16[256,8192]{1,0:T(8,128)(2,1)}, u32[]{:S(2)}) copy-start(bf16[256,8192]{1,0:T(8,128)(2,1)} %refs_1_.1) | copy-start | bytes 12582916
  42.1 1.8 %copy-start.10 = (s32[16]{0:T(128)S(1)}, s32[16]{0:T(128)}, u32[]{:S(2)}) copy-start(s32[16]{0:T(128)} %constant.39.clone) | copy-start | bytes 196
  42.1 1.8 %copy-start.11 = (s32[16]{0:T(128)S(1)}, s32[16]{0:T(128)}, u32[]{:S(2)}) copy-start(s32[16]{0:T(128)} %constant.40.clone) | copy-start | bytes 196
  42.1 16.0 %copy-start.5 = (bf16[256,1792]{1,0:T(8,128)(2,1)S(1)}, bf16[256,1792]{1,0:T(8,128)(2,1)}, u32[]{:S(2)}) copy-start(bf16[256,1792]{1,0:T(8,128)(2,1)} %get-tuple-element.73) | copy-start | bytes 2752516
  43.0 3.2 %collective-permute-start.7 = (bf16[128,256]{1,0:T(8,128)(2,1)S(1)}, bf16[128,256]{1,0:T(8,128)(2,1)S(1)}, u32[]{:S(2)}, u32[]{:S(2)}) collective-permute-start(bf16[128,256]{1,0:T(8,128)(2,1)S(1)} %fusion.13.refs_0_), channel_id=1, source_target_pairs={{0,1},{1,0},{2,3},{3,2},{4,5},{5,4},{6,7},{7,6},{8,9},{9,8},{10,11... | collective-permute-start | bytes 196616 | tf_op jit(solution)/shard_map/ppermute | solution.py:21
  46.2 5.2 %collective-permute-start.10 = (bf16[256,256]{1,0:T(8,128)(2,1)S(1)}, bf16[256,256]{1,0:T(8,128)(2,1)S(1)}, u32[]{:S(2)}, u32[]{:S(2)}) collective-permute-start(bf16[256,256]{1,0:T(8,128)(2,1)S(1)} %shard_map.160.refs_0_), channel_id=1, source_target_pairs={{0,6},{1,7},{2,4},{3,5},{4,2},{5,3},{6,0},{7,1},{8,14},{9,15},{10,... | collective-permute-start | bytes 393224 | tf_op jit(solution)/shard_map/ppermute | solution.py:21
  49.0 4.1 %collective-permute-start.8 = (bf16[256,256]{1,0:T(8,128)(2,1)S(1)}, bf16[256,256]{1,0:T(8,128)(2,1)S(1)}, u32[]{:S(2)}, u32[]{:S(2)}) collective-permute-start(bf16[256,256]{1,0:T(8,128)(2,1)S(1)} %shard_map.160.refs_0_), channel_id=1, source_target_pairs={{0,2},{1,3},{2,0},{3,1},{4,6},{5,7},{6,4},{7,5},{8,10},{9,11},{10,... | collective-permute-start | bytes 393224 | tf_op jit(solution)/shard_map/ppermute | solution.py:21
  49.0 6.3 %collective-permute-start.9 = (bf16[256,256]{1,0:T(8,128)(2,1)S(1)}, bf16[256,256]{1,0:T(8,128)(2,1)S(1)}, u32[]{:S(2)}, u32[]{:S(2)}) collective-permute-start(bf16[256,256]{1,0:T(8,128)(2,1)S(1)} %shard_map.160.refs_0_), channel_id=1, source_target_pairs={{0,4},{1,5},{2,6},{3,7},{4,0},{5,1},{6,2},{7,3},{8,12},{9,13},{10,... | collective-permute-start | bytes 393224 | tf_op jit(solution)/shard_map/ppermute | solution.py:21
  55.3 6.8 %copy-start.1 = (bf16[1024,256]{1,0:T(8,128)(2,1)}, bf16[1024,256]{1,0:T(8,128)(2,1)S(1)}, u32[]{:S(2)}) copy-start(bf16[1024,256]{1,0:T(8,128)(2,1)S(1)} %shard_map.161.refs_1_) | copy-start | bytes 1572868
  55.3 4.2 %collective-permute-start.11 = (bf16[1024,256]{1,0:T(8,128)(2,1)S(1)}, bf16[1024,256]{1,0:T(8,128)(2,1)S(1)}, u32[]{:S(2)}, u32[]{:S(2)}) collective-permute-start(bf16[1024,256]{1,0:T(8,128)(2,1)S(1)} %shard_map.161.refs_1_), channel_id=1, source_target_pairs={{0,8},{1,9},{2,10},{3,11},{4,12},{5,13},{6,14},{7,15},{8,0},{9,1},... | collective-permute-start | bytes 1572872 | tf_op jit(solution)/shard_map/ppermute | solution.py:21
  58.3 4.1 %copy-start.9 = (f32[32,3584]{1,0:T(8,128)S(1)}, f32[32,3584]{1,0:T(8,128)}, u32[]{:S(2)}) copy-start(f32[32,3584]{1,0:T(8,128)} %param.18) | copy-start | bytes 1376260
  59.5 2.6 %copy-start.3 = (bf16[1024,256]{1,0:T(8,128)(2,1)}, bf16[1024,256]{1,0:T(8,128)(2,1)S(1)}, u32[]{:S(2)}) copy-start(bf16[1024,256]{1,0:T(8,128)(2,1)S(1)} %collective-permute-done.11.refs_2_) | copy-start | bytes 1572868
  62.1 18.6 %collective-permute-start.13 = (bf16[512,1280]{1,0:T(8,128)(2,1)}, bf16[512,1280]{1,0:T(8,128)(2,1)S(1)}, u32[]{:S(2)}, u32[]{:S(2)}) collective-permute-start(bf16[512,1280]{1,0:T(8,128)(2,1)} %get-tuple-element.40), channel_id=1, source_target_pairs={{0,16},{1,17},{2,18},{3,19},{4,20},{5,21},{6,22},{7,23},{8,56},{9,... | collective-permute-start | bytes 3932168 | tf_op jit(solution)/shard_map/ppermute | solution.py:21
  64.1 21.6 %collective-permute-start.23 = (f32[64,1792]{1,0:T(8,128)}, f32[64,1792]{1,0:T(8,128)}, u32[]{:S(2)}, u32[]{:S(2)}) collective-permute-start(f32[64,1792]{1,0:T(8,128)} %constant_dynamic-slice_fusion.1), channel_id=1, source_target_pairs={{0,8},{1,9},{2,10},{3,11},{4,12},{5,13},{6,14},{7,15},{8,0},{9,1},... | collective-permute-start | bytes 1376264 | tf_op jit(solution)/shard_map/ppermute | solution.py:21
  64.3 16.4 %collective-permute-start.14 = (bf16[512,512]{1,0:T(8,128)(2,1)}, bf16[512,512]{1,0:T(8,128)(2,1)}, u32[]{:S(2)}, u32[]{:S(2)}) collective-permute-start(bf16[512,512]{1,0:T(8,128)(2,1)} %get-tuple-element.41), channel_id=1, source_target_pairs={{0,64},{1,65},{2,66},{3,67},{4,68},{5,69},{6,70},{7,71},{8,200},{9... | collective-permute-start | bytes 1572872 | tf_op jit(solution)/shard_map/ppermute | solution.py:21
  82.1 11.1 %collective-permute-start.15 = (bf16[256,1280]{1,0:T(8,128)(2,1)S(1)}, bf16[256,1280]{1,0:T(8,128)(2,1)S(1)}, u32[]{:S(2)}, u32[]{:S(2)}) collective-permute-start(bf16[256,1280]{1,0:T(8,128)(2,1)S(1)} %get-tuple-element.44), channel_id=1, source_target_pairs={{0,48},{1,49},{2,50},{3,51},{4,52},{5,53},{6,54},{7,55},{8,24},{9,... | collective-permute-start | bytes 1966088 | tf_op jit(solution)/shard_map/ppermute | solution.py:21
  84.0 9.3 %collective-permute-start.16 = (bf16[256,512]{1,0:T(8,128)(2,1)S(1)}, bf16[256,512]{1,0:T(8,128)(2,1)S(1)}, u32[]{:S(2)}, u32[]{:S(2)}) collective-permute-start(bf16[256,512]{1,0:T(8,128)(2,1)S(1)} %get-tuple-element.45), channel_id=1, source_target_pairs={{0,192},{1,193},{2,194},{3,195},{4,196},{5,197},{6,198},{7,199},{8... | collective-permute-start | bytes 786440 | tf_op jit(solution)/shard_map/ppermute | solution.py:21
  86.8 4.7 %collective-permute-start.17 = (f32[8,128]{1,0:T(8,128)S(1)}, f32[8,128]{1,0:T(8,128)S(1)}, u32[]{:S(2)}, u32[]{:S(2)}) collective-permute-start(f32[8,128]{1,0:T(8,128)S(1)} %get-tuple-element.46), channel_id=1, source_target_pairs={{0,8},{1,9},{2,10},{3,11},{4,12},{5,13},{6,14},{7,15},{8,0},{9,1},... | collective-permute-start | bytes 12296 | tf_op jit(solution)/shard_map/ppermute | solution.py:21
  93.4 10.6 %collective-permute-start.18 = (bf16[128,1280]{1,0:T(8,128)(2,1)S(1)}, bf16[128,1280]{1,0:T(8,128)(2,1)S(1)}, u32[]{:S(2)}, u32[]{:S(2)}) collective-permute-start(bf16[128,1280]{1,0:T(8,128)(2,1)S(1)} %get-tuple-element.49), channel_id=1, source_target_pairs={{0,64},{1,65},{2,66},{3,67},{4,68},{5,69},{6,70},{7,71},{8,200},{9... | collective-permute-start | bytes 983048 | tf_op jit(solution)/shard_map/ppermute | solution.py:21
  97.5 5.3 %collective-permute-start.19 = (bf16[128,512]{1,0:T(8,128)(2,1)S(1)}, bf16[128,512]{1,0:T(8,128)(2,1)S(1)}, u32[]{:S(2)}, u32[]{:S(2)}) collective-permute-start(bf16[128,512]{1,0:T(8,128)(2,1)S(1)} %get-tuple-element.50), channel_id=1, source_target_pairs={{0,16},{1,17},{2,18},{3,19},{4,20},{5,21},{6,22},{7,23},{8,56},{9,... | collective-permute-start | bytes 393224 | tf_op jit(solution)/shard_map/ppermute | solution.py:21
  99.7 1.3 collective-permute-start.20
  104.1 10.3 %collective-permute-start.21 = (bf16[64,1280]{1,0:T(8,128)(2,1)S(1)}, bf16[64,1280]{1,0:T(8,128)(2,1)S(1)}, u32[]{:S(2)}, u32[]{:S(2)}) collective-permute-start(bf16[64,1280]{1,0:T(8,128)(2,1)S(1)} %get-tuple-element.54), channel_id=1, source_target_pairs={{0,192},{1,193},{2,194},{3,195},{4,196},{5,197},{6,198},{7,199},{8... | collective-permute-start | bytes 491528 | tf_op jit(solution)/shard_map/ppermute | solution.py:21
  106.8 7.6 %collective-permute-start.22 = (bf16[64,512]{1,0:T(8,128)(2,1)S(1)}, bf16[64,512]{1,0:T(8,128)(2,1)S(1)}, u32[]{:S(2)}, u32[]{:S(2)}) collective-permute-start(bf16[64,512]{1,0:T(8,128)(2,1)S(1)} %get-tuple-element.55), channel_id=1, source_target_pairs={{0,48},{1,49},{2,50},{3,51},{4,52},{5,53},{6,54},{7,55},{8,24},{9,... | collective-permute-start | bytes 196616 | tf_op jit(solution)/shard_map/ppermute | solution.py:21
  106.8 7.6 %collective-permute-start.25 = (f32[8,128]{1,0:T(8,128)S(1)}, f32[8,128]{1,0:T(8,128)S(1)}, u32[]{:S(2)}, u32[]{:S(2)}) collective-permute-start(f32[8,128]{1,0:T(8,128)S(1)} %get-tuple-element.56), channel_id=1, source_target_pairs={{0,8},{1,9},{2,10},{3,11},{4,12},{5,13},{6,14},{7,15},{8,0},{9,1},... | collective-permute-start | bytes 12296 | tf_op jit(solution)/shard_map/ppermute | solution.py:21
  114.9 9.2 %collective-permute-start.26 = (f32[64,1792]{1,0:T(8,128)S(1)}, f32[64,1792]{1,0:T(8,128)S(1)}, u32[]{:S(2)}, u32[]{:S(2)}) collective-permute-start(f32[64,1792]{1,0:T(8,128)S(1)} %shard_map.168), channel_id=1, source_target_pairs={{0,8},{1,9},{2,10},{3,11},{4,12},{5,13},{6,14},{7,15},{8,0},{9,1},... | collective-permute-start | bytes 1376264 | tf_op jit(solution)/shard_map/ppermute | solution.py:21
  117.7 6.4 %collective-permute-start.27 = (bf16[64,1280]{1,0:T(8,128)(2,1)S(1)}, bf16[64,1280]{1,0:T(8,128)(2,1)S(1)}, u32[]{:S(2)}, u32[]{:S(2)}) collective-permute-start(bf16[64,1280]{1,0:T(8,128)(2,1)S(1)} %get-tuple-element.61.refs_0_), channel_id=1, source_target_pairs={{0,192},{1,193},{2,194},{3,195},{4,196},{5,197},{6,198},{7,199},{8... | collective-permute-start | bytes 491528 | tf_op jit(solution)/shard_map/ppermute | solution.py:21
  118.4 3.1 %collective-permute-start.28 = (bf16[64,512]{1,0:T(8,128)(2,1)S(1)}, bf16[64,512]{1,0:T(8,128)(2,1)S(1)}, u32[]{:S(2)}, u32[]{:S(2)}) collective-permute-start(bf16[64,512]{1,0:T(8,128)(2,1)S(1)} %get-tuple-element.62.refs_2_), channel_id=1, source_target_pairs={{0,48},{1,49},{2,50},{3,51},{4,52},{5,53},{6,54},{7,55},{8,24},{9,... | collective-permute-start | bytes 196616 | tf_op jit(solution)/shard_map/ppermute | solution.py:21
  124.1 11.9 %collective-permute-start.29 = (bf16[128,1280]{1,0:T(8,128)(2,1)S(1)}, bf16[128,1280]{1,0:T(8,128)(2,1)S(1)}, u32[]{:S(2)}, u32[]{:S(2)}) collective-permute-start(bf16[128,1280]{1,0:T(8,128)(2,1)S(1)} %get-tuple-element.63.refs_0_), channel_id=1, source_target_pairs={{0,64},{1,65},{2,66},{3,67},{4,68},{5,69},{6,70},{7,71},{8,200},{9... | collective-permute-start | bytes 983048 | tf_op jit(solution)/shard_map/ppermute | solution.py:21
  125.5 5.2 %collective-permute-start.30 = (bf16[128,512]{1,0:T(8,128)(2,1)S(1)}, bf16[128,512]{1,0:T(8,128)(2,1)S(1)}, u32[]{:S(2)}, u32[]{:S(2)}) collective-permute-start(bf16[128,512]{1,0:T(8,128)(2,1)S(1)} %get-tuple-element.64.refs_2_), channel_id=1, source_target_pairs={{0,16},{1,17},{2,18},{3,19},{4,20},{5,21},{6,22},{7,23},{8,56},{9,... | collective-permute-start | bytes 393224 | tf_op jit(solution)/shard_map/ppermute | solution.py:21
  127.1 2.2 %collective-permute-start.31 = (f32[8,128]{1,0:T(8,128)S(1)}, f32[8,128]{1,0:T(8,128)S(1)}, u32[]{:S(2)}, u32[]{:S(2)}) collective-permute-start(f32[8,128]{1,0:T(8,128)S(1)} %get-tuple-element.65), channel_id=1, source_target_pairs={{0,8},{1,9},{2,10},{3,11},{4,12},{5,13},{6,14},{7,15},{8,0},{9,1},... | collective-permute-start | bytes 12296 | tf_op jit(solution)/shard_map/ppermute | solution.py:21
  136.0 9.8 %collective-permute-start.32 = (bf16[256,1280]{1,0:T(8,128)(2,1)S(1)}, bf16[256,1280]{1,0:T(8,128)(2,1)S(1)}, u32[]{:S(2)}, u32[]{:S(2)}) collective-permute-start(bf16[256,1280]{1,0:T(8,128)(2,1)S(1)} %get-tuple-element.67.refs_0_), channel_id=1, source_target_pairs={{0,48},{1,49},{2,50},{3,51},{4,52},{5,53},{6,54},{7,55},{8,24},{9,... | collective-permute-start | bytes 1966088 | tf_op jit(solution)/shard_map/ppermute | solution.py:21
  136.1 8.8 %collective-permute-start.33 = (bf16[256,512]{1,0:T(8,128)(2,1)S(1)}, bf16[256,512]{1,0:T(8,128)(2,1)S(1)}, u32[]{:S(2)}, u32[]{:S(2)}) collective-permute-start(bf16[256,512]{1,0:T(8,128)(2,1)S(1)} %get-tuple-element.68.refs_2_), channel_id=1, source_target_pairs={{0,192},{1,193},{2,194},{3,195},{4,196},{5,197},{6,198},{7,199},{8... | collective-permute-start | bytes 786440 | tf_op jit(solution)/shard_map/ppermute | solution.py:21
  137.6 5.8 %collective-permute-start.34 = (f32[8,128]{1,0:T(8,128)S(1)}, f32[8,128]{1,0:T(8,128)S(1)}, u32[]{:S(2)}, u32[]{:S(2)}) collective-permute-start(f32[8,128]{1,0:T(8,128)S(1)} %get-tuple-element.69), channel_id=1, source_target_pairs={{0,8},{1,9},{2,10},{3,11},{4,12},{5,13},{6,14},{7,15},{8,0},{9,1},... | collective-permute-start | bytes 12296 | tf_op jit(solution)/shard_map/ppermute | solution.py:21
  146.0 18.6 %collective-permute-start.35 = (bf16[512,1280]{1,0:T(8,128)(2,1)S(1)}, bf16[512,1280]{1,0:T(8,128)(2,1)S(1)}, u32[]{:S(2)}, u32[]{:S(2)}) collective-permute-start(bf16[512,1280]{1,0:T(8,128)(2,1)S(1)} %get-tuple-element.70.refs_2_), channel_id=1, source_target_pairs={{0,16},{1,17},{2,18},{3,19},{4,20},{5,21},{6,22},{7,23},{8,56},{9,... | collective-permute-start | bytes 3932168 | tf_op jit(solution)/shard_map/ppermute | solution.py:21
  146.1 15.8 %collective-permute-start.36 = (bf16[512,512]{1,0:T(8,128)(2,1)S(1)}, bf16[512,512]{1,0:T(8,128)(2,1)S(1)}, u32[]{:S(2)}, u32[]{:S(2)}) collective-permute-start(bf16[512,512]{1,0:T(8,128)(2,1)S(1)} %get-tuple-element.71.refs_3_), channel_id=1, source_target_pairs={{0,64},{1,65},{2,66},{3,67},{4,68},{5,69},{6,70},{7,71},{8,200},{9... | collective-permute-start | bytes 1572872 | tf_op jit(solution)/shard_map/ppermute | solution.py:21
  148.7 7.3 %collective-permute-start.37 = (f32[8,128]{1,0:T(8,128)S(1)}, f32[8,128]{1,0:T(8,128)S(1)}, u32[]{:S(2)}, u32[]{:S(2)}) collective-permute-start(f32[8,128]{1,0:T(8,128)S(1)} %get-tuple-element.72), channel_id=1, source_target_pairs={{0,8},{1,9},{2,10},{3,11},{4,12},{5,13},{6,14},{7,15},{8,0},{9,1},... | collective-permute-start | bytes 12296 | tf_op jit(solution)/shard_map/ppermute | solution.py:21
  165.2 10.2 %collective-permute-start.38 = (bf16[256,1792]{1,0:T(8,128)(2,1)S(1)}, bf16[256,1792]{1,0:T(8,128)(2,1)S(1)}, u32[]{:S(2)}, u32[]{:S(2)}) collective-permute-start(bf16[256,1792]{1,0:T(8,128)(2,1)S(1)} %shard_map.175), channel_id=1, source_target_pairs={{0,8},{1,9},{2,10},{3,11},{4,12},{5,13},{6,14},{7,15},{8,0},{9,1},... | collective-permute-start | bytes 2752520 | tf_op jit(solution)/shard_map/ppermute | solution.py:21
  (6 other events, 6.5 us)
where the time goes:
time: 178 us; the launch traced here: 177 us
  starting transfers between devices  83.8 us (47%)
  waiting for transfers between devices  60.9 us (34%)
  local copies, waits for them, and re-layouts  12.6 us (7%)
  Pallas kernels  11.2 us (6%)
  matrix products  5.56 us (3%)
  other arithmetic  2.08 us (1%)
    ppermute x39, starting transfers between devices, swap(): lax.ppermute(array, ('fsdp', 'tp'), [(i, i ^ scale * masks[i // inner % 2...  83.8 us
    ppermute x39, waiting for transfers between devices, swap(): lax.ppermute(array, ('fsdp', 'tp'), [(i, i ^ scale * masks[i // inner % 2...  60.9 us
    pallas_call x19, Pallas kernels, call(): pl.pallas_call(body, out_shape=list(outs), in_specs=specs, out_specs=[pl....  11.2 us
    unnamed x32, local copies, waits for them, and re-layouts  6.36 us
  transfers between devices with their start and end apart: 39, of which 25 were waited for; matrix products, arithmetic and copies ran while one was open for 7% of the time, Pallas kernels for 6%

commit v1 on v0

--- a/solution.py
+++ b/solution.py
@@ -94,12 +94,13 @@
         at += size
 
 
-def stack(groups):
+def stack(groups, after=()):
     outs = [shape(sum(a.shape[0] for a in g), g[0].shape[1], g[0].dtype) for g in groups]
     return call(
         functools.partial(stack_kernel, [len(g) for g in groups]),
         outs,
         [a for g in groups for a in g],
+        after=after,
     )
 
 
@@ -120,10 +121,10 @@
         out_ref[:, k * width : (k + 1) * width] = in_ref[:, pl.ds(start, width)]
 
 
-def reorder(array, index, width):
+def reorder(array, index, width, after):
     outs = [shape(array.shape[0], array.shape[1], array.dtype)]
     return call(
-        functools.partial(reorder_kernel, width), outs, [index, array], vmem=8, smem=1
+        functools.partial(reorder_kernel, width), outs, [index, array], smem=1, after=after
     )[0]
 
 
@@ -208,6 +209,28 @@
     return result[0], result[1], result[2:]
 
 
+def split_kernel(core_ref, first_ref, second_ref, own_ref, other_ref):
+    rows, half = first_ref.shape[0], own_ref.shape[1]
+    core = core_ref[0]
+    own = pl.ds(pl.multiple_of(core * half, half), half)
+    other = pl.ds(pl.multiple_of((1 - core) * half, half), half)
+    own_ref[:rows, :] = first_ref[:, own]
+    own_ref[rows:, :] = second_ref[:, own]
+    other_ref[:rows, :] = first_ref[:, other]
+    other_ref[rows:, :] = second_ref[:, other]
+
+
+def merge_kernel(core_ref, own_ref, got_ref, first_ref, second_ref):
+    rows = own_ref.shape[0] // 2
+    core = core_ref[0]
+    own = pl.ds(pl.multiple_of(core * rows, rows), rows)
+    other = pl.ds(pl.multiple_of((1 - core) * rows, rows), rows)
+    first_ref[own, :] = own_ref[:rows, :]
+    first_ref[other, :] = got_ref[:rows, :]
+    second_ref[own, :] = own_ref[rows:, :]
+    second_ref[other, :] = got_ref[rows:, :]
+
+
 def pick_kernel(which_ref, first_ref, second_ref, out_ref):
     rows = out_ref.shape[0] // 2
     start = pl.multiple_of(which_ref[0] * rows, rows)
@@ -277,13 +300,33 @@
     def other_half(array):
         return lax.dynamic_slice_in_dim(array, (1 - core) * half, half, 1)
 
-    columns = lax.dynamic_slice_in_dim(projector, tp_place * column_count, column_count, 1)
-    for masks in ((8, 16, 24), (2, 4, 6)):
-        columns = stack([[columns] + [swap(columns, "fsdp", (m, m)) for m in masks]])[0]
-    columns_other = swap_core(columns)
+    sum_orders = (([1, 3, 4, 12], [3, 1, 12, 4]), ([4, 12, 1, 3], [12, 4, 3, 1]))
+    back_orders = [[o[::-1] for o in orders] for orders in sum_orders]
+    ranks = jnp.arange(rank, dtype=jnp.int32)
+    rank_tables = []
+    for orders in back_orders:
+        blocks = chip ^ table(core, [doubled(o) for o in orders])
+        rank_tables.append((blocks[:, None] * block + ranks[None, :block]).reshape(-1))
+
+    moments_own, moments_other = call(
+        split_kernel,
+        [shape(2 * rows, half, F32)] * 2,
+        [core[None], first_moment, second_moment],
+        smem=1,
+    )
+    moments_got = swap_core(moments_other)
+    projector_other = swap_core(projector)
+
+    grads_got = swap_core(other_half(grad_output))
     order = jnp.array([x + z for x in (0, 2, 4, 6) for z in (0, 8, 16, 24)], jnp.int32)
     index = jnp.concatenate([place ^ order, place ^ 1 ^ order])
-    act = reorder(activations, index, projector.shape[0])
+    act = reorder(activations, index, projector.shape[0], rank_tables)
+
+    columns = lax.dynamic_slice_in_dim(projector, tp_place * column_count, column_count, 1)
+    for masks, after in (((8, 16, 24), ()), ((2, 4, 6), (act, grads_got))):
+        got = [swap(columns, "fsdp", (m, m)) for m in masks]
+        columns = stack([[columns] + got], after)[0]
+    columns_other = swap_core(columns)
     depth = columns.shape[0]
     dims = (((0,), (1,)), ((), ()))
     own = lax.dot_general(columns, act[:, :depth], dims, preferred_element_type=F32)
@@ -291,32 +334,31 @@
     own = own.astype(BF)
 
     coords = stack([[own, swap(own, "tp", (1, 1))]])[0]
-    coords = stack([[coords] + [swap(coords, "tp", (m, m)) for m in (2, 4, 6)]])[0]
+    coords = stack(
+        [[coords] + [swap(coords, "tp", (m, m)) for m in (2, 4, 6)]],
+        [moments_got, projector_other],
+    )[0]
     coords_other = swap_core(coords)
 
     grads = jnp.concatenate(
-        [my_half(grad_output), swap_core(other_half(grad_output))], axis=0
-    )
-    moments = jnp.concatenate([first_moment, second_moment], axis=0)
-    moments_other = swap_core(other_half(moments))
-    moments_own = my_half(moments)
-    first = by_core(core, moments_own[:rows], moments_other[:rows], 0)
-    second = by_core(core, moments_own[rows:], moments_other[rows:], 0)
-    both = jnp.concatenate([projector, swap_core(projector)], axis=0)
-
-    sum_orders = (([1, 3, 4, 12], [3, 1, 12, 4]), ([4, 12, 1, 3], [12, 4, 3, 1]))
-    back_orders = [[o[::-1] for o in orders] for orders in sum_orders]
+        [my_half(grad_output), grads_got], axis=0
+    )
+    first, second = call(
+        merge_kernel,
+        [shape(2 * rows, half, F32)] * 2,
+        [core[None], moments_own, moments_got],
+        smem=1,
+    )
+    both = jnp.concatenate([projector, projector_other], axis=0)
+
     keep_index, send_index = [], []
     for orders in sum_orders:
         wanted = chip ^ table(core, [doubled(o[::-1]) for o in orders])
         position = 2 * (tp_place ^ (wanted >> 1)) + (wanted & 1)
         keep_index.append(position[:8])
         send_index.append(position[8:])
-    ranks = jnp.arange(rank, dtype=jnp.int32)
     factors = []
-    for orders in back_orders:
-        blocks = chip ^ table(core, [doubled(o) for o in orders])
-        wanted = (blocks[:, None] * block + ranks[None, :block]).reshape(-1)
+    for wanted in rank_tables:
         choose = (ranks[:, None] == wanted[None, :]).astype(BF)
         factors.append(jnp.dot(both, choose, preferred_element_type=F32).astype(BF))
 

time: 178 us -> 165 us (0.927)
  starting transfers between devices: 83.8 us -> 74.8 us
  local copies, waits for them, and re-layouts: 12.6 us -> 5.04 us
  waiting for transfers between devices: 60.9 us -> 68.2 us
    ppermute x39, starting transfers between devices: 83.8 us -> 74.8 us  [swap(): lax.ppermute(array, ('fsdp', 'tp'), [(i, i ^ scale * masks[i // inner % 2...]
    ppermute x39, waiting for transfers between devices: 60.9 us -> 68.2 us  [swap(): lax.ppermute(array, ('fsdp', 'tp'), [(i, i ^ scale * masks[i // inner % 2...]
    unnamed x32 -> x19, local copies, waits for them, and re-layouts: 6.36 us -> 2.27 us
    slice x3 -> x1, local copies, waits for them, and re-layouts: 2.17 us -> 0.01 us  [body(): ranks[None, :block]]
    pallas_call x19 -> x21, Pallas kernels: 11.2 us -> 9.43 us  [call(): pl.pallas_call(body, out_shape=list(outs), in_specs=specs, out_specs=[pl....]
  transfers between devices with their start and end apart: 39 -> 39, of which waited for: 25 -> 28; matrix products, arithmetic and copies ran while one was open for 7% -> 4% of each run, Pallas kernels for 6% -> 3%
where the time goes in v1:
time: 165 us
  starting transfers between devices  74.8 us (45%)
  waiting for transfers between devices  68.2 us (41%)
  Pallas kernels  9.43 us (6%)
  local copies, waits for them, and re-layouts  5.04 us (3%)
  matrix products  4.3 us (3%)
  other arithmetic  2.02 us (1%)
    ppermute x39, starting transfers between devices, swap(): lax.ppermute(array, ('fsdp', 'tp'), [(i, i ^ scale * masks[i // inner % 2...  74.8 us
    ppermute x39, waiting for transfers between devices, swap(): lax.ppermute(array, ('fsdp', 'tp'), [(i, i ^ scale * masks[i // inner % 2...  68.2 us
    pallas_call x21, Pallas kernels, call(): pl.pallas_call(body, out_shape=list(outs), in_specs=specs, out_specs=[pl....  9.43 us
  transfers between devices with their start and end apart: 39, of which 28 were waited for; matrix products, arithmetic and copies ran while one was open for 4% of the time, Pallas kernels for 3%

profile of v1, /device:TPU:1, one launch (start us, length us, event | category | flops | bytes accessed | tf_op | source)
XLA Modules:
  0.0 164.8 jit_solution(16161738741437248326)
XLA Ops:
  1.5 3.8 %collective-permute-start = (bf16[256,128]{1,0:T(8,128)(2,1)S(1)}, bf16[256,128]{1,0:T(8,128)(2,1)S(1)}, u32[]{:S(2)}, u32[]{:S(2)}) collective-permute-start(bf16[256,128]{1,0:T(8,128)(2,1)S(1)} %constant_dynamic-slice_fusion.2.refs_0_), channel_id=1, source_target_pairs={{0,64},{1,65},{2,66},{3,67},{4,68},{5,69},{6,70},{7,71},{8,72},{9,... | collective-permute-start | bytes 196616 | tf_op jit(solution)/shard_map/ppermute | solution.py:21
  5.4 5.1 %collective-permute-start.1 = (bf16[256,128]{1,0:T(8,128)(2,1)S(1)}, bf16[256,128]{1,0:T(8,128)(2,1)S(1)}, u32[]{:S(2)}, u32[]{:S(2)}) collective-permute-start(bf16[256,128]{1,0:T(8,128)(2,1)S(1)} %constant_dynamic-slice_fusion.2.refs_0_), channel_id=1, source_target_pairs={{0,128},{1,129},{2,130},{3,131},{4,132},{5,133},{6,134},{7,135},{8... | collective-permute-start | bytes 196616 | tf_op jit(solution)/shard_map/ppermute | solution.py:21
  10.5 1.6 constant_dynamic-slice_fusion
  12.1 1.3 collective-permute-start.6
  13.7 2.3 %collective-permute-done.2.refs_3_ = bf16[256,128]{1,0:T(8,128)(2,1)S(1)} collective-permute-done((bf16[256,128]{1,0:T(8,128)(2,1)S(1)}, bf16[256,128]{1,0:T(8,128)(2,1)S(1)}, u32[]{:S(2)}, u32[]{:S(2)}) %collective-permute-start.2) | collective-permute-done | bytes 65568 | tf_op jit(solution)/shard_map/ppermute | solution.py:21
  16.0 1.3 collective-permute-start.3
  17.3 2.5 %collective-permute-start.4 = (bf16[1024,128]{1,0:T(8,128)(2,1)S(1)}, bf16[1024,128]{1,0:T(8,128)(2,1)S(1)}, u32[]{:S(2)}, u32[]{:S(2)}) collective-permute-start(bf16[1024,128]{1,0:T(8,128)(2,1)S(1)} %shard_map.157.refs_0_), channel_id=1, source_target_pairs={{0,32},{1,33},{2,34},{3,35},{4,36},{5,37},{6,38},{7,39},{8,40},{9,... | collective-permute-start | bytes 786440 | tf_op jit(solution)/shard_map/ppermute | solution.py:21
  20.0 2.2 %copy-done = bf16[256,8192]{1,0:T(8,128)(2,1)S(1)} copy-done((bf16[256,8192]{1,0:T(8,128)(2,1)S(1)}, bf16[256,8192]{1,0:T(8,128)(2,1)}, u32[]{:S(2)}) %copy-start) | copy-done | bytes 4194328
  23.4 6.2 %collective-permute-done.4.refs_2_ = bf16[1024,128]{1,0:T(8,128)(2,1)S(1)} collective-permute-done((bf16[1024,128]{1,0:T(8,128)(2,1)S(1)}, bf16[1024,128]{1,0:T(8,128)(2,1)S(1)}, u32[]{:S(2)}, u32[]{:S(2)}) %collective-permute-start.4) | collective-permute-done | bytes 262176 | tf_op jit(solution)/shard_map/ppermute | solution.py:21
  29.6 3.5 %collective-permute-done.5.refs_3_ = bf16[1024,128]{1,0:T(8,128)(2,1)S(1)} collective-permute-done((bf16[1024,128]{1,0:T(8,128)(2,1)S(1)}, bf16[1024,128]{1,0:T(8,128)(2,1)S(1)}, u32[]{:S(2)}, u32[]{:S(2)}) %collective-permute-start.5) | collective-permute-done | bytes 262176 | tf_op jit(solution)/shard_map/ppermute | solution.py:21
  33.2 2.3 %collective-permute-start.7 = (bf16[4096,128]{1,0:T(8,128)(2,1)S(1)}, bf16[4096,128]{1,0:T(8,128)(2,1)S(1)}, u32[]{:S(2)}, u32[]{:S(2)}) collective-permute-start(bf16[4096,128]{1,0:T(8,128)(2,1)S(1)} %shard_map.159), channel_id=1, source_target_pairs={{0,8},{1,9},{2,10},{3,11},{4,12},{5,13},{6,14},{7,15},{8,0},{9,1},... | collective-permute-start | bytes 3145736 | tf_op jit(solution)/shard_map/ppermute | solution.py:21
  36.1 1.6 collective-permute-done.7
  40.3 2.3 %collective-permute-done.8.refs_1_ = bf16[128,256]{1,0:T(8,128)(2,1)S(1)} collective-permute-done((bf16[128,256]{1,0:T(8,128)(2,1)S(1)}, bf16[128,256]{1,0:T(8,128)(2,1)S(1)}, u32[]{:S(2)}, u32[]{:S(2)}) %collective-permute-start.8) | collective-permute-done | bytes 65568 | tf_op jit(solution)/shard_map/ppermute | solution.py:21
  42.6 3.0 %collective-permute-start.10 = (bf16[256,256]{1,0:T(8,128)(2,1)S(1)}, bf16[256,256]{1,0:T(8,128)(2,1)S(1)}, u32[]{:S(2)}, u32[]{:S(2)}) collective-permute-start(bf16[256,256]{1,0:T(8,128)(2,1)S(1)} %shard_map.160.refs_0_), channel_id=1, source_target_pairs={{0,4},{1,5},{2,6},{3,7},{4,0},{5,1},{6,2},{7,3},{8,12},{9,13},{10,... | collective-permute-start | bytes 393224 | tf_op jit(solution)/shard_map/ppermute | solution.py:21
  46.5 1.6 collective-permute-done.10.refs_2_
  48.1 3.4 %collective-permute-done.11.refs_3_ = bf16[256,256]{1,0:T(8,128)(2,1)S(1)} collective-permute-done((bf16[256,256]{1,0:T(8,128)(2,1)S(1)}, bf16[256,256]{1,0:T(8,128)(2,1)S(1)}, u32[]{:S(2)}, u32[]{:S(2)}) %collective-permute-start.11) | collective-permute-done | bytes 131104 | tf_op jit(solution)/shard_map/ppermute | solution.py:21
  51.5 2.3 %collective-permute-start.14 = (bf16[1024,256]{1,0:T(8,128)(2,1)S(1)}, bf16[1024,256]{1,0:T(8,128)(2,1)S(1)}, u32[]{:S(2)}, u32[]{:S(2)}) collective-permute-start(bf16[1024,256]{1,0:T(8,128)(2,1)S(1)} %shard_map.162.refs_1_), channel_id=1, source_target_pairs={{0,8},{1,9},{2,10},{3,11},{4,12},{5,13},{6,14},{7,15},{8,0},{9,1},... | collective-permute-start | bytes 1572872 | tf_op jit(solution)/shard_map/ppermute | solution.py:21
  54.1 1.3 collective-permute-done.14.refs_2_
  55.4 1.7 %shard_map.164 = (bf16[512,1280]{1,0:T(8,128)(2,1)S(1)}, bf16[512,512]{1,0:T(8,128)(2,1)S(1)}) custom-call(s32[16]{0:T(128)S(1)} %get-tuple-element.96.refs_0_, bf16[1024,256]{1,0:T(8,128)(2,1)S(1)} %shard_map.162.refs_1_, bf16[1024,256]{1,0:T(8,128)(2,1)S(1)} %collective-permute-done.14.refs_2_, bf16[512,1792]{1,0:T(8,128)(2,1)S(1)} %pad_maximum_fusion.refs_3_), custom_call_target="tpu_custom_call" | custom-call | flops 939524096 | bytes 4718656 | tf_op jit(solution)/shard_map/pallas_call | solution.py:63
  57.5 4.3 %collective-permute-start.16 = (bf16[512,512]{1,0:T(8,128)(2,1)S(1)}, bf16[512,512]{1,0:T(8,128)(2,1)S(1)}, u32[]{:S(2)}, u32[]{:S(2)}) collective-permute-start(bf16[512,512]{1,0:T(8,128)(2,1)S(1)} %get-tuple-element.46), channel_id=1, source_target_pairs={{0,64},{1,65},{2,66},{3,67},{4,68},{5,69},{6,70},{7,71},{8,200},{9... | collective-permute-start | bytes 1572872 | tf_op jit(solution)/shard_map/ppermute | solution.py:21
  61.9 1.7 %shard_map.163 = (f32[512,1280]{1,0:T(8,128)S(1)}, f32[512,512]{1,0:T(8,128)S(1)}) custom-call(s32[16]{0:T(128)S(1)} %get-tuple-element.95.refs_0_, bf16[1024,256]{1,0:T(8,128)(2,1)S(1)} %shard_map.162.refs_1_, bf16[1024,256]{1,0:T(8,128)(2,1)S(1)} %collective-permute-done.14.refs_2_, bf16[512,1792]{1,0:T(8,128)(2,1)S(1)} %pad_maximum_fusion.refs_3_), custom_call_target="tpu_custom_call" | custom-call | flops 939524096 | bytes 6553664 | tf_op jit(solution)/shard_map/pallas_call | solution.py:63
  63.6 9.9 %collective-permute-done.16.refs_3_ = bf16[512,512]{1,0:T(8,128)(2,1)S(1)} collective-permute-done((bf16[512,512]{1,0:T(8,128)(2,1)S(1)}, bf16[512,512]{1,0:T(8,128)(2,1)S(1)}, u32[]{:S(2)}, u32[]{:S(2)}) %collective-permute-start.16) | collective-permute-done | bytes 524320 | tf_op jit(solution)/shard_map/ppermute | solution.py:21
  73.4 1.6 collective-permute-done.15.refs_2_
  76.5 4.4 %collective-permute-start.19 = (f32[8,128]{1,0:T(8,128)S(1)}, f32[8,128]{1,0:T(8,128)S(1)}, u32[]{:S(2)}, u32[]{:S(2)}) collective-permute-start(f32[8,128]{1,0:T(8,128)S(1)} %get-tuple-element.51), channel_id=1, source_target_pairs={{0,8},{1,9},{2,10},{3,11},{4,12},{5,13},{6,14},{7,15},{8,0},{9,1},... | collective-permute-start | bytes 12296 | tf_op jit(solution)/shard_map/ppermute | solution.py:21
  81.7 3.1 %collective-permute-done.18.refs_3_ = bf16[256,512]{1,0:T(8,128)(2,1)S(1)} collective-permute-done((bf16[256,512]{1,0:T(8,128)(2,1)S(1)}, bf16[256,512]{1,0:T(8,128)(2,1)S(1)}, u32[]{:S(2)}, u32[]{:S(2)}) %collective-permute-start.18) | collective-permute-done | bytes 262176 | tf_op jit(solution)/shard_map/ppermute | solution.py:21
  85.4 4.4 %collective-permute-start.20 = (bf16[128,1280]{1,0:T(8,128)(2,1)S(1)}, bf16[128,1280]{1,0:T(8,128)(2,1)S(1)}, u32[]{:S(2)}, u32[]{:S(2)}) collective-permute-start(bf16[128,1280]{1,0:T(8,128)(2,1)S(1)} %get-tuple-element.54), channel_id=1, source_target_pairs={{0,64},{1,65},{2,66},{3,67},{4,68},{5,69},{6,70},{7,71},{8,200},{9... | collective-permute-start | bytes 983048 | tf_op jit(solution)/shard_map/ppermute | solution.py:21
  90.5 1.3 fusion.8.refs_7_.refs_1_
  91.9 3.2 %collective-permute-done.21.refs_3_ = bf16[128,512]{1,0:T(8,128)(2,1)S(1)} collective-permute-done((bf16[128,512]{1,0:T(8,128)(2,1)S(1)}, bf16[128,512]{1,0:T(8,128)(2,1)S(1)}, u32[]{:S(2)}, u32[]{:S(2)}) %collective-permute-start.21) | collective-permute-done | bytes 131104 | tf_op jit(solution)/shard_map/ppermute | solution.py:21
  95.1 2.0 %collective-permute-done.20.refs_2_ = bf16[128,1280]{1,0:T(8,128)(2,1)S(1)} collective-permute-done((bf16[128,1280]{1,0:T(8,128)(2,1)S(1)}, bf16[128,1280]{1,0:T(8,128)(2,1)S(1)}, u32[]{:S(2)}, u32[]{:S(2)}) %collective-permute-start.20) | collective-permute-done | bytes 327712 | tf_op jit(solution)/shard_map/ppermute | solution.py:21
  97.2 1.9 %collective-permute-start.23 = (bf16[64,1280]{1,0:T(8,128)(2,1)S(1)}, bf16[64,1280]{1,0:T(8,128)(2,1)S(1)}, u32[]{:S(2)}, u32[]{:S(2)}) collective-permute-start(bf16[64,1280]{1,0:T(8,128)(2,1)S(1)} %get-tuple-element.59), channel_id=1, source_target_pairs={{0,192},{1,193},{2,194},{3,195},{4,196},{5,197},{6,198},{7,199},{8... | collective-permute-start | bytes 491528 | tf_op jit(solution)/shard_map/ppermute | solution.py:21
  99.1 7.8 %collective-permute-start.25 = (f32[8,128]{1,0:T(8,128)S(1)}, f32[8,128]{1,0:T(8,128)S(1)}, u32[]{:S(2)}, u32[]{:S(2)}) collective-permute-start(f32[8,128]{1,0:T(8,128)S(1)} %get-tuple-element.64), channel_id=1, source_target_pairs={{0,8},{1,9},{2,10},{3,11},{4,12},{5,13},{6,14},{7,15},{8,0},{9,1},... | collective-permute-start | bytes 12296 | tf_op jit(solution)/shard_map/ppermute | solution.py:21
  106.9 1.3 fusion.9.refs_6_.refs_0_
  108.7 1.4 collective-permute-start.26
  110.5 3.1 %collective-permute-done.28.refs_3_ = bf16[64,512]{1,0:T(8,128)(2,1)S(1)} collective-permute-done((bf16[64,512]{1,0:T(8,128)(2,1)S(1)}, bf16[64,512]{1,0:T(8,128)(2,1)S(1)}, u32[]{:S(2)}, u32[]{:S(2)}) %collective-permute-start.28) | collective-permute-done | bytes 65568 | tf_op jit(solution)/shard_map/ppermute | solution.py:21
  113.6 2.9 %collective-permute-done.27.refs_1_ = bf16[64,1280]{1,0:T(8,128)(2,1)S(1)} collective-permute-done((bf16[64,1280]{1,0:T(8,128)(2,1)S(1)}, bf16[64,1280]{1,0:T(8,128)(2,1)S(1)}, u32[]{:S(2)}, u32[]{:S(2)}) %collective-permute-start.27) | collective-permute-done | bytes 163872 | tf_op jit(solution)/shard_map/ppermute | solution.py:21
  116.5 1.7 %collective-permute-start.29 = (bf16[128,1280]{1,0:T(8,128)(2,1)S(1)}, bf16[128,1280]{1,0:T(8,128)(2,1)S(1)}, u32[]{:S(2)}, u32[]{:S(2)}) collective-permute-start(bf16[128,1280]{1,0:T(8,128)(2,1)S(1)} %get-tuple-element.71.refs_0_), channel_id=1, source_target_pairs={{0,64},{1,65},{2,66},{3,67},{4,68},{5,69},{6,70},{7,71},{8,200},{9... | collective-permute-start | bytes 983048 | tf_op jit(solution)/shard_map/ppermute | solution.py:21
  118.3 1.9 %collective-permute-start.30 = (bf16[128,512]{1,0:T(8,128)(2,1)S(1)}, bf16[128,512]{1,0:T(8,128)(2,1)S(1)}, u32[]{:S(2)}, u32[]{:S(2)}) collective-permute-start(bf16[128,512]{1,0:T(8,128)(2,1)S(1)} %get-tuple-element.72.refs_2_), channel_id=1, source_target_pairs={{0,16},{1,17},{2,18},{3,19},{4,20},{5,21},{6,22},{7,23},{8,56},{9,... | collective-permute-start | bytes 393224 | tf_op jit(solution)/shard_map/ppermute | solution.py:21
  121.4 2.1 %collective-permute-done.30.refs_3_ = bf16[128,512]{1,0:T(8,128)(2,1)S(1)} collective-permute-done((bf16[128,512]{1,0:T(8,128)(2,1)S(1)}, bf16[128,512]{1,0:T(8,128)(2,1)S(1)}, u32[]{:S(2)}, u32[]{:S(2)}) %collective-permute-start.30) | collective-permute-done | bytes 131104 | tf_op jit(solution)/shard_map/ppermute | solution.py:21
  123.4 2.5 %collective-permute-done.29.refs_1_ = bf16[128,1280]{1,0:T(8,128)(2,1)S(1)} collective-permute-done((bf16[128,1280]{1,0:T(8,128)(2,1)S(1)}, bf16[128,1280]{1,0:T(8,128)(2,1)S(1)}, u32[]{:S(2)}, u32[]{:S(2)}) %collective-permute-start.29) | collective-permute-done | bytes 327712 | tf_op jit(solution)/shard_map/ppermute | solution.py:21
  126.1 1.9 %collective-permute-start.33 = (bf16[256,512]{1,0:T(8,128)(2,1)S(1)}, bf16[256,512]{1,0:T(8,128)(2,1)S(1)}, u32[]{:S(2)}, u32[]{:S(2)}) collective-permute-start(bf16[256,512]{1,0:T(8,128)(2,1)S(1)} %get-tuple-element.76.refs_2_), channel_id=1, source_target_pairs={{0,192},{1,193},{2,194},{3,195},{4,196},{5,197},{6,198},{7,199},{8... | collective-permute-start | bytes 786440 | tf_op jit(solution)/shard_map/ppermute | solution.py:21
  127.9 5.9 %collective-permute-start.34 = (f32[8,128]{1,0:T(8,128)S(1)}, f32[8,128]{1,0:T(8,128)S(1)}, u32[]{:S(2)}, u32[]{:S(2)}) collective-permute-start(f32[8,128]{1,0:T(8,128)S(1)} %get-tuple-element.77), channel_id=1, source_target_pairs={{0,8},{1,9},{2,10},{3,11},{4,12},{5,13},{6,14},{7,15},{8,0},{9,1},... | collective-permute-start | bytes 12296 | tf_op jit(solution)/shard_map/ppermute | solution.py:21
  135.9 4.8 %collective-permute-start.35 = (bf16[512,1280]{1,0:T(8,128)(2,1)S(1)}, bf16[512,1280]{1,0:T(8,128)(2,1)S(1)}, u32[]{:S(2)}, u32[]{:S(2)}) collective-permute-start(bf16[512,1280]{1,0:T(8,128)(2,1)S(1)} %get-tuple-element.78.refs_2_), channel_id=1, source_target_pairs={{0,16},{1,17},{2,18},{3,19},{4,20},{5,21},{6,22},{7,23},{8,56},{9,... | collective-permute-start | bytes 3932168 | tf_op jit(solution)/shard_map/ppermute | solution.py:21
  141.7 2.2 %collective-permute-start.37 = (f32[8,128]{1,0:T(8,128)S(1)}, f32[8,128]{1,0:T(8,128)S(1)}, u32[]{:S(2)}, u32[]{:S(2)}) collective-permute-start(f32[8,128]{1,0:T(8,128)S(1)} %get-tuple-element.80), channel_id=1, source_target_pairs={{0,8},{1,9},{2,10},{3,11},{4,12},{5,13},{6,14},{7,15},{8,0},{9,1},... | collective-permute-start | bytes 12296 | tf_op jit(solution)/shard_map/ppermute | solution.py:21
  145.9 6.9 %collective-permute-done.36.refs_3_ = bf16[512,512]{1,0:T(8,128)(2,1)S(1)} collective-permute-done((bf16[512,512]{1,0:T(8,128)(2,1)S(1)}, bf16[512,512]{1,0:T(8,128)(2,1)S(1)}, u32[]{:S(2)}, u32[]{:S(2)}) %collective-permute-start.36) | collective-permute-done | bytes 524320 | tf_op jit(solution)/shard_map/ppermute | solution.py:21
  152.7 3.2 %collective-permute-done.35.refs_2_ = bf16[512,1280]{1,0:T(8,128)(2,1)S(1)} collective-permute-done((bf16[512,1280]{1,0:T(8,128)(2,1)S(1)}, bf16[512,1280]{1,0:T(8,128)(2,1)S(1)}, u32[]{:S(2)}, u32[]{:S(2)}) %collective-permute-start.35) | collective-permute-done | bytes 1310752 | tf_op jit(solution)/shard_map/ppermute | solution.py:21
  156.6 4.4 %collective-permute-start.38 = (bf16[256,1792]{1,0:T(8,128)(2,1)S(1)}, bf16[256,1792]{1,0:T(8,128)(2,1)S(1)}, u32[]{:S(2)}, u32[]{:S(2)}) collective-permute-start(bf16[256,1792]{1,0:T(8,128)(2,1)S(1)} %shard_map.177), channel_id=1, source_target_pairs={{0,8},{1,9},{2,10},{3,11},{4,12},{5,13},{6,14},{7,15},{8,0},{9,1},... | collective-permute-start | bytes 2752520 | tf_op jit(solution)/shard_map/ppermute | solution.py:21
  161.7 1.4 collective-permute-done.38
  163.1 1.6 maximum_select_fusion
  (91 shorter events, 19.6 us)
Async XLA Ops:
  0.6 12.8 %copy-start.7 = (s32[16]{0:T(128)S(1)}, s32[16]{0:T(128)}, u32[]{:S(2)}) copy-start(s32[16]{0:T(128)} %constant.36.clone) | copy-start | bytes 196
  0.6 12.8 %copy-start.8 = (s32[16]{0:T(128)S(1)}, s32[16]{0:T(128)}, u32[]{:S(2)}) copy-start(s32[16]{0:T(128)} %constant.37.clone) | copy-start | bytes 196
  0.7 12.8 %copy-start.5 = (s32[16]{0:T(128)S(1)}, s32[16]{0:T(128)}, u32[]{:S(2)}) copy-start(s32[16]{0:T(128)} %constant.38.clone) | copy-start | bytes 196
  0.7 12.8 %copy-start.6 = (s32[16]{0:T(128)S(1)}, s32[16]{0:T(128)}, u32[]{:S(2)}) copy-start(s32[16]{0:T(128)} %constant.39.clone) | copy-start | bytes 196
  1.5 12.1 %collective-permute-start = (bf16[256,128]{1,0:T(8,128)(2,1)S(1)}, bf16[256,128]{1,0:T(8,128)(2,1)S(1)}, u32[]{:S(2)}, u32[]{:S(2)}) collective-permute-start(bf16[256,128]{1,0:T(8,128)(2,1)S(1)} %constant_dynamic-slice_fusion.2.refs_0_), channel_id=1, source_target_pairs={{0,64},{1,65},{2,66},{3,67},{4,68},{5,69},{6,70},{7,71},{8,72},{9,... | collective-permute-start | bytes 196616 | tf_op jit(solution)/shard_map/ppermute | solution.py:21
  5.4 8.3 %collective-permute-start.1 = (bf16[256,128]{1,0:T(8,128)(2,1)S(1)}, bf16[256,128]{1,0:T(8,128)(2,1)S(1)}, u32[]{:S(2)}, u32[]{:S(2)}) collective-permute-start(bf16[256,128]{1,0:T(8,128)(2,1)S(1)} %constant_dynamic-slice_fusion.2.refs_0_), channel_id=1, source_target_pairs={{0,128},{1,129},{2,130},{3,131},{4,132},{5,133},{6,134},{7,135},{8... | collective-permute-start | bytes 196616 | tf_op jit(solution)/shard_map/ppermute | solution.py:21
  10.5 5.5 %collective-permute-start.2 = (bf16[256,128]{1,0:T(8,128)(2,1)S(1)}, bf16[256,128]{1,0:T(8,128)(2,1)S(1)}, u32[]{:S(2)}, u32[]{:S(2)}) collective-permute-start(bf16[256,128]{1,0:T(8,128)(2,1)S(1)} %constant_dynamic-slice_fusion.2.refs_0_), channel_id=1, source_target_pairs={{0,192},{1,193},{2,194},{3,195},{4,196},{5,197},{6,198},{7,199},{8... | collective-permute-start | bytes 196616 | tf_op jit(solution)/shard_map/ppermute | solution.py:21
  10.5 9.5 %copy-start.4 = (s32[16]{0:T(128)S(1)}, s32[16]{0:T(128)}, u32[]{:S(2)}) copy-start(s32[16]{0:T(128)} %constant.40.clone) | copy-start | bytes 196
  12.1 21.0 %collective-permute-start.6 = (bf16[256,1792]{1,0:T(8,128)(2,1)S(1)}, bf16[256,1792]{1,0:T(8,128)(2,1)S(1)}, u32[]{:S(2)}, u32[]{:S(2)}) collective-permute-start(bf16[256,1792]{1,0:T(8,128)(2,1)S(1)} %get-tuple-element.82), channel_id=1, source_target_pairs={{0,8},{1,9},{2,10},{3,11},{4,12},{5,13},{6,14},{7,15},{8,0},{9,1},... | collective-permute-start | bytes 2752520 | tf_op jit(solution)/shard_map/ppermute | solution.py:21
  16.0 7.4 %collective-permute-start.3 = (bf16[1024,128]{1,0:T(8,128)(2,1)S(1)}, bf16[1024,128]{1,0:T(8,128)(2,1)S(1)}, u32[]{:S(2)}, u32[]{:S(2)}) collective-permute-start(bf16[1024,128]{1,0:T(8,128)(2,1)S(1)} %shard_map.157.refs_0_), channel_id=1, source_target_pairs={{0,16},{1,17},{2,18},{3,19},{4,20},{5,21},{6,22},{7,23},{8,24},{9,... | collective-permute-start | bytes 786440 | tf_op jit(solution)/shard_map/ppermute | solution.py:21
  17.3 12.3 %collective-permute-start.4 = (bf16[1024,128]{1,0:T(8,128)(2,1)S(1)}, bf16[1024,128]{1,0:T(8,128)(2,1)S(1)}, u32[]{:S(2)}, u32[]{:S(2)}) collective-permute-start(bf16[1024,128]{1,0:T(8,128)(2,1)S(1)} %shard_map.157.refs_0_), channel_id=1, source_target_pairs={{0,32},{1,33},{2,34},{3,35},{4,36},{5,37},{6,38},{7,39},{8,40},{9,... | collective-permute-start | bytes 786440 | tf_op jit(solution)/shard_map/ppermute | solution.py:21
  19.7 13.4 %collective-permute-start.5 = (bf16[1024,128]{1,0:T(8,128)(2,1)S(1)}, bf16[1024,128]{1,0:T(8,128)(2,1)S(1)}, u32[]{:S(2)}, u32[]{:S(2)}) collective-permute-start(bf16[1024,128]{1,0:T(8,128)(2,1)S(1)} %shard_map.157.refs_0_), channel_id=1, source_target_pairs={{0,48},{1,49},{2,50},{3,51},{4,52},{5,53},{6,54},{7,55},{8,56},{9,... | collective-permute-start | bytes 786440 | tf_op jit(solution)/shard_map/ppermute | solution.py:21
  20.0 2.2 %copy-start = (bf16[256,8192]{1,0:T(8,128)(2,1)S(1)}, bf16[256,8192]{1,0:T(8,128)(2,1)}, u32[]{:S(2)}) copy-start(bf16[256,8192]{1,0:T(8,128)(2,1)} %refs_1_.2) | copy-start | bytes 12582916
  23.3 12.1 %copy-start.3 = (bf16[256,1024]{1,0:T(8,128)(2,1)S(1)}, bf16[256,1024]{1,0:T(8,128)(2,1)}, u32[]{:S(2)}) copy-start(bf16[256,1024]{1,0:T(8,128)(2,1)} %param.16) | copy-start | bytes 1572868
  23.4 12.2 %copy-start.1 = (f32[32,3584]{1,0:T(8,128)S(1)}, f32[32,3584]{1,0:T(8,128)}, u32[]{:S(2)}) copy-start(f32[32,3584]{1,0:T(8,128)} %refs_1_.3) | copy-start | bytes 1376260
  23.4 12.2 %copy-start.2 = (f32[32,3584]{1,0:T(8,128)S(1)}, f32[32,3584]{1,0:T(8,128)}, u32[]{:S(2)}) copy-start(f32[32,3584]{1,0:T(8,128)} %refs_2_.1) | copy-start | bytes 1376260
  33.2 4.6 %collective-permute-start.7 = (bf16[4096,128]{1,0:T(8,128)(2,1)S(1)}, bf16[4096,128]{1,0:T(8,128)(2,1)S(1)}, u32[]{:S(2)}, u32[]{:S(2)}) collective-permute-start(bf16[4096,128]{1,0:T(8,128)(2,1)S(1)} %shard_map.159), channel_id=1, source_target_pairs={{0,8},{1,9},{2,10},{3,11},{4,12},{5,13},{6,14},{7,15},{8,0},{9,1},... | collective-permute-start | bytes 3145736 | tf_op jit(solution)/shard_map/ppermute | solution.py:21
  35.4 11.1 %collective-permute-start.13 = (bf16[256,1024]{1,0:T(8,128)(2,1)S(1)}, bf16[256,1024]{1,0:T(8,128)(2,1)S(1)}, u32[]{:S(2)}, u32[]{:S(2)}) collective-permute-start(bf16[256,1024]{1,0:T(8,128)(2,1)S(1)} %copy-done.3), channel_id=1, source_target_pairs={{0,8},{1,9},{2,10},{3,11},{4,12},{5,13},{6,14},{7,15},{8,0},{9,1},... | collective-permute-start | bytes 1572872 | tf_op jit(solution)/shard_map/ppermute | solution.py:21
  35.6 10.9 %collective-permute-start.12 = (f32[64,1792]{1,0:T(8,128)S(1)}, f32[64,1792]{1,0:T(8,128)S(1)}, u32[]{:S(2)}, u32[]{:S(2)}) collective-permute-start(f32[64,1792]{1,0:T(8,128)S(1)} %get-tuple-element.42), channel_id=1, source_target_pairs={{0,8},{1,9},{2,10},{3,11},{4,12},{5,13},{6,14},{7,15},{8,0},{9,1},... | collective-permute-start | bytes 1376264 | tf_op jit(solution)/shard_map/ppermute | solution.py:21
  39.4 3.2 %collective-permute-start.8 = (bf16[128,256]{1,0:T(8,128)(2,1)S(1)}, bf16[128,256]{1,0:T(8,128)(2,1)S(1)}, u32[]{:S(2)}, u32[]{:S(2)}) collective-permute-start(bf16[128,256]{1,0:T(8,128)(2,1)S(1)} %fusion.13.refs_0_), channel_id=1, source_target_pairs={{0,1},{1,0},{2,3},{3,2},{4,5},{5,4},{6,7},{7,6},{8,9},{9,8},{10,11... | collective-permute-start | bytes 196616 | tf_op jit(solution)/shard_map/ppermute | solution.py:21
  42.6 5.4 %collective-permute-start.10 = (bf16[256,256]{1,0:T(8,128)(2,1)S(1)}, bf16[256,256]{1,0:T(8,128)(2,1)S(1)}, u32[]{:S(2)}, u32[]{:S(2)}) collective-permute-start(bf16[256,256]{1,0:T(8,128)(2,1)S(1)} %shard_map.160.refs_0_), channel_id=1, source_target_pairs={{0,4},{1,5},{2,6},{3,7},{4,0},{5,1},{6,2},{7,3},{8,12},{9,13},{10,... | collective-permute-start | bytes 393224 | tf_op jit(solution)/shard_map/ppermute | solution.py:21
  45.6 5.8 %collective-permute-start.11 = (bf16[256,256]{1,0:T(8,128)(2,1)S(1)}, bf16[256,256]{1,0:T(8,128)(2,1)S(1)}, u32[]{:S(2)}, u32[]{:S(2)}) collective-permute-start(bf16[256,256]{1,0:T(8,128)(2,1)S(1)} %shard_map.160.refs_0_), channel_id=1, source_target_pairs={{0,6},{1,7},{2,4},{3,5},{4,2},{5,3},{6,0},{7,1},{8,14},{9,15},{10,... | collective-permute-start | bytes 393224 | tf_op jit(solution)/shard_map/ppermute | solution.py:21
  46.4 5.1 %collective-permute-start.9 = (bf16[256,256]{1,0:T(8,128)(2,1)S(1)}, bf16[256,256]{1,0:T(8,128)(2,1)S(1)}, u32[]{:S(2)}, u32[]{:S(2)}) collective-permute-start(bf16[256,256]{1,0:T(8,128)(2,1)S(1)} %shard_map.160.refs_0_), channel_id=1, source_target_pairs={{0,2},{1,3},{2,0},{3,1},{4,6},{5,7},{6,4},{7,5},{8,10},{9,11},{10,... | collective-permute-start | bytes 393224 | tf_op jit(solution)/shard_map/ppermute | solution.py:21
  51.5 3.9 %collective-permute-start.14 = (bf16[1024,256]{1,0:T(8,128)(2,1)S(1)}, bf16[1024,256]{1,0:T(8,128)(2,1)S(1)}, u32[]{:S(2)}, u32[]{:S(2)}) collective-permute-start(bf16[1024,256]{1,0:T(8,128)(2,1)S(1)} %shard_map.162.refs_1_), channel_id=1, source_target_pairs={{0,8},{1,9},{2,10},{3,11},{4,12},{5,13},{6,14},{7,15},{8,0},{9,1},... | collective-permute-start | bytes 1572872 | tf_op jit(solution)/shard_map/ppermute | solution.py:21
  57.1 17.9 %collective-permute-start.15 = (bf16[512,1280]{1,0:T(8,128)(2,1)S(1)}, bf16[512,1280]{1,0:T(8,128)(2,1)S(1)}, u32[]{:S(2)}, u32[]{:S(2)}) collective-permute-start(bf16[512,1280]{1,0:T(8,128)(2,1)S(1)} %get-tuple-element.45), channel_id=1, source_target_pairs={{0,16},{1,17},{2,18},{3,19},{4,20},{5,21},{6,22},{7,23},{8,56},{9,... | collective-permute-start | bytes 3932168 | tf_op jit(solution)/shard_map/ppermute | solution.py:21
  57.5 15.9 %collective-permute-start.16 = (bf16[512,512]{1,0:T(8,128)(2,1)S(1)}, bf16[512,512]{1,0:T(8,128)(2,1)S(1)}, u32[]{:S(2)}, u32[]{:S(2)}) collective-permute-start(bf16[512,512]{1,0:T(8,128)(2,1)S(1)} %get-tuple-element.46), channel_id=1, source_target_pairs={{0,64},{1,65},{2,66},{3,67},{4,68},{5,69},{6,70},{7,71},{8,200},{9... | collective-permute-start | bytes 1572872 | tf_op jit(solution)/shard_map/ppermute | solution.py:21
  75.4 9.8 %collective-permute-start.17 = (bf16[256,1280]{1,0:T(8,128)(2,1)S(1)}, bf16[256,1280]{1,0:T(8,128)(2,1)S(1)}, u32[]{:S(2)}, u32[]{:S(2)}) collective-permute-start(bf16[256,1280]{1,0:T(8,128)(2,1)S(1)} %get-tuple-element.49), channel_id=1, source_target_pairs={{0,48},{1,49},{2,50},{3,51},{4,52},{5,53},{6,54},{7,55},{8,24},{9,... | collective-permute-start | bytes 1966088 | tf_op jit(solution)/shard_map/ppermute | solution.py:21
  75.5 9.4 %collective-permute-start.18 = (bf16[256,512]{1,0:T(8,128)(2,1)S(1)}, bf16[256,512]{1,0:T(8,128)(2,1)S(1)}, u32[]{:S(2)}, u32[]{:S(2)}) collective-permute-start(bf16[256,512]{1,0:T(8,128)(2,1)S(1)} %get-tuple-element.50), channel_id=1, source_target_pairs={{0,192},{1,193},{2,194},{3,195},{4,196},{5,197},{6,198},{7,199},{8... | collective-permute-start | bytes 786440 | tf_op jit(solution)/shard_map/ppermute | solution.py:21
  76.5 5.2 %collective-permute-start.19 = (f32[8,128]{1,0:T(8,128)S(1)}, f32[8,128]{1,0:T(8,128)S(1)}, u32[]{:S(2)}, u32[]{:S(2)}) collective-permute-start(f32[8,128]{1,0:T(8,128)S(1)} %get-tuple-element.51), channel_id=1, source_target_pairs={{0,8},{1,9},{2,10},{3,11},{4,12},{5,13},{6,14},{7,15},{8,0},{9,1},... | collective-permute-start | bytes 12296 | tf_op jit(solution)/shard_map/ppermute | solution.py:21
  85.4 11.7 %collective-permute-start.20 = (bf16[128,1280]{1,0:T(8,128)(2,1)S(1)}, bf16[128,1280]{1,0:T(8,128)(2,1)S(1)}, u32[]{:S(2)}, u32[]{:S(2)}) collective-permute-start(bf16[128,1280]{1,0:T(8,128)(2,1)S(1)} %get-tuple-element.54), channel_id=1, source_target_pairs={{0,64},{1,65},{2,66},{3,67},{4,68},{5,69},{6,70},{7,71},{8,200},{9... | collective-permute-start | bytes 983048 | tf_op jit(solution)/shard_map/ppermute | solution.py:21
  89.8 5.3 %collective-permute-start.21 = (bf16[128,512]{1,0:T(8,128)(2,1)S(1)}, bf16[128,512]{1,0:T(8,128)(2,1)S(1)}, u32[]{:S(2)}, u32[]{:S(2)}) collective-permute-start(bf16[128,512]{1,0:T(8,128)(2,1)S(1)} %get-tuple-element.55), channel_id=1, source_target_pairs={{0,16},{1,17},{2,18},{3,19},{4,20},{5,21},{6,22},{7,23},{8,56},{9,... | collective-permute-start | bytes 393224 | tf_op jit(solution)/shard_map/ppermute | solution.py:21
  90.5 1.3 collective-permute-start.22
  97.2 11.0 %collective-permute-start.23 = (bf16[64,1280]{1,0:T(8,128)(2,1)S(1)}, bf16[64,1280]{1,0:T(8,128)(2,1)S(1)}, u32[]{:S(2)}, u32[]{:S(2)}) collective-permute-start(bf16[64,1280]{1,0:T(8,128)(2,1)S(1)} %get-tuple-element.59), channel_id=1, source_target_pairs={{0,192},{1,193},{2,194},{3,195},{4,196},{5,197},{6,198},{7,199},{8... | collective-permute-start | bytes 491528 | tf_op jit(solution)/shard_map/ppermute | solution.py:21
  99.1 9.1 %collective-permute-start.24 = (bf16[64,512]{1,0:T(8,128)(2,1)S(1)}, bf16[64,512]{1,0:T(8,128)(2,1)S(1)}, u32[]{:S(2)}, u32[]{:S(2)}) collective-permute-start(bf16[64,512]{1,0:T(8,128)(2,1)S(1)} %get-tuple-element.60), channel_id=1, source_target_pairs={{0,48},{1,49},{2,50},{3,51},{4,52},{5,53},{6,54},{7,55},{8,24},{9,... | collective-permute-start | bytes 196616 | tf_op jit(solution)/shard_map/ppermute | solution.py:21
  99.1 9.1 %collective-permute-start.25 = (f32[8,128]{1,0:T(8,128)S(1)}, f32[8,128]{1,0:T(8,128)S(1)}, u32[]{:S(2)}, u32[]{:S(2)}) collective-permute-start(f32[8,128]{1,0:T(8,128)S(1)} %get-tuple-element.64), channel_id=1, source_target_pairs={{0,8},{1,9},{2,10},{3,11},{4,12},{5,13},{6,14},{7,15},{8,0},{9,1},... | collective-permute-start | bytes 12296 | tf_op jit(solution)/shard_map/ppermute | solution.py:21
  108.7 7.8 %collective-permute-start.26 = (f32[64,1792]{1,0:T(8,128)S(1)}, f32[64,1792]{1,0:T(8,128)S(1)}, u32[]{:S(2)}, u32[]{:S(2)}) collective-permute-start(f32[64,1792]{1,0:T(8,128)S(1)} %shard_map.170), channel_id=1, source_target_pairs={{0,8},{1,9},{2,10},{3,11},{4,12},{5,13},{6,14},{7,15},{8,0},{9,1},... | collective-permute-start | bytes 1376264 | tf_op jit(solution)/shard_map/ppermute | solution.py:21
  110.1 6.4 %collective-permute-start.27 = (bf16[64,1280]{1,0:T(8,128)(2,1)S(1)}, bf16[64,1280]{1,0:T(8,128)(2,1)S(1)}, u32[]{:S(2)}, u32[]{:S(2)}) collective-permute-start(bf16[64,1280]{1,0:T(8,128)(2,1)S(1)} %get-tuple-element.69.refs_0_), channel_id=1, source_target_pairs={{0,192},{1,193},{2,194},{3,195},{4,196},{5,197},{6,198},{7,199},{8... | collective-permute-start | bytes 491528 | tf_op jit(solution)/shard_map/ppermute | solution.py:21
  110.5 3.1 %collective-permute-start.28 = (bf16[64,512]{1,0:T(8,128)(2,1)S(1)}, bf16[64,512]{1,0:T(8,128)(2,1)S(1)}, u32[]{:S(2)}, u32[]{:S(2)}) collective-permute-start(bf16[64,512]{1,0:T(8,128)(2,1)S(1)} %get-tuple-element.70.refs_2_), channel_id=1, source_target_pairs={{0,48},{1,49},{2,50},{3,51},{4,52},{5,53},{6,54},{7,55},{8,24},{9,... | collective-permute-start | bytes 196616 | tf_op jit(solution)/shard_map/ppermute | solution.py:21
  116.5 9.4 %collective-permute-start.29 = (bf16[128,1280]{1,0:T(8,128)(2,1)S(1)}, bf16[128,1280]{1,0:T(8,128)(2,1)S(1)}, u32[]{:S(2)}, u32[]{:S(2)}) collective-permute-start(bf16[128,1280]{1,0:T(8,128)(2,1)S(1)} %get-tuple-element.71.refs_0_), channel_id=1, source_target_pairs={{0,64},{1,65},{2,66},{3,67},{4,68},{5,69},{6,70},{7,71},{8,200},{9... | collective-permute-start | bytes 983048 | tf_op jit(solution)/shard_map/ppermute | solution.py:21
  118.3 5.2 %collective-permute-start.30 = (bf16[128,512]{1,0:T(8,128)(2,1)S(1)}, bf16[128,512]{1,0:T(8,128)(2,1)S(1)}, u32[]{:S(2)}, u32[]{:S(2)}) collective-permute-start(bf16[128,512]{1,0:T(8,128)(2,1)S(1)} %get-tuple-element.72.refs_2_), channel_id=1, source_target_pairs={{0,16},{1,17},{2,18},{3,19},{4,20},{5,21},{6,22},{7,23},{8,56},{9,... | collective-permute-start | bytes 393224 | tf_op jit(solution)/shard_map/ppermute | solution.py:21
  120.2 1.2 collective-permute-start.31
  126.0 9.8 %collective-permute-start.32 = (bf16[256,1280]{1,0:T(8,128)(2,1)S(1)}, bf16[256,1280]{1,0:T(8,128)(2,1)S(1)}, u32[]{:S(2)}, u32[]{:S(2)}) collective-permute-start(bf16[256,1280]{1,0:T(8,128)(2,1)S(1)} %get-tuple-element.75.refs_0_), channel_id=1, source_target_pairs={{0,48},{1,49},{2,50},{3,51},{4,52},{5,53},{6,54},{7,55},{8,24},{9,... | collective-permute-start | bytes 1966088 | tf_op jit(solution)/shard_map/ppermute | solution.py:21
  126.1 9.5 %collective-permute-start.33 = (bf16[256,512]{1,0:T(8,128)(2,1)S(1)}, bf16[256,512]{1,0:T(8,128)(2,1)S(1)}, u32[]{:S(2)}, u32[]{:S(2)}) collective-permute-start(bf16[256,512]{1,0:T(8,128)(2,1)S(1)} %get-tuple-element.76.refs_2_), channel_id=1, source_target_pairs={{0,192},{1,193},{2,194},{3,195},{4,196},{5,197},{6,198},{7,199},{8... | collective-permute-start | bytes 786440 | tf_op jit(solution)/shard_map/ppermute | solution.py:21
  127.9 6.8 %collective-permute-start.34 = (f32[8,128]{1,0:T(8,128)S(1)}, f32[8,128]{1,0:T(8,128)S(1)}, u32[]{:S(2)}, u32[]{:S(2)}) collective-permute-start(f32[8,128]{1,0:T(8,128)S(1)} %get-tuple-element.77), channel_id=1, source_target_pairs={{0,8},{1,9},{2,10},{3,11},{4,12},{5,13},{6,14},{7,15},{8,0},{9,1},... | collective-permute-start | bytes 12296 | tf_op jit(solution)/shard_map/ppermute | solution.py:21
  135.9 20.0 %collective-permute-start.35 = (bf16[512,1280]{1,0:T(8,128)(2,1)S(1)}, bf16[512,1280]{1,0:T(8,128)(2,1)S(1)}, u32[]{:S(2)}, u32[]{:S(2)}) collective-permute-start(bf16[512,1280]{1,0:T(8,128)(2,1)S(1)} %get-tuple-element.78.refs_2_), channel_id=1, source_target_pairs={{0,16},{1,17},{2,18},{3,19},{4,20},{5,21},{6,22},{7,23},{8,56},{9,... | collective-permute-start | bytes 3932168 | tf_op jit(solution)/shard_map/ppermute | solution.py:21
  140.8 12.0 %collective-permute-start.36 = (bf16[512,512]{1,0:T(8,128)(2,1)S(1)}, bf16[512,512]{1,0:T(8,128)(2,1)S(1)}, u32[]{:S(2)}, u32[]{:S(2)}) collective-permute-start(bf16[512,512]{1,0:T(8,128)(2,1)S(1)} %get-tuple-element.79.refs_3_), channel_id=1, source_target_pairs={{0,64},{1,65},{2,66},{3,67},{4,68},{5,69},{6,70},{7,71},{8,200},{9... | collective-permute-start | bytes 1572872 | tf_op jit(solution)/shard_map/ppermute | solution.py:21
  141.7 3.1 %collective-permute-start.37 = (f32[8,128]{1,0:T(8,128)S(1)}, f32[8,128]{1,0:T(8,128)S(1)}, u32[]{:S(2)}, u32[]{:S(2)}) collective-permute-start(f32[8,128]{1,0:T(8,128)S(1)} %get-tuple-element.80), channel_id=1, source_target_pairs={{0,8},{1,9},{2,10},{3,11},{4,12},{5,13},{6,14},{7,15},{8,0},{9,1},... | collective-permute-start | bytes 12296 | tf_op jit(solution)/shard_map/ppermute | solution.py:21
  156.6 6.5 %collective-permute-start.38 = (bf16[256,1792]{1,0:T(8,128)(2,1)S(1)}, bf16[256,1792]{1,0:T(8,128)(2,1)S(1)}, u32[]{:S(2)}, u32[]{:S(2)}) collective-permute-start(bf16[256,1792]{1,0:T(8,128)(2,1)S(1)} %shard_map.177), channel_id=1, source_target_pairs={{0,8},{1,9},{2,10},{3,11},{4,12},{5,13},{6,14},{7,15},{8,0},{9,1},... | collective-permute-start | bytes 2752520 | tf_op jit(solution)/shard_map/ppermute | solution.py:21

commit v2 on v1

--- a/solution.py
+++ b/solution.py
@@ -180,10 +180,11 @@
 
 
 def adam_kernel(count, *refs):
-    kept, got = refs[:count], refs[count : 2 * count]
-    first_ref, second_ref = refs[2 * count : 2 * count + 2]
-    new_first_ref, new_second_ref = refs[2 * count + 2 : 2 * count + 4]
-    directions = refs[2 * count + 4 :]
+    core_ref, kept, got = refs[0], refs[1 : 1 + count], refs[1 + count : 1 + 2 * count]
+    first_ref, second_ref, new_first_ref, new_second_ref, other_ref = refs[
+        1 + 2 * count : 6 + 2 * count
+    ]
+    directions = refs[6 + 2 * count :]
     at = 0
     for k, g, d in zip(kept, got, directions):
         span = slice(at, at + k.shape[1])
@@ -196,17 +197,22 @@
         d[...] = (new_first / first_fix / (jnp.sqrt(new_second / second_fix) + 1e-08)).astype(
             d.dtype
         )
-
-
-def adam(kept, got, first, second, after):
-    outs = [shape(*first.shape, F32)] * 2 + [shape(*k.shape, BF) for k in kept]
+    rows = other_ref.shape[0] // 2
+    start = pl.multiple_of((1 - core_ref[0]) * rows, rows)
+    other_ref[:rows, :] = new_first_ref[pl.ds(start, rows), :]
+    other_ref[rows:, :] = new_second_ref[pl.ds(start, rows), :]
+
+
+def adam(core, kept, got, first, second, after):
+    outs = [shape(*first.shape, F32)] * 3 + [shape(*k.shape, BF) for k in kept]
     result = call(
         functools.partial(adam_kernel, len(kept)),
         outs,
-        [*kept, *got, first, second],
+        [core[None], *kept, *got, first, second],
+        smem=1,
         after=after,
     )
-    return result[0], result[1], result[2:]
+    return *result[:3], result[3:]
 
 
 def split_kernel(core_ref, first_ref, second_ref, own_ref, other_ref):
@@ -229,13 +235,6 @@
     first_ref[other, :] = got_ref[:rows, :]
     second_ref[own, :] = own_ref[rows:, :]
     second_ref[other, :] = got_ref[rows:, :]
-
-
-def pick_kernel(which_ref, first_ref, second_ref, out_ref):
-    rows = out_ref.shape[0] // 2
-    start = pl.multiple_of(which_ref[0] * rows, rows)
-    out_ref[:rows, :] = first_ref[pl.ds(start, rows), :]
-    out_ref[rows:, :] = second_ref[pl.ds(start, rows), :]
 
 
 def join_kernel(core_ref, first_ref, second_ref, other_ref, out_first_ref, out_second_ref):
@@ -375,16 +374,12 @@
         kept, sent, mark = halve(kept, exchange(sent, sum_orders, stage), marks)
         marks = [swap_core(mark)]
     got = exchange(sent, sum_orders, 3)
-    new_first, new_second, parts = adam(kept, got, first, second, [*factors, *marks])
-
-    states_other = swap_core(
-        call(
-            pick_kernel,
-            [shape(2 * rows, half, F32)],
-            [(1 - core)[None], new_first, new_second],
-            smem=1,
-        )[0]
-    )
+    new_first, new_second, states_sent, parts = adam(
+        core, kept, got, first, second, [*factors, *marks]
+    )
+
+    got = exchange(parts, back_orders, 0)
+    states_other = swap_core(states_sent)
     out_first, out_second, joined = call(
         with_mark(join_kernel),
         [shape(rows, width, F32)] * 2 + [shape(8, 128, F32)],
@@ -393,7 +388,8 @@
     )
     marks = [states_other]
     for stage in range(4):
-        got = exchange(parts, back_orders, stage)
+        if stage > 0:
+            got = exchange(parts, back_orders, stage)
         if stage == 1:
             marks = [*marks, joined]
         if stage < 3:

time: 165 us -> 165 us (level)
    pallas_call x21 -> x20, Pallas kernels: 9.43 us -> 9.58 us  [call(): pl.pallas_call(body, out_shape=list(outs), in_specs=specs, out_specs=[pl....]
where the time goes in v2:
time: 165 us
  starting transfers between devices  74.8 us (45%)
  waiting for transfers between devices  68.2 us (41%)
  Pallas kernels  9.58 us (6%)
  local copies, waits for them, and re-layouts  5.04 us (3%)
  matrix products  4.3 us (3%)
  other arithmetic  2.02 us (1%)
    ppermute x39, starting transfers between devices, swap(): lax.ppermute(array, ('fsdp', 'tp'), [(i, i ^ scale * masks[i // inner % 2...  74.8 us
    ppermute x39, waiting for transfers between devices, swap(): lax.ppermute(array, ('fsdp', 'tp'), [(i, i ^ scale * masks[i // inner % 2...  68.2 us
    pallas_call x20, Pallas kernels, call(): pl.pallas_call(body, out_shape=list(outs), in_specs=specs, out_specs=[pl....  9.58 us
  transfers between devices with their start and end apart: 39, of which 28 were waited for; matrix products, arithmetic and copies ran while one was open for 4% of the time, Pallas kernels for 3%

profile of v2, /device:TPU:1, one launch (start us, length us, event | category | flops | bytes accessed | tf_op | source)
XLA Modules:
  0.0 164.9 jit_solution(2177491523360445555)
XLA Ops:
  1.5 3.8 %collective-permute-start = (bf16[256,128]{1,0:T(8,128)(2,1)S(1)}, bf16[256,128]{1,0:T(8,128)(2,1)S(1)}, u32[]{:S(2)}, u32[]{:S(2)}) collective-permute-start(bf16[256,128]{1,0:T(8,128)(2,1)S(1)} %constant_dynamic-slice_fusion.2.refs_0_), channel_id=1, source_target_pairs={{0,64},{1,65},{2,66},{3,67},{4,68},{5,69},{6,70},{7,71},{8,72},{9,... | collective-permute-start | bytes 196616 | tf_op jit(solution)/shard_map/ppermute | solution.py:21
  5.4 5.1 %collective-permute-start.1 = (bf16[256,128]{1,0:T(8,128)(2,1)S(1)}, bf16[256,128]{1,0:T(8,128)(2,1)S(1)}, u32[]{:S(2)}, u32[]{:S(2)}) collective-permute-start(bf16[256,128]{1,0:T(8,128)(2,1)S(1)} %constant_dynamic-slice_fusion.2.refs_0_), channel_id=1, source_target_pairs={{0,128},{1,129},{2,130},{3,131},{4,132},{5,133},{6,134},{7,135},{8... | collective-permute-start | bytes 196616 | tf_op jit(solution)/shard_map/ppermute | solution.py:21
  10.5 1.6 constant_dynamic-slice_fusion
  12.1 1.3 collective-permute-start.6
  13.7 2.3 %collective-permute-done.2.refs_3_ = bf16[256,128]{1,0:T(8,128)(2,1)S(1)} collective-permute-done((bf16[256,128]{1,0:T(8,128)(2,1)S(1)}, bf16[256,128]{1,0:T(8,128)(2,1)S(1)}, u32[]{:S(2)}, u32[]{:S(2)}) %collective-permute-start.2) | collective-permute-done | bytes 65568 | tf_op jit(solution)/shard_map/ppermute | solution.py:21
  16.0 1.3 collective-permute-start.3
  17.3 2.5 %collective-permute-start.4 = (bf16[1024,128]{1,0:T(8,128)(2,1)S(1)}, bf16[1024,128]{1,0:T(8,128)(2,1)S(1)}, u32[]{:S(2)}, u32[]{:S(2)}) collective-permute-start(bf16[1024,128]{1,0:T(8,128)(2,1)S(1)} %shard_map.157.refs_0_), channel_id=1, source_target_pairs={{0,32},{1,33},{2,34},{3,35},{4,36},{5,37},{6,38},{7,39},{8,40},{9,... | collective-permute-start | bytes 786440 | tf_op jit(solution)/shard_map/ppermute | solution.py:21
  20.0 2.2 %copy-done = bf16[256,8192]{1,0:T(8,128)(2,1)S(1)} copy-done((bf16[256,8192]{1,0:T(8,128)(2,1)S(1)}, bf16[256,8192]{1,0:T(8,128)(2,1)}, u32[]{:S(2)}) %copy-start) | copy-done | bytes 4194328
  23.4 6.2 %collective-permute-done.4.refs_2_ = bf16[1024,128]{1,0:T(8,128)(2,1)S(1)} collective-permute-done((bf16[1024,128]{1,0:T(8,128)(2,1)S(1)}, bf16[1024,128]{1,0:T(8,128)(2,1)S(1)}, u32[]{:S(2)}, u32[]{:S(2)}) %collective-permute-start.4) | collective-permute-done | bytes 262176 | tf_op jit(solution)/shard_map/ppermute | solution.py:21
  29.6 3.5 %collective-permute-done.5.refs_3_ = bf16[1024,128]{1,0:T(8,128)(2,1)S(1)} collective-permute-done((bf16[1024,128]{1,0:T(8,128)(2,1)S(1)}, bf16[1024,128]{1,0:T(8,128)(2,1)S(1)}, u32[]{:S(2)}, u32[]{:S(2)}) %collective-permute-start.5) | collective-permute-done | bytes 262176 | tf_op jit(solution)/shard_map/ppermute | solution.py:21
  33.2 2.3 %collective-permute-start.7 = (bf16[4096,128]{1,0:T(8,128)(2,1)S(1)}, bf16[4096,128]{1,0:T(8,128)(2,1)S(1)}, u32[]{:S(2)}, u32[]{:S(2)}) collective-permute-start(bf16[4096,128]{1,0:T(8,128)(2,1)S(1)} %shard_map.159), channel_id=1, source_target_pairs={{0,8},{1,9},{2,10},{3,11},{4,12},{5,13},{6,14},{7,15},{8,0},{9,1},... | collective-permute-start | bytes 3145736 | tf_op jit(solution)/shard_map/ppermute | solution.py:21
  36.1 1.6 collective-permute-done.7
  40.3 2.3 %collective-permute-done.8.refs_1_ = bf16[128,256]{1,0:T(8,128)(2,1)S(1)} collective-permute-done((bf16[128,256]{1,0:T(8,128)(2,1)S(1)}, bf16[128,256]{1,0:T(8,128)(2,1)S(1)}, u32[]{:S(2)}, u32[]{:S(2)}) %collective-permute-start.8) | collective-permute-done | bytes 65568 | tf_op jit(solution)/shard_map/ppermute | solution.py:21
  42.6 3.0 %collective-permute-start.10 = (bf16[256,256]{1,0:T(8,128)(2,1)S(1)}, bf16[256,256]{1,0:T(8,128)(2,1)S(1)}, u32[]{:S(2)}, u32[]{:S(2)}) collective-permute-start(bf16[256,256]{1,0:T(8,128)(2,1)S(1)} %shard_map.160.refs_0_), channel_id=1, source_target_pairs={{0,4},{1,5},{2,6},{3,7},{4,0},{5,1},{6,2},{7,3},{8,12},{9,13},{10,... | collective-permute-start | bytes 393224 | tf_op jit(solution)/shard_map/ppermute | solution.py:21
  46.5 1.6 collective-permute-done.10.refs_2_
  48.1 3.4 %collective-permute-done.11.refs_3_ = bf16[256,256]{1,0:T(8,128)(2,1)S(1)} collective-permute-done((bf16[256,256]{1,0:T(8,128)(2,1)S(1)}, bf16[256,256]{1,0:T(8,128)(2,1)S(1)}, u32[]{:S(2)}, u32[]{:S(2)}) %collective-permute-start.11) | collective-permute-done | bytes 131104 | tf_op jit(solution)/shard_map/ppermute | solution.py:21
  51.5 2.3 %collective-permute-start.14 = (bf16[1024,256]{1,0:T(8,128)(2,1)S(1)}, bf16[1024,256]{1,0:T(8,128)(2,1)S(1)}, u32[]{:S(2)}, u32[]{:S(2)}) collective-permute-start(bf16[1024,256]{1,0:T(8,128)(2,1)S(1)} %shard_map.162.refs_1_), channel_id=1, source_target_pairs={{0,8},{1,9},{2,10},{3,11},{4,12},{5,13},{6,14},{7,15},{8,0},{9,1},... | collective-permute-start | bytes 1572872 | tf_op jit(solution)/shard_map/ppermute | solution.py:21
  54.1 1.3 collective-permute-done.14.refs_2_
  55.4 1.7 %shard_map.164 = (bf16[512,1280]{1,0:T(8,128)(2,1)S(1)}, bf16[512,512]{1,0:T(8,128)(2,1)S(1)}) custom-call(s32[16]{0:T(128)S(1)} %get-tuple-element.98.refs_0_, bf16[1024,256]{1,0:T(8,128)(2,1)S(1)} %shard_map.162.refs_1_, bf16[1024,256]{1,0:T(8,128)(2,1)S(1)} %collective-permute-done.14.refs_2_, bf16[512,1792]{1,0:T(8,128)(2,1)S(1)} %pad_maximum_fusion.refs_3_), custom_call_target="tpu_custom_call" | custom-call | flops 939524096 | bytes 4718656 | tf_op jit(solution)/shard_map/pallas_call | solution.py:63
  57.5 4.3 %collective-permute-start.16 = (bf16[512,512]{1,0:T(8,128)(2,1)S(1)}, bf16[512,512]{1,0:T(8,128)(2,1)S(1)}, u32[]{:S(2)}, u32[]{:S(2)}) collective-permute-start(bf16[512,512]{1,0:T(8,128)(2,1)S(1)} %get-tuple-element.47), channel_id=1, source_target_pairs={{0,64},{1,65},{2,66},{3,67},{4,68},{5,69},{6,70},{7,71},{8,200},{9... | collective-permute-start | bytes 1572872 | tf_op jit(solution)/shard_map/ppermute | solution.py:21
  61.9 1.7 %shard_map.163 = (f32[512,1280]{1,0:T(8,128)S(1)}, f32[512,512]{1,0:T(8,128)S(1)}) custom-call(s32[16]{0:T(128)S(1)} %get-tuple-element.97.refs_0_, bf16[1024,256]{1,0:T(8,128)(2,1)S(1)} %shard_map.162.refs_1_, bf16[1024,256]{1,0:T(8,128)(2,1)S(1)} %collective-permute-done.14.refs_2_, bf16[512,1792]{1,0:T(8,128)(2,1)S(1)} %pad_maximum_fusion.refs_3_), custom_call_target="tpu_custom_call" | custom-call | flops 939524096 | bytes 6553664 | tf_op jit(solution)/shard_map/pallas_call | solution.py:63
  63.6 9.9 %collective-permute-done.16.refs_3_ = bf16[512,512]{1,0:T(8,128)(2,1)S(1)} collective-permute-done((bf16[512,512]{1,0:T(8,128)(2,1)S(1)}, bf16[512,512]{1,0:T(8,128)(2,1)S(1)}, u32[]{:S(2)}, u32[]{:S(2)}) %collective-permute-start.16) | collective-permute-done | bytes 524320 | tf_op jit(solution)/shard_map/ppermute | solution.py:21
  73.4 1.6 collective-permute-done.15.refs_2_
  76.5 4.4 %collective-permute-start.19 = (f32[8,128]{1,0:T(8,128)S(1)}, f32[8,128]{1,0:T(8,128)S(1)}, u32[]{:S(2)}, u32[]{:S(2)}) collective-permute-start(f32[8,128]{1,0:T(8,128)S(1)} %get-tuple-element.52), channel_id=1, source_target_pairs={{0,8},{1,9},{2,10},{3,11},{4,12},{5,13},{6,14},{7,15},{8,0},{9,1},... | collective-permute-start | bytes 12296 | tf_op jit(solution)/shard_map/ppermute | solution.py:21
  81.7 3.1 %collective-permute-done.18.refs_3_ = bf16[256,512]{1,0:T(8,128)(2,1)S(1)} collective-permute-done((bf16[256,512]{1,0:T(8,128)(2,1)S(1)}, bf16[256,512]{1,0:T(8,128)(2,1)S(1)}, u32[]{:S(2)}, u32[]{:S(2)}) %collective-permute-start.18) | collective-permute-done | bytes 262176 | tf_op jit(solution)/shard_map/ppermute | solution.py:21
  85.4 4.4 %collective-permute-start.20 = (bf16[128,1280]{1,0:T(8,128)(2,1)S(1)}, bf16[128,1280]{1,0:T(8,128)(2,1)S(1)}, u32[]{:S(2)}, u32[]{:S(2)}) collective-permute-start(bf16[128,1280]{1,0:T(8,128)(2,1)S(1)} %get-tuple-element.55), channel_id=1, source_target_pairs={{0,64},{1,65},{2,66},{3,67},{4,68},{5,69},{6,70},{7,71},{8,200},{9... | collective-permute-start | bytes 983048 | tf_op jit(solution)/shard_map/ppermute | solution.py:21
  90.5 1.3 fusion.8.refs_8_.refs_1_
  91.9 3.2 %collective-permute-done.21.refs_3_ = bf16[128,512]{1,0:T(8,128)(2,1)S(1)} collective-permute-done((bf16[128,512]{1,0:T(8,128)(2,1)S(1)}, bf16[128,512]{1,0:T(8,128)(2,1)S(1)}, u32[]{:S(2)}, u32[]{:S(2)}) %collective-permute-start.21) | collective-permute-done | bytes 131104 | tf_op jit(solution)/shard_map/ppermute | solution.py:21
  95.1 2.0 %collective-permute-done.20.refs_2_ = bf16[128,1280]{1,0:T(8,128)(2,1)S(1)} collective-permute-done((bf16[128,1280]{1,0:T(8,128)(2,1)S(1)}, bf16[128,1280]{1,0:T(8,128)(2,1)S(1)}, u32[]{:S(2)}, u32[]{:S(2)}) %collective-permute-start.20) | collective-permute-done | bytes 327712 | tf_op jit(solution)/shard_map/ppermute | solution.py:21
  97.2 1.9 %collective-permute-start.23 = (bf16[64,1280]{1,0:T(8,128)(2,1)S(1)}, bf16[64,1280]{1,0:T(8,128)(2,1)S(1)}, u32[]{:S(2)}, u32[]{:S(2)}) collective-permute-start(bf16[64,1280]{1,0:T(8,128)(2,1)S(1)} %get-tuple-element.60), channel_id=1, source_target_pairs={{0,192},{1,193},{2,194},{3,195},{4,196},{5,197},{6,198},{7,199},{8... | collective-permute-start | bytes 491528 | tf_op jit(solution)/shard_map/ppermute | solution.py:21
  99.1 7.8 %collective-permute-start.25 = (f32[8,128]{1,0:T(8,128)S(1)}, f32[8,128]{1,0:T(8,128)S(1)}, u32[]{:S(2)}, u32[]{:S(2)}) collective-permute-start(f32[8,128]{1,0:T(8,128)S(1)} %get-tuple-element.65), channel_id=1, source_target_pairs={{0,8},{1,9},{2,10},{3,11},{4,12},{5,13},{6,14},{7,15},{8,0},{9,1},... | collective-permute-start | bytes 12296 | tf_op jit(solution)/shard_map/ppermute | solution.py:21
  106.9 1.3 fusion.9.refs_7_.refs_0_
  108.9 1.4 collective-permute-start.26
  110.6 3.1 %collective-permute-done.28.refs_3_ = bf16[64,512]{1,0:T(8,128)(2,1)S(1)} collective-permute-done((bf16[64,512]{1,0:T(8,128)(2,1)S(1)}, bf16[64,512]{1,0:T(8,128)(2,1)S(1)}, u32[]{:S(2)}, u32[]{:S(2)}) %collective-permute-start.28) | collective-permute-done | bytes 65568 | tf_op jit(solution)/shard_map/ppermute | solution.py:21
  113.7 2.9 %collective-permute-done.27.refs_1_ = bf16[64,1280]{1,0:T(8,128)(2,1)S(1)} collective-permute-done((bf16[64,1280]{1,0:T(8,128)(2,1)S(1)}, bf16[64,1280]{1,0:T(8,128)(2,1)S(1)}, u32[]{:S(2)}, u32[]{:S(2)}) %collective-permute-start.27) | collective-permute-done | bytes 163872 | tf_op jit(solution)/shard_map/ppermute | solution.py:21
  116.7 1.7 %collective-permute-start.29 = (bf16[128,1280]{1,0:T(8,128)(2,1)S(1)}, bf16[128,1280]{1,0:T(8,128)(2,1)S(1)}, u32[]{:S(2)}, u32[]{:S(2)}) collective-permute-start(bf16[128,1280]{1,0:T(8,128)(2,1)S(1)} %get-tuple-element.73.refs_0_), channel_id=1, source_target_pairs={{0,64},{1,65},{2,66},{3,67},{4,68},{5,69},{6,70},{7,71},{8,200},{9... | collective-permute-start | bytes 983048 | tf_op jit(solution)/shard_map/ppermute | solution.py:21
  118.4 1.9 %collective-permute-start.30 = (bf16[128,512]{1,0:T(8,128)(2,1)S(1)}, bf16[128,512]{1,0:T(8,128)(2,1)S(1)}, u32[]{:S(2)}, u32[]{:S(2)}) collective-permute-start(bf16[128,512]{1,0:T(8,128)(2,1)S(1)} %get-tuple-element.74.refs_2_), channel_id=1, source_target_pairs={{0,16},{1,17},{2,18},{3,19},{4,20},{5,21},{6,22},{7,23},{8,56},{9,... | collective-permute-start | bytes 393224 | tf_op jit(solution)/shard_map/ppermute | solution.py:21
  121.5 2.1 %collective-permute-done.30.refs_3_ = bf16[128,512]{1,0:T(8,128)(2,1)S(1)} collective-permute-done((bf16[128,512]{1,0:T(8,128)(2,1)S(1)}, bf16[128,512]{1,0:T(8,128)(2,1)S(1)}, u32[]{:S(2)}, u32[]{:S(2)}) %collective-permute-start.30) | collective-permute-done | bytes 131104 | tf_op jit(solution)/shard_map/ppermute | solution.py:21
  123.6 2.5 %collective-permute-done.29.refs_1_ = bf16[128,1280]{1,0:T(8,128)(2,1)S(1)} collective-permute-done((bf16[128,1280]{1,0:T(8,128)(2,1)S(1)}, bf16[128,1280]{1,0:T(8,128)(2,1)S(1)}, u32[]{:S(2)}, u32[]{:S(2)}) %collective-permute-start.29) | collective-permute-done | bytes 327712 | tf_op jit(solution)/shard_map/ppermute | solution.py:21
  126.2 1.9 %collective-permute-start.33 = (bf16[256,512]{1,0:T(8,128)(2,1)S(1)}, bf16[256,512]{1,0:T(8,128)(2,1)S(1)}, u32[]{:S(2)}, u32[]{:S(2)}) collective-permute-start(bf16[256,512]{1,0:T(8,128)(2,1)S(1)} %get-tuple-element.78.refs_2_), channel_id=1, source_target_pairs={{0,192},{1,193},{2,194},{3,195},{4,196},{5,197},{6,198},{7,199},{8... | collective-permute-start | bytes 786440 | tf_op jit(solution)/shard_map/ppermute | solution.py:21
  128.1 5.9 %collective-permute-start.34 = (f32[8,128]{1,0:T(8,128)S(1)}, f32[8,128]{1,0:T(8,128)S(1)}, u32[]{:S(2)}, u32[]{:S(2)}) collective-permute-start(f32[8,128]{1,0:T(8,128)S(1)} %get-tuple-element.79), channel_id=1, source_target_pairs={{0,8},{1,9},{2,10},{3,11},{4,12},{5,13},{6,14},{7,15},{8,0},{9,1},... | collective-permute-start | bytes 12296 | tf_op jit(solution)/shard_map/ppermute | solution.py:21
  136.1 4.8 %collective-permute-start.35 = (bf16[512,1280]{1,0:T(8,128)(2,1)S(1)}, bf16[512,1280]{1,0:T(8,128)(2,1)S(1)}, u32[]{:S(2)}, u32[]{:S(2)}) collective-permute-start(bf16[512,1280]{1,0:T(8,128)(2,1)S(1)} %get-tuple-element.80.refs_2_), channel_id=1, source_target_pairs={{0,16},{1,17},{2,18},{3,19},{4,20},{5,21},{6,22},{7,23},{8,56},{9,... | collective-permute-start | bytes 3932168 | tf_op jit(solution)/shard_map/ppermute | solution.py:21
  141.8 2.2 %collective-permute-start.37 = (f32[8,128]{1,0:T(8,128)S(1)}, f32[8,128]{1,0:T(8,128)S(1)}, u32[]{:S(2)}, u32[]{:S(2)}) collective-permute-start(f32[8,128]{1,0:T(8,128)S(1)} %get-tuple-element.82), channel_id=1, source_target_pairs={{0,8},{1,9},{2,10},{3,11},{4,12},{5,13},{6,14},{7,15},{8,0},{9,1},... | collective-permute-start | bytes 12296 | tf_op jit(solution)/shard_map/ppermute | solution.py:21
  146.0 6.9 %collective-permute-done.36.refs_3_ = bf16[512,512]{1,0:T(8,128)(2,1)S(1)} collective-permute-done((bf16[512,512]{1,0:T(8,128)(2,1)S(1)}, bf16[512,512]{1,0:T(8,128)(2,1)S(1)}, u32[]{:S(2)}, u32[]{:S(2)}) %collective-permute-start.36) | collective-permute-done | bytes 524320 | tf_op jit(solution)/shard_map/ppermute | solution.py:21
  152.9 3.2 %collective-permute-done.35.refs_2_ = bf16[512,1280]{1,0:T(8,128)(2,1)S(1)} collective-permute-done((bf16[512,1280]{1,0:T(8,128)(2,1)S(1)}, bf16[512,1280]{1,0:T(8,128)(2,1)S(1)}, u32[]{:S(2)}, u32[]{:S(2)}) %collective-permute-start.35) | collective-permute-done | bytes 1310752 | tf_op jit(solution)/shard_map/ppermute | solution.py:21
  156.8 4.4 %collective-permute-start.38 = (bf16[256,1792]{1,0:T(8,128)(2,1)S(1)}, bf16[256,1792]{1,0:T(8,128)(2,1)S(1)}, u32[]{:S(2)}, u32[]{:S(2)}) collective-permute-start(bf16[256,1792]{1,0:T(8,128)(2,1)S(1)} %shard_map.176), channel_id=1, source_target_pairs={{0,8},{1,9},{2,10},{3,11},{4,12},{5,13},{6,14},{7,15},{8,0},{9,1},... | collective-permute-start | bytes 2752520 | tf_op jit(solution)/shard_map/ppermute | solution.py:21
  161.8 1.4 collective-permute-done.38
  163.3 1.6 maximum_select_fusion
  (90 shorter events, 19.8 us)
Async XLA Ops:
  0.6 12.8 %copy-start.7 = (s32[16]{0:T(128)S(1)}, s32[16]{0:T(128)}, u32[]{:S(2)}) copy-start(s32[16]{0:T(128)} %constant.36.clone) | copy-start | bytes 196
  0.6 12.8 %copy-start.8 = (s32[16]{0:T(128)S(1)}, s32[16]{0:T(128)}, u32[]{:S(2)}) copy-start(s32[16]{0:T(128)} %constant.37.clone) | copy-start | bytes 196
  0.7 12.8 %copy-start.5 = (s32[16]{0:T(128)S(1)}, s32[16]{0:T(128)}, u32[]{:S(2)}) copy-start(s32[16]{0:T(128)} %constant.38.clone) | copy-start | bytes 196
  0.7 12.8 %copy-start.6 = (s32[16]{0:T(128)S(1)}, s32[16]{0:T(128)}, u32[]{:S(2)}) copy-start(s32[16]{0:T(128)} %constant.39.clone) | copy-start | bytes 196
  1.5 12.1 %collective-permute-start = (bf16[256,128]{1,0:T(8,128)(2,1)S(1)}, bf16[256,128]{1,0:T(8,128)(2,1)S(1)}, u32[]{:S(2)}, u32[]{:S(2)}) collective-permute-start(bf16[256,128]{1,0:T(8,128)(2,1)S(1)} %constant_dynamic-slice_fusion.2.refs_0_), channel_id=1, source_target_pairs={{0,64},{1,65},{2,66},{3,67},{4,68},{5,69},{6,70},{7,71},{8,72},{9,... | collective-permute-start | bytes 196616 | tf_op jit(solution)/shard_map/ppermute | solution.py:21
  5.4 8.3 %collective-permute-start.1 = (bf16[256,128]{1,0:T(8,128)(2,1)S(1)}, bf16[256,128]{1,0:T(8,128)(2,1)S(1)}, u32[]{:S(2)}, u32[]{:S(2)}) collective-permute-start(bf16[256,128]{1,0:T(8,128)(2,1)S(1)} %constant_dynamic-slice_fusion.2.refs_0_), channel_id=1, source_target_pairs={{0,128},{1,129},{2,130},{3,131},{4,132},{5,133},{6,134},{7,135},{8... | collective-permute-start | bytes 196616 | tf_op jit(solution)/shard_map/ppermute | solution.py:21
  10.5 5.5 %collective-permute-start.2 = (bf16[256,128]{1,0:T(8,128)(2,1)S(1)}, bf16[256,128]{1,0:T(8,128)(2,1)S(1)}, u32[]{:S(2)}, u32[]{:S(2)}) collective-permute-start(bf16[256,128]{1,0:T(8,128)(2,1)S(1)} %constant_dynamic-slice_fusion.2.refs_0_), channel_id=1, source_target_pairs={{0,192},{1,193},{2,194},{3,195},{4,196},{5,197},{6,198},{7,199},{8... | collective-permute-start | bytes 196616 | tf_op jit(solution)/shard_map/ppermute | solution.py:21
  10.5 9.5 %copy-start.4 = (s32[16]{0:T(128)S(1)}, s32[16]{0:T(128)}, u32[]{:S(2)}) copy-start(s32[16]{0:T(128)} %constant.40.clone) | copy-start | bytes 196
  12.1 21.0 %collective-permute-start.6 = (bf16[256,1792]{1,0:T(8,128)(2,1)S(1)}, bf16[256,1792]{1,0:T(8,128)(2,1)S(1)}, u32[]{:S(2)}, u32[]{:S(2)}) collective-permute-start(bf16[256,1792]{1,0:T(8,128)(2,1)S(1)} %get-tuple-element.84), channel_id=1, source_target_pairs={{0,8},{1,9},{2,10},{3,11},{4,12},{5,13},{6,14},{7,15},{8,0},{9,1},... | collective-permute-start | bytes 2752520 | tf_op jit(solution)/shard_map/ppermute | solution.py:21
  16.0 7.4 %collective-permute-start.3 = (bf16[1024,128]{1,0:T(8,128)(2,1)S(1)}, bf16[1024,128]{1,0:T(8,128)(2,1)S(1)}, u32[]{:S(2)}, u32[]{:S(2)}) collective-permute-start(bf16[1024,128]{1,0:T(8,128)(2,1)S(1)} %shard_map.157.refs_0_), channel_id=1, source_target_pairs={{0,16},{1,17},{2,18},{3,19},{4,20},{5,21},{6,22},{7,23},{8,24},{9,... | collective-permute-start | bytes 786440 | tf_op jit(solution)/shard_map/ppermute | solution.py:21
  17.3 12.3 %collective-permute-start.4 = (bf16[1024,128]{1,0:T(8,128)(2,1)S(1)}, bf16[1024,128]{1,0:T(8,128)(2,1)S(1)}, u32[]{:S(2)}, u32[]{:S(2)}) collective-permute-start(bf16[1024,128]{1,0:T(8,128)(2,1)S(1)} %shard_map.157.refs_0_), channel_id=1, source_target_pairs={{0,32},{1,33},{2,34},{3,35},{4,36},{5,37},{6,38},{7,39},{8,40},{9,... | collective-permute-start | bytes 786440 | tf_op jit(solution)/shard_map/ppermute | solution.py:21
  19.7 13.4 %collective-permute-start.5 = (bf16[1024,128]{1,0:T(8,128)(2,1)S(1)}, bf16[1024,128]{1,0:T(8,128)(2,1)S(1)}, u32[]{:S(2)}, u32[]{:S(2)}) collective-permute-start(bf16[1024,128]{1,0:T(8,128)(2,1)S(1)} %shard_map.157.refs_0_), channel_id=1, source_target_pairs={{0,48},{1,49},{2,50},{3,51},{4,52},{5,53},{6,54},{7,55},{8,56},{9,... | collective-permute-start | bytes 786440 | tf_op jit(solution)/shard_map/ppermute | solution.py:21
  20.0 2.2 %copy-start = (bf16[256,8192]{1,0:T(8,128)(2,1)S(1)}, bf16[256,8192]{1,0:T(8,128)(2,1)}, u32[]{:S(2)}) copy-start(bf16[256,8192]{1,0:T(8,128)(2,1)} %refs_1_.2) | copy-start | bytes 12582916
  23.3 12.1 %copy-start.3 = (bf16[256,1024]{1,0:T(8,128)(2,1)S(1)}, bf16[256,1024]{1,0:T(8,128)(2,1)}, u32[]{:S(2)}) copy-start(bf16[256,1024]{1,0:T(8,128)(2,1)} %param.16) | copy-start | bytes 1572868
  23.4 12.2 %copy-start.1 = (f32[32,3584]{1,0:T(8,128)S(1)}, f32[32,3584]{1,0:T(8,128)}, u32[]{:S(2)}) copy-start(f32[32,3584]{1,0:T(8,128)} %refs_1_.3) | copy-start | bytes 1376260
  23.4 12.2 %copy-start.2 = (f32[32,3584]{1,0:T(8,128)S(1)}, f32[32,3584]{1,0:T(8,128)}, u32[]{:S(2)}) copy-start(f32[32,3584]{1,0:T(8,128)} %refs_2_.1) | copy-start | bytes 1376260
  33.2 4.6 %collective-permute-start.7 = (bf16[4096,128]{1,0:T(8,128)(2,1)S(1)}, bf16[4096,128]{1,0:T(8,128)(2,1)S(1)}, u32[]{:S(2)}, u32[]{:S(2)}) collective-permute-start(bf16[4096,128]{1,0:T(8,128)(2,1)S(1)} %shard_map.159), channel_id=1, source_target_pairs={{0,8},{1,9},{2,10},{3,11},{4,12},{5,13},{6,14},{7,15},{8,0},{9,1},... | collective-permute-start | bytes 3145736 | tf_op jit(solution)/shard_map/ppermute | solution.py:21
  35.4 11.1 %collective-permute-start.13 = (bf16[256,1024]{1,0:T(8,128)(2,1)S(1)}, bf16[256,1024]{1,0:T(8,128)(2,1)S(1)}, u32[]{:S(2)}, u32[]{:S(2)}) collective-permute-start(bf16[256,1024]{1,0:T(8,128)(2,1)S(1)} %copy-done.3), channel_id=1, source_target_pairs={{0,8},{1,9},{2,10},{3,11},{4,12},{5,13},{6,14},{7,15},{8,0},{9,1},... | collective-permute-start | bytes 1572872 | tf_op jit(solution)/shard_map/ppermute | solution.py:21
  35.6 10.9 %collective-permute-start.12 = (f32[64,1792]{1,0:T(8,128)S(1)}, f32[64,1792]{1,0:T(8,128)S(1)}, u32[]{:S(2)}, u32[]{:S(2)}) collective-permute-start(f32[64,1792]{1,0:T(8,128)S(1)} %get-tuple-element.43), channel_id=1, source_target_pairs={{0,8},{1,9},{2,10},{3,11},{4,12},{5,13},{6,14},{7,15},{8,0},{9,1},... | collective-permute-start | bytes 1376264 | tf_op jit(solution)/shard_map/ppermute | solution.py:21
  39.4 3.2 %collective-permute-start.8 = (bf16[128,256]{1,0:T(8,128)(2,1)S(1)}, bf16[128,256]{1,0:T(8,128)(2,1)S(1)}, u32[]{:S(2)}, u32[]{:S(2)}) collective-permute-start(bf16[128,256]{1,0:T(8,128)(2,1)S(1)} %fusion.13.refs_0_), channel_id=1, source_target_pairs={{0,1},{1,0},{2,3},{3,2},{4,5},{5,4},{6,7},{7,6},{8,9},{9,8},{10,11... | collective-permute-start | bytes 196616 | tf_op jit(solution)/shard_map/ppermute | solution.py:21
  42.6 5.4 %collective-permute-start.10 = (bf16[256,256]{1,0:T(8,128)(2,1)S(1)}, bf16[256,256]{1,0:T(8,128)(2,1)S(1)}, u32[]{:S(2)}, u32[]{:S(2)}) collective-permute-start(bf16[256,256]{1,0:T(8,128)(2,1)S(1)} %shard_map.160.refs_0_), channel_id=1, source_target_pairs={{0,4},{1,5},{2,6},{3,7},{4,0},{5,1},{6,2},{7,3},{8,12},{9,13},{10,... | collective-permute-start | bytes 393224 | tf_op jit(solution)/shard_map/ppermute | solution.py:21
  45.6 5.8 %collective-permute-start.11 = (bf16[256,256]{1,0:T(8,128)(2,1)S(1)}, bf16[256,256]{1,0:T(8,128)(2,1)S(1)}, u32[]{:S(2)}, u32[]{:S(2)}) collective-permute-start(bf16[256,256]{1,0:T(8,128)(2,1)S(1)} %shard_map.160.refs_0_), channel_id=1, source_target_pairs={{0,6},{1,7},{2,4},{3,5},{4,2},{5,3},{6,0},{7,1},{8,14},{9,15},{10,... | collective-permute-start | bytes 393224 | tf_op jit(solution)/shard_map/ppermute | solution.py:21
  46.4 5.1 %collective-permute-start.9 = (bf16[256,256]{1,0:T(8,128)(2,1)S(1)}, bf16[256,256]{1,0:T(8,128)(2,1)S(1)}, u32[]{:S(2)}, u32[]{:S(2)}) collective-permute-start(bf16[256,256]{1,0:T(8,128)(2,1)S(1)} %shard_map.160.refs_0_), channel_id=1, source_target_pairs={{0,2},{1,3},{2,0},{3,1},{4,6},{5,7},{6,4},{7,5},{8,10},{9,11},{10,... | collective-permute-start | bytes 393224 | tf_op jit(solution)/shard_map/ppermute | solution.py:21
  51.5 3.9 %collective-permute-start.14 = (bf16[1024,256]{1,0:T(8,128)(2,1)S(1)}, bf16[1024,256]{1,0:T(8,128)(2,1)S(1)}, u32[]{:S(2)}, u32[]{:S(2)}) collective-permute-start(bf16[1024,256]{1,0:T(8,128)(2,1)S(1)} %shard_map.162.refs_1_), channel_id=1, source_target_pairs={{0,8},{1,9},{2,10},{3,11},{4,12},{5,13},{6,14},{7,15},{8,0},{9,1},... | collective-permute-start | bytes 1572872 | tf_op jit(solution)/shard_map/ppermute | solution.py:21
  57.1 17.9 %collective-permute-start.15 = (bf16[512,1280]{1,0:T(8,128)(2,1)S(1)}, bf16[512,1280]{1,0:T(8,128)(2,1)S(1)}, u32[]{:S(2)}, u32[]{:S(2)}) collective-permute-start(bf16[512,1280]{1,0:T(8,128)(2,1)S(1)} %get-tuple-element.46), channel_id=1, source_target_pairs={{0,16},{1,17},{2,18},{3,19},{4,20},{5,21},{6,22},{7,23},{8,56},{9,... | collective-permute-start | bytes 3932168 | tf_op jit(solution)/shard_map/ppermute | solution.py:21
  57.5 15.9 %collective-permute-start.16 = (bf16[512,512]{1,0:T(8,128)(2,1)S(1)}, bf16[512,512]{1,0:T(8,128)(2,1)S(1)}, u32[]{:S(2)}, u32[]{:S(2)}) collective-permute-start(bf16[512,512]{1,0:T(8,128)(2,1)S(1)} %get-tuple-element.47), channel_id=1, source_target_pairs={{0,64},{1,65},{2,66},{3,67},{4,68},{5,69},{6,70},{7,71},{8,200},{9... | collective-permute-start | bytes 1572872 | tf_op jit(solution)/shard_map/ppermute | solution.py:21
  75.4 9.8 %collective-permute-start.17 = (bf16[256,1280]{1,0:T(8,128)(2,1)S(1)}, bf16[256,1280]{1,0:T(8,128)(2,1)S(1)}, u32[]{:S(2)}, u32[]{:S(2)}) collective-permute-start(bf16[256,1280]{1,0:T(8,128)(2,1)S(1)} %get-tuple-element.50), channel_id=1, source_target_pairs={{0,48},{1,49},{2,50},{3,51},{4,52},{5,53},{6,54},{7,55},{8,24},{9,... | collective-permute-start | bytes 1966088 | tf_op jit(solution)/shard_map/ppermute | solution.py:21
  75.5 9.4 %collective-permute-start.18 = (bf16[256,512]{1,0:T(8,128)(2,1)S(1)}, bf16[256,512]{1,0:T(8,128)(2,1)S(1)}, u32[]{:S(2)}, u32[]{:S(2)}) collective-permute-start(bf16[256,512]{1,0:T(8,128)(2,1)S(1)} %get-tuple-element.51), channel_id=1, source_target_pairs={{0,192},{1,193},{2,194},{3,195},{4,196},{5,197},{6,198},{7,199},{8... | collective-permute-start | bytes 786440 | tf_op jit(solution)/shard_map/ppermute | solution.py:21
  76.5 5.2 %collective-permute-start.19 = (f32[8,128]{1,0:T(8,128)S(1)}, f32[8,128]{1,0:T(8,128)S(1)}, u32[]{:S(2)}, u32[]{:S(2)}) collective-permute-start(f32[8,128]{1,0:T(8,128)S(1)} %get-tuple-element.52), channel_id=1, source_target_pairs={{0,8},{1,9},{2,10},{3,11},{4,12},{5,13},{6,14},{7,15},{8,0},{9,1},... | collective-permute-start | bytes 12296 | tf_op jit(solution)/shard_map/ppermute | solution.py:21
  85.4 11.7 %collective-permute-start.20 = (bf16[128,1280]{1,0:T(8,128)(2,1)S(1)}, bf16[128,1280]{1,0:T(8,128)(2,1)S(1)}, u32[]{:S(2)}, u32[]{:S(2)}) collective-permute-start(bf16[128,1280]{1,0:T(8,128)(2,1)S(1)} %get-tuple-element.55), channel_id=1, source_target_pairs={{0,64},{1,65},{2,66},{3,67},{4,68},{5,69},{6,70},{7,71},{8,200},{9... | collective-permute-start | bytes 983048 | tf_op jit(solution)/shard_map/ppermute | solution.py:21
  89.8 5.3 %collective-permute-start.21 = (bf16[128,512]{1,0:T(8,128)(2,1)S(1)}, bf16[128,512]{1,0:T(8,128)(2,1)S(1)}, u32[]{:S(2)}, u32[]{:S(2)}) collective-permute-start(bf16[128,512]{1,0:T(8,128)(2,1)S(1)} %get-tuple-element.56), channel_id=1, source_target_pairs={{0,16},{1,17},{2,18},{3,19},{4,20},{5,21},{6,22},{7,23},{8,56},{9,... | collective-permute-start | bytes 393224 | tf_op jit(solution)/shard_map/ppermute | solution.py:21
  90.5 1.3 collective-permute-start.22
  97.2 11.0 %collective-permute-start.23 = (bf16[64,1280]{1,0:T(8,128)(2,1)S(1)}, bf16[64,1280]{1,0:T(8,128)(2,1)S(1)}, u32[]{:S(2)}, u32[]{:S(2)}) collective-permute-start(bf16[64,1280]{1,0:T(8,128)(2,1)S(1)} %get-tuple-element.60), channel_id=1, source_target_pairs={{0,192},{1,193},{2,194},{3,195},{4,196},{5,197},{6,198},{7,199},{8... | collective-permute-start | bytes 491528 | tf_op jit(solution)/shard_map/ppermute | solution.py:21
  99.1 9.1 %collective-permute-start.24 = (bf16[64,512]{1,0:T(8,128)(2,1)S(1)}, bf16[64,512]{1,0:T(8,128)(2,1)S(1)}, u32[]{:S(2)}, u32[]{:S(2)}) collective-permute-start(bf16[64,512]{1,0:T(8,128)(2,1)S(1)} %get-tuple-element.61), channel_id=1, source_target_pairs={{0,48},{1,49},{2,50},{3,51},{4,52},{5,53},{6,54},{7,55},{8,24},{9,... | collective-permute-start | bytes 196616 | tf_op jit(solution)/shard_map/ppermute | solution.py:21
  99.1 9.1 %collective-permute-start.25 = (f32[8,128]{1,0:T(8,128)S(1)}, f32[8,128]{1,0:T(8,128)S(1)}, u32[]{:S(2)}, u32[]{:S(2)}) collective-permute-start(f32[8,128]{1,0:T(8,128)S(1)} %get-tuple-element.65), channel_id=1, source_target_pairs={{0,8},{1,9},{2,10},{3,11},{4,12},{5,13},{6,14},{7,15},{8,0},{9,1},... | collective-permute-start | bytes 12296 | tf_op jit(solution)/shard_map/ppermute | solution.py:21
  108.9 7.8 %collective-permute-start.26 = (f32[64,1792]{1,0:T(8,128)S(1)}, f32[64,1792]{1,0:T(8,128)S(1)}, u32[]{:S(2)}, u32[]{:S(2)}) collective-permute-start(f32[64,1792]{1,0:T(8,128)S(1)} %get-tuple-element.68), channel_id=1, source_target_pairs={{0,8},{1,9},{2,10},{3,11},{4,12},{5,13},{6,14},{7,15},{8,0},{9,1},... | collective-permute-start | bytes 1376264 | tf_op jit(solution)/shard_map/ppermute | solution.py:21
  110.3 6.4 %collective-permute-start.27 = (bf16[64,1280]{1,0:T(8,128)(2,1)S(1)}, bf16[64,1280]{1,0:T(8,128)(2,1)S(1)}, u32[]{:S(2)}, u32[]{:S(2)}) collective-permute-start(bf16[64,1280]{1,0:T(8,128)(2,1)S(1)} %get-tuple-element.71.refs_0_), channel_id=1, source_target_pairs={{0,192},{1,193},{2,194},{3,195},{4,196},{5,197},{6,198},{7,199},{8... | collective-permute-start | bytes 491528 | tf_op jit(solution)/shard_map/ppermute | solution.py:21
  110.6 3.1 %collective-permute-start.28 = (bf16[64,512]{1,0:T(8,128)(2,1)S(1)}, bf16[64,512]{1,0:T(8,128)(2,1)S(1)}, u32[]{:S(2)}, u32[]{:S(2)}) collective-permute-start(bf16[64,512]{1,0:T(8,128)(2,1)S(1)} %get-tuple-element.72.refs_2_), channel_id=1, source_target_pairs={{0,48},{1,49},{2,50},{3,51},{4,52},{5,53},{6,54},{7,55},{8,24},{9,... | collective-permute-start | bytes 196616 | tf_op jit(solution)/shard_map/ppermute | solution.py:21
  116.7 9.4 %collective-permute-start.29 = (bf16[128,1280]{1,0:T(8,128)(2,1)S(1)}, bf16[128,1280]{1,0:T(8,128)(2,1)S(1)}, u32[]{:S(2)}, u32[]{:S(2)}) collective-permute-start(bf16[128,1280]{1,0:T(8,128)(2,1)S(1)} %get-tuple-element.73.refs_0_), channel_id=1, source_target_pairs={{0,64},{1,65},{2,66},{3,67},{4,68},{5,69},{6,70},{7,71},{8,200},{9... | collective-permute-start | bytes 983048 | tf_op jit(solution)/shard_map/ppermute | solution.py:21
  118.4 5.2 %collective-permute-start.30 = (bf16[128,512]{1,0:T(8,128)(2,1)S(1)}, bf16[128,512]{1,0:T(8,128)(2,1)S(1)}, u32[]{:S(2)}, u32[]{:S(2)}) collective-permute-start(bf16[128,512]{1,0:T(8,128)(2,1)S(1)} %get-tuple-element.74.refs_2_), channel_id=1, source_target_pairs={{0,16},{1,17},{2,18},{3,19},{4,20},{5,21},{6,22},{7,23},{8,56},{9,... | collective-permute-start | bytes 393224 | tf_op jit(solution)/shard_map/ppermute | solution.py:21
  120.3 1.2 collective-permute-start.31
  126.1 9.8 %collective-permute-start.32 = (bf16[256,1280]{1,0:T(8,128)(2,1)S(1)}, bf16[256,1280]{1,0:T(8,128)(2,1)S(1)}, u32[]{:S(2)}, u32[]{:S(2)}) collective-permute-start(bf16[256,1280]{1,0:T(8,128)(2,1)S(1)} %get-tuple-element.77.refs_0_), channel_id=1, source_target_pairs={{0,48},{1,49},{2,50},{3,51},{4,52},{5,53},{6,54},{7,55},{8,24},{9,... | collective-permute-start | bytes 1966088 | tf_op jit(solution)/shard_map/ppermute | solution.py:21
  126.2 9.5 %collective-permute-start.33 = (bf16[256,512]{1,0:T(8,128)(2,1)S(1)}, bf16[256,512]{1,0:T(8,128)(2,1)S(1)}, u32[]{:S(2)}, u32[]{:S(2)}) collective-permute-start(bf16[256,512]{1,0:T(8,128)(2,1)S(1)} %get-tuple-element.78.refs_2_), channel_id=1, source_target_pairs={{0,192},{1,193},{2,194},{3,195},{4,196},{5,197},{6,198},{7,199},{8... | collective-permute-start | bytes 786440 | tf_op jit(solution)/shard_map/ppermute | solution.py:21
  128.1 6.8 %collective-permute-start.34 = (f32[8,128]{1,0:T(8,128)S(1)}, f32[8,128]{1,0:T(8,128)S(1)}, u32[]{:S(2)}, u32[]{:S(2)}) collective-permute-start(f32[8,128]{1,0:T(8,128)S(1)} %get-tuple-element.79), channel_id=1, source_target_pairs={{0,8},{1,9},{2,10},{3,11},{4,12},{5,13},{6,14},{7,15},{8,0},{9,1},... | collective-permute-start | bytes 12296 | tf_op jit(solution)/shard_map/ppermute | solution.py:21
  136.1 20.0 %collective-permute-start.35 = (bf16[512,1280]{1,0:T(8,128)(2,1)S(1)}, bf16[512,1280]{1,0:T(8,128)(2,1)S(1)}, u32[]{:S(2)}, u32[]{:S(2)}) collective-permute-start(bf16[512,1280]{1,0:T(8,128)(2,1)S(1)} %get-tuple-element.80.refs_2_), channel_id=1, source_target_pairs={{0,16},{1,17},{2,18},{3,19},{4,20},{5,21},{6,22},{7,23},{8,56},{9,... | collective-permute-start | bytes 3932168 | tf_op jit(solution)/shard_map/ppermute | solution.py:21
  140.9 12.0 %collective-permute-start.36 = (bf16[512,512]{1,0:T(8,128)(2,1)S(1)}, bf16[512,512]{1,0:T(8,128)(2,1)S(1)}, u32[]{:S(2)}, u32[]{:S(2)}) collective-permute-start(bf16[512,512]{1,0:T(8,128)(2,1)S(1)} %get-tuple-element.81.refs_3_), channel_id=1, source_target_pairs={{0,64},{1,65},{2,66},{3,67},{4,68},{5,69},{6,70},{7,71},{8,200},{9... | collective-permute-start | bytes 1572872 | tf_op jit(solution)/shard_map/ppermute | solution.py:21
  141.8 3.1 %collective-permute-start.37 = (f32[8,128]{1,0:T(8,128)S(1)}, f32[8,128]{1,0:T(8,128)S(1)}, u32[]{:S(2)}, u32[]{:S(2)}) collective-permute-start(f32[8,128]{1,0:T(8,128)S(1)} %get-tuple-element.82), channel_id=1, source_target_pairs={{0,8},{1,9},{2,10},{3,11},{4,12},{5,13},{6,14},{7,15},{8,0},{9,1},... | collective-permute-start | bytes 12296 | tf_op jit(solution)/shard_map/ppermute | solution.py:21
  156.8 6.5 %collective-permute-start.38 = (bf16[256,1792]{1,0:T(8,128)(2,1)S(1)}, bf16[256,1792]{1,0:T(8,128)(2,1)S(1)}, u32[]{:S(2)}, u32[]{:S(2)}) collective-permute-start(bf16[256,1792]{1,0:T(8,128)(2,1)S(1)} %shard_map.176), channel_id=1, source_target_pairs={{0,8},{1,9},{2,10},{3,11},{4,12},{5,13},{6,14},{7,15},{8,0},{9,1},... | collective-permute-start | bytes 2752520 | tf_op jit(solution)/shard_map/ppermute | solution.py:21

commit v3 on v1

--- a/solution.py
+++ b/solution.py
@@ -128,10 +128,9 @@
     )[0]
 
 
-def sums_kernel(count, block, index_ref, own_ref, other_ref, grads_ref, *refs):
+def sums_kernel(count, block, at, index_ref, own_ref, other_ref, grads_ref, *refs):
     outs, chosen = refs[:count], refs[count]
     tokens = own_ref.shape[1]
-    at = 0
     for part, out_ref in enumerate(outs):
         blocks = out_ref.shape[0] // block
         for k in range(blocks):
@@ -146,9 +145,9 @@
         at += width
 
 
-def partial_sums(index, own, other, grads, rows, widths, block, kind, after=()):
+def partial_sums(index, own, other, grads, rows, widths, block, kind, after=(), at=0):
     return call(
-        functools.partial(sums_kernel, len(widths), block),
+        functools.partial(sums_kernel, len(widths), block, at),
         [shape(rows, w, kind) for w in widths],
         [index, own, other, grads],
         flops=2 * rows * grads.size,
@@ -368,7 +367,9 @@
         ]
 
     arrays = (coords, coords_other, grads, rank // 2, widths, block)
-    sent = partial_sums(jnp.concatenate(send_index), *arrays, BF)
+    tail = (rank // 2, widths[1:], block, BF)
+    sent = partial_sums(send_index[0], *arrays[:3], rank // 2, widths[:1], block, BF)
+    sent += partial_sums(send_index[1], *arrays[:3], *tail, after=sent, at=widths[0])
     kept = partial_sums(jnp.concatenate(keep_index), *arrays, F32)
     marks = []
     for stage in range(3):

time: 165 us -> 166 us (level)
  other arithmetic: 2.02 us -> 3.83 us
    pallas_call x21 -> x22, Pallas kernels: 9.43 us -> 10.2 us  [call(): pl.pallas_call(body, out_shape=list(outs), in_specs=specs, out_specs=[pl....]
  transfers between devices with their start and end apart: 39 -> 39, of which waited for: 28 -> 25; matrix products, arithmetic and copies ran while one was open for 4% -> 5% of each run, Pallas kernels for 3% -> 4%
where the time goes in v3:
time: 166 us
  starting transfers between devices  74.2 us (45%)
  waiting for transfers between devices  67.6 us (41%)
  Pallas kernels  10.2 us (6%)
  local copies, waits for them, and re-layouts  4.95 us (3%)
  matrix products  4.32 us (3%)
  other arithmetic  3.83 us (2%)
    ppermute x39, starting transfers between devices, swap(): lax.ppermute(array, ('fsdp', 'tp'), [(i, i ^ scale * masks[i // inner % 2...  74.2 us
    ppermute x39, waiting for transfers between devices, swap(): lax.ppermute(array, ('fsdp', 'tp'), [(i, i ^ scale * masks[i // inner % 2...  67.6 us
    pallas_call x22, Pallas kernels, call(): pl.pallas_call(body, out_shape=list(outs), in_specs=specs, out_specs=[pl....  10.2 us
  transfers between devices with their start and end apart: 39, of which 25 were waited for; matrix products, arithmetic and copies ran while one was open for 5% of the time, Pallas kernels for 4%

profile of v3, /device:TPU:1, one launch (start us, length us, event | category | flops | bytes accessed | tf_op | source)
XLA Modules:
  0.0 166.1 jit_solution(8473711790547726365)
XLA Ops:
  0.7 1.6 constant_dynamic-slice_fusion
  2.3 3.3 %collective-permute-start.6 = (bf16[256,1792]{1,0:T(8,128)(2,1)S(1)}, bf16[256,1792]{1,0:T(8,128)(2,1)S(1)}, u32[]{:S(2)}, u32[]{:S(2)}) collective-permute-start(bf16[256,1792]{1,0:T(8,128)(2,1)S(1)} %get-tuple-element.78), channel_id=1, source_target_pairs={{0,8},{1,9},{2,10},{3,11},{4,12},{5,13},{6,14},{7,15},{8,0},{9,1},... | collective-permute-start | bytes 2752520 | tf_op jit(solution)/shard_map/ppermute | solution.py:21
  5.7 1.3 collective-permute-start
  7.0 5.1 %collective-permute-start.1 = (bf16[256,128]{1,0:T(8,128)(2,1)S(1)}, bf16[256,128]{1,0:T(8,128)(2,1)S(1)}, u32[]{:S(2)}, u32[]{:S(2)}) collective-permute-start(bf16[256,128]{1,0:T(8,128)(2,1)S(1)} %constant_dynamic-slice_fusion.2.refs_0_), channel_id=1, source_target_pairs={{0,128},{1,129},{2,130},{3,131},{4,132},{5,133},{6,134},{7,135},{8... | collective-permute-start | bytes 196616 | tf_op jit(solution)/shard_map/ppermute | solution.py:21
  14.3 1.5 collective-permute-done.1.refs_2_
  15.8 1.9 %collective-permute-done.2.refs_3_ = bf16[256,128]{1,0:T(8,128)(2,1)S(1)} collective-permute-done((bf16[256,128]{1,0:T(8,128)(2,1)S(1)}, bf16[256,128]{1,0:T(8,128)(2,1)S(1)}, u32[]{:S(2)}, u32[]{:S(2)}) %collective-permute-start.2) | collective-permute-done | bytes 65568 | tf_op jit(solution)/shard_map/ppermute | solution.py:21
  19.0 2.5 %collective-permute-start.4 = (bf16[1024,128]{1,0:T(8,128)(2,1)S(1)}, bf16[1024,128]{1,0:T(8,128)(2,1)S(1)}, u32[]{:S(2)}, u32[]{:S(2)}) collective-permute-start(bf16[1024,128]{1,0:T(8,128)(2,1)S(1)} %shard_map.157.refs_0_), channel_id=1, source_target_pairs={{0,32},{1,33},{2,34},{3,35},{4,36},{5,37},{6,38},{7,39},{8,40},{9,... | collective-permute-start | bytes 786440 | tf_op jit(solution)/shard_map/ppermute | solution.py:21
  22.4 2.2 %copy-done = bf16[256,8192]{1,0:T(8,128)(2,1)S(1)} copy-done((bf16[256,8192]{1,0:T(8,128)(2,1)S(1)}, bf16[256,8192]{1,0:T(8,128)(2,1)}, u32[]{:S(2)}) %copy-start) | copy-done | bytes 4194328
  25.7 6.2 %collective-permute-done.4.refs_2_ = bf16[1024,128]{1,0:T(8,128)(2,1)S(1)} collective-permute-done((bf16[1024,128]{1,0:T(8,128)(2,1)S(1)}, bf16[1024,128]{1,0:T(8,128)(2,1)S(1)}, u32[]{:S(2)}, u32[]{:S(2)}) %collective-permute-start.4) | collective-permute-done | bytes 262176 | tf_op jit(solution)/shard_map/ppermute | solution.py:21
  32.0 2.8 %collective-permute-done.5.refs_3_ = bf16[1024,128]{1,0:T(8,128)(2,1)S(1)} collective-permute-done((bf16[1024,128]{1,0:T(8,128)(2,1)S(1)}, bf16[1024,128]{1,0:T(8,128)(2,1)S(1)}, u32[]{:S(2)}, u32[]{:S(2)}) %collective-permute-start.5) | collective-permute-done | bytes 262176 | tf_op jit(solution)/shard_map/ppermute | solution.py:21
  34.9 2.3 %collective-permute-start.7 = (bf16[4096,128]{1,0:T(8,128)(2,1)S(1)}, bf16[4096,128]{1,0:T(8,128)(2,1)S(1)}, u32[]{:S(2)}, u32[]{:S(2)}) collective-permute-start(bf16[4096,128]{1,0:T(8,128)(2,1)S(1)} %shard_map.159), channel_id=1, source_target_pairs={{0,8},{1,9},{2,10},{3,11},{4,12},{5,13},{6,14},{7,15},{8,0},{9,1},... | collective-permute-start | bytes 3145736 | tf_op jit(solution)/shard_map/ppermute | solution.py:21
  37.8 1.6 collective-permute-done.7
  42.0 2.4 %collective-permute-done.8.refs_1_ = bf16[128,256]{1,0:T(8,128)(2,1)S(1)} collective-permute-done((bf16[128,256]{1,0:T(8,128)(2,1)S(1)}, bf16[128,256]{1,0:T(8,128)(2,1)S(1)}, u32[]{:S(2)}, u32[]{:S(2)}) %collective-permute-start.8) | collective-permute-done | bytes 65568 | tf_op jit(solution)/shard_map/ppermute | solution.py:21
  44.4 3.0 %collective-permute-start.10 = (bf16[256,256]{1,0:T(8,128)(2,1)S(1)}, bf16[256,256]{1,0:T(8,128)(2,1)S(1)}, u32[]{:S(2)}, u32[]{:S(2)}) collective-permute-start(bf16[256,256]{1,0:T(8,128)(2,1)S(1)} %shard_map.160.refs_0_), channel_id=1, source_target_pairs={{0,4},{1,5},{2,6},{3,7},{4,0},{5,1},{6,2},{7,3},{8,12},{9,13},{10,... | collective-permute-start | bytes 393224 | tf_op jit(solution)/shard_map/ppermute | solution.py:21
  48.2 1.6 collective-permute-done.10.refs_2_
  49.8 3.4 %collective-permute-done.11.refs_3_ = bf16[256,256]{1,0:T(8,128)(2,1)S(1)} collective-permute-done((bf16[256,256]{1,0:T(8,128)(2,1)S(1)}, bf16[256,256]{1,0:T(8,128)(2,1)S(1)}, u32[]{:S(2)}, u32[]{:S(2)}) %collective-permute-start.11) | collective-permute-done | bytes 131104 | tf_op jit(solution)/shard_map/ppermute | solution.py:21
  53.3 2.3 %collective-permute-start.14 = (bf16[1024,256]{1,0:T(8,128)(2,1)S(1)}, bf16[1024,256]{1,0:T(8,128)(2,1)S(1)}, u32[]{:S(2)}, u32[]{:S(2)}) collective-permute-start(bf16[1024,256]{1,0:T(8,128)(2,1)S(1)} %shard_map.162.refs_1_), channel_id=1, source_target_pairs={{0,8},{1,9},{2,10},{3,11},{4,12},{5,13},{6,14},{7,15},{8,0},{9,1},... | collective-permute-start | bytes 1572872 | tf_op jit(solution)/shard_map/ppermute | solution.py:21
  55.8 1.3 collective-permute-done.14.refs_2_
  57.1 1.4 shard_map.164.refs_4_
  60.1 4.5 %collective-permute-start.16 = (bf16[512,512]{1,0:T(8,128)(2,1)S(1)}, bf16[512,512]{1,0:T(8,128)(2,1)S(1)}, u32[]{:S(2)}, u32[]{:S(2)}) collective-permute-start(bf16[512,512]{1,0:T(8,128)(2,1)S(1)} %shard_map.165), channel_id=1, source_target_pairs={{0,64},{1,65},{2,66},{3,67},{4,68},{5,69},{6,70},{7,71},{8,200},{9... | collective-permute-start | bytes 1572872 | tf_op jit(solution)/shard_map/ppermute | solution.py:21
  64.6 1.7 %shard_map.163 = (f32[512,1280]{1,0:T(8,128)S(1)}, f32[512,512]{1,0:T(8,128)S(1)}) custom-call(s32[16]{0:T(128)S(1)} %pad_add_fusion.refs_0_, bf16[1024,256]{1,0:T(8,128)(2,1)S(1)} %shard_map.162.refs_1_, bf16[1024,256]{1,0:T(8,128)(2,1)S(1)} %collective-permute-done.14.refs_2_, bf16[512,1792]{1,0:T(8,128)(2,1)S(1)} %pad_maximum_fusion.refs_3_), custom_call_target="tpu_custom_call" | custom-call | flops 939524096 | bytes 6553664 | tf_op jit(solution)/shard_map/pallas_call | solution.py:63
  66.3 9.8 %collective-permute-done.16.refs_3_ = bf16[512,512]{1,0:T(8,128)(2,1)S(1)} collective-permute-done((bf16[512,512]{1,0:T(8,128)(2,1)S(1)}, bf16[512,512]{1,0:T(8,128)(2,1)S(1)}, u32[]{:S(2)}, u32[]{:S(2)}) %collective-permute-start.16) | collective-permute-done | bytes 524320 | tf_op jit(solution)/shard_map/ppermute | solution.py:21
  77.0 1.4 collective-permute-start.18
  78.4 4.1 %collective-permute-start.19 = (f32[8,128]{1,0:T(8,128)S(1)}, f32[8,128]{1,0:T(8,128)S(1)}, u32[]{:S(2)}, u32[]{:S(2)}) collective-permute-start(f32[8,128]{1,0:T(8,128)S(1)} %get-tuple-element.47), channel_id=1, source_target_pairs={{0,8},{1,9},{2,10},{3,11},{4,12},{5,13},{6,14},{7,15},{8,0},{9,1},... | collective-permute-start | bytes 12296 | tf_op jit(solution)/shard_map/ppermute | solution.py:21
  83.3 3.1 %collective-permute-done.18.refs_3_ = bf16[256,512]{1,0:T(8,128)(2,1)S(1)} collective-permute-done((bf16[256,512]{1,0:T(8,128)(2,1)S(1)}, bf16[256,512]{1,0:T(8,128)(2,1)S(1)}, u32[]{:S(2)}, u32[]{:S(2)}) %collective-permute-start.18) | collective-permute-done | bytes 262176 | tf_op jit(solution)/shard_map/ppermute | solution.py:21
  86.9 4.5 %collective-permute-start.20 = (bf16[128,1280]{1,0:T(8,128)(2,1)S(1)}, bf16[128,1280]{1,0:T(8,128)(2,1)S(1)}, u32[]{:S(2)}, u32[]{:S(2)}) collective-permute-start(bf16[128,1280]{1,0:T(8,128)(2,1)S(1)} %get-tuple-element.50), channel_id=1, source_target_pairs={{0,64},{1,65},{2,66},{3,67},{4,68},{5,69},{6,70},{7,71},{8,200},{9... | collective-permute-start | bytes 983048 | tf_op jit(solution)/shard_map/ppermute | solution.py:21
  91.4 1.8 %collective-permute-start.21 = (bf16[128,512]{1,0:T(8,128)(2,1)S(1)}, bf16[128,512]{1,0:T(8,128)(2,1)S(1)}, u32[]{:S(2)}, u32[]{:S(2)}) collective-permute-start(bf16[128,512]{1,0:T(8,128)(2,1)S(1)} %get-tuple-element.51), channel_id=1, source_target_pairs={{0,16},{1,17},{2,18},{3,19},{4,20},{5,21},{6,22},{7,23},{8,56},{9,... | collective-permute-start | bytes 393224 | tf_op jit(solution)/shard_map/ppermute | solution.py:21
  93.2 1.3 fusion.8.refs_7_.refs_1_
  94.6 2.1 %collective-permute-done.21.refs_3_ = bf16[128,512]{1,0:T(8,128)(2,1)S(1)} collective-permute-done((bf16[128,512]{1,0:T(8,128)(2,1)S(1)}, bf16[128,512]{1,0:T(8,128)(2,1)S(1)}, u32[]{:S(2)}, u32[]{:S(2)}) %collective-permute-start.21) | collective-permute-done | bytes 131104 | tf_op jit(solution)/shard_map/ppermute | solution.py:21
  96.7 2.0 %collective-permute-done.20.refs_2_ = bf16[128,1280]{1,0:T(8,128)(2,1)S(1)} collective-permute-done((bf16[128,1280]{1,0:T(8,128)(2,1)S(1)}, bf16[128,1280]{1,0:T(8,128)(2,1)S(1)}, u32[]{:S(2)}, u32[]{:S(2)}) %collective-permute-start.20) | collective-permute-done | bytes 327712 | tf_op jit(solution)/shard_map/ppermute | solution.py:21
  98.8 1.8 %collective-permute-start.23 = (bf16[64,1280]{1,0:T(8,128)(2,1)S(1)}, bf16[64,1280]{1,0:T(8,128)(2,1)S(1)}, u32[]{:S(2)}, u32[]{:S(2)}) collective-permute-start(bf16[64,1280]{1,0:T(8,128)(2,1)S(1)} %get-tuple-element.55), channel_id=1, source_target_pairs={{0,192},{1,193},{2,194},{3,195},{4,196},{5,197},{6,198},{7,199},{8... | collective-permute-start | bytes 491528 | tf_op jit(solution)/shard_map/ppermute | solution.py:21
  101.2 7.1 %collective-permute-start.25 = (f32[8,128]{1,0:T(8,128)S(1)}, f32[8,128]{1,0:T(8,128)S(1)}, u32[]{:S(2)}, u32[]{:S(2)}) collective-permute-start(f32[8,128]{1,0:T(8,128)S(1)} %get-tuple-element.60), channel_id=1, source_target_pairs={{0,8},{1,9},{2,10},{3,11},{4,12},{5,13},{6,14},{7,15},{8,0},{9,1},... | collective-permute-start | bytes 12296 | tf_op jit(solution)/shard_map/ppermute | solution.py:21
  110.1 1.5 collective-permute-start.26
  112.1 3.0 %collective-permute-done.28.refs_3_ = bf16[64,512]{1,0:T(8,128)(2,1)S(1)} collective-permute-done((bf16[64,512]{1,0:T(8,128)(2,1)S(1)}, bf16[64,512]{1,0:T(8,128)(2,1)S(1)}, u32[]{:S(2)}, u32[]{:S(2)}) %collective-permute-start.28) | collective-permute-done | bytes 65568 | tf_op jit(solution)/shard_map/ppermute | solution.py:21
  115.1 2.8 %collective-permute-done.27.refs_1_ = bf16[64,1280]{1,0:T(8,128)(2,1)S(1)} collective-permute-done((bf16[64,1280]{1,0:T(8,128)(2,1)S(1)}, bf16[64,1280]{1,0:T(8,128)(2,1)S(1)}, u32[]{:S(2)}, u32[]{:S(2)}) %collective-permute-start.27) | collective-permute-done | bytes 163872 | tf_op jit(solution)/shard_map/ppermute | solution.py:21
  118.0 1.7 %collective-permute-start.29 = (bf16[128,1280]{1,0:T(8,128)(2,1)S(1)}, bf16[128,1280]{1,0:T(8,128)(2,1)S(1)}, u32[]{:S(2)}, u32[]{:S(2)}) collective-permute-start(bf16[128,1280]{1,0:T(8,128)(2,1)S(1)} %get-tuple-element.67.refs_0_), channel_id=1, source_target_pairs={{0,64},{1,65},{2,66},{3,67},{4,68},{5,69},{6,70},{7,71},{8,200},{9... | collective-permute-start | bytes 983048 | tf_op jit(solution)/shard_map/ppermute | solution.py:21
  119.7 1.9 %collective-permute-start.30 = (bf16[128,512]{1,0:T(8,128)(2,1)S(1)}, bf16[128,512]{1,0:T(8,128)(2,1)S(1)}, u32[]{:S(2)}, u32[]{:S(2)}) collective-permute-start(bf16[128,512]{1,0:T(8,128)(2,1)S(1)} %get-tuple-element.68.refs_2_), channel_id=1, source_target_pairs={{0,16},{1,17},{2,18},{3,19},{4,20},{5,21},{6,22},{7,23},{8,56},{9,... | collective-permute-start | bytes 393224 | tf_op jit(solution)/shard_map/ppermute | solution.py:21
  123.3 1.6 collective-permute-done.30.refs_3_
  124.9 2.5 %collective-permute-done.29.refs_1_ = bf16[128,1280]{1,0:T(8,128)(2,1)S(1)} collective-permute-done((bf16[128,1280]{1,0:T(8,128)(2,1)S(1)}, bf16[128,1280]{1,0:T(8,128)(2,1)S(1)}, u32[]{:S(2)}, u32[]{:S(2)}) %collective-permute-start.29) | collective-permute-done | bytes 327712 | tf_op jit(solution)/shard_map/ppermute | solution.py:21
  127.5 1.8 %collective-permute-start.32 = (bf16[256,1280]{1,0:T(8,128)(2,1)S(1)}, bf16[256,1280]{1,0:T(8,128)(2,1)S(1)}, u32[]{:S(2)}, u32[]{:S(2)}) collective-permute-start(bf16[256,1280]{1,0:T(8,128)(2,1)S(1)} %get-tuple-element.71.refs_0_), channel_id=1, source_target_pairs={{0,48},{1,49},{2,50},{3,51},{4,52},{5,53},{6,54},{7,55},{8,24},{9,... | collective-permute-start | bytes 1966088 | tf_op jit(solution)/shard_map/ppermute | solution.py:21
  130.3 5.1 %collective-permute-start.34 = (f32[8,128]{1,0:T(8,128)S(1)}, f32[8,128]{1,0:T(8,128)S(1)}, u32[]{:S(2)}, u32[]{:S(2)}) collective-permute-start(f32[8,128]{1,0:T(8,128)S(1)} %get-tuple-element.73), channel_id=1, source_target_pairs={{0,8},{1,9},{2,10},{3,11},{4,12},{5,13},{6,14},{7,15},{8,0},{9,1},... | collective-permute-start | bytes 12296 | tf_op jit(solution)/shard_map/ppermute | solution.py:21
  136.2 2.3 %collective-permute-done.33.refs_3_ = bf16[256,512]{1,0:T(8,128)(2,1)S(1)} collective-permute-done((bf16[256,512]{1,0:T(8,128)(2,1)S(1)}, bf16[256,512]{1,0:T(8,128)(2,1)S(1)}, u32[]{:S(2)}, u32[]{:S(2)}) %collective-permute-start.33) | collective-permute-done | bytes 262176 | tf_op jit(solution)/shard_map/ppermute | solution.py:21
  138.6 4.1 %collective-permute-start.35 = (bf16[512,1280]{1,0:T(8,128)(2,1)S(1)}, bf16[512,1280]{1,0:T(8,128)(2,1)S(1)}, u32[]{:S(2)}, u32[]{:S(2)}) collective-permute-start(bf16[512,1280]{1,0:T(8,128)(2,1)S(1)} %get-tuple-element.74.refs_2_), channel_id=1, source_target_pairs={{0,16},{1,17},{2,18},{3,19},{4,20},{5,21},{6,22},{7,23},{8,56},{9,... | collective-permute-start | bytes 3932168 | tf_op jit(solution)/shard_map/ppermute | solution.py:21
  143.2 2.3 %collective-permute-start.37 = (f32[8,128]{1,0:T(8,128)S(1)}, f32[8,128]{1,0:T(8,128)S(1)}, u32[]{:S(2)}, u32[]{:S(2)}) collective-permute-start(f32[8,128]{1,0:T(8,128)S(1)} %get-tuple-element.76), channel_id=1, source_target_pairs={{0,8},{1,9},{2,10},{3,11},{4,12},{5,13},{6,14},{7,15},{8,0},{9,1},... | collective-permute-start | bytes 12296 | tf_op jit(solution)/shard_map/ppermute | solution.py:21
  147.5 11.1 %collective-permute-done.36.refs_3_ = bf16[512,512]{1,0:T(8,128)(2,1)S(1)} collective-permute-done((bf16[512,512]{1,0:T(8,128)(2,1)S(1)}, bf16[512,512]{1,0:T(8,128)(2,1)S(1)}, u32[]{:S(2)}, u32[]{:S(2)}) %collective-permute-start.36) | collective-permute-done | bytes 524320 | tf_op jit(solution)/shard_map/ppermute | solution.py:21
  159.2 3.2 %collective-permute-start.38 = (bf16[256,1792]{1,0:T(8,128)(2,1)S(1)}, bf16[256,1792]{1,0:T(8,128)(2,1)S(1)}, u32[]{:S(2)}, u32[]{:S(2)}) collective-permute-start(bf16[256,1792]{1,0:T(8,128)(2,1)S(1)} %shard_map.178), channel_id=1, source_target_pairs={{0,8},{1,9},{2,10},{3,11},{4,12},{5,13},{6,14},{7,15},{8,0},{9,1},... | collective-permute-start | bytes 2752520 | tf_op jit(solution)/shard_map/ppermute | solution.py:21
  163.0 1.4 collective-permute-done.38
  164.5 1.6 maximum_select_fusion
  (93 shorter events, 24.3 us)
Async XLA Ops:
  0.6 11.5 %copy-start.6 = (s32[16]{0:T(128)S(1)}, s32[16]{0:T(128)}, u32[]{:S(2)}) copy-start(s32[16]{0:T(128)} %constant.36.clone) | copy-start | bytes 196
  0.6 11.5 %copy-start.7 = (s32[16]{0:T(128)S(1)}, s32[16]{0:T(128)}, u32[]{:S(2)}) copy-start(s32[16]{0:T(128)} %constant.37.clone) | copy-start | bytes 196
  0.7 11.5 %copy-start.8 = (s32[16]{0:T(128)S(1)}, s32[16]{0:T(128)}, u32[]{:S(2)}) copy-start(s32[16]{0:T(128)} %constant.38.clone) | copy-start | bytes 196
  0.7 11.5 %copy-start.9 = (s32[16]{0:T(128)S(1)}, s32[16]{0:T(128)}, u32[]{:S(2)}) copy-start(s32[16]{0:T(128)} %constant.39.clone) | copy-start | bytes 196
  0.7 5.0 %copy-start.3 = (bf16[256,1024]{1,0:T(8,128)(2,1)S(1)}, bf16[256,1024]{1,0:T(8,128)(2,1)}, u32[]{:S(2)}) copy-start(bf16[256,1024]{1,0:T(8,128)(2,1)} %param.16) | copy-start | bytes 1572868
  2.3 32.5 %collective-permute-start.6 = (bf16[256,1792]{1,0:T(8,128)(2,1)S(1)}, bf16[256,1792]{1,0:T(8,128)(2,1)S(1)}, u32[]{:S(2)}, u32[]{:S(2)}) collective-permute-start(bf16[256,1792]{1,0:T(8,128)(2,1)S(1)} %get-tuple-element.78), channel_id=1, source_target_pairs={{0,8},{1,9},{2,10},{3,11},{4,12},{5,13},{6,14},{7,15},{8,0},{9,1},... | collective-permute-start | bytes 2752520 | tf_op jit(solution)/shard_map/ppermute | solution.py:21
  5.7 8.6 %collective-permute-start = (bf16[256,128]{1,0:T(8,128)(2,1)S(1)}, bf16[256,128]{1,0:T(8,128)(2,1)S(1)}, u32[]{:S(2)}, u32[]{:S(2)}) collective-permute-start(bf16[256,128]{1,0:T(8,128)(2,1)S(1)} %constant_dynamic-slice_fusion.2.refs_0_), channel_id=1, source_target_pairs={{0,64},{1,65},{2,66},{3,67},{4,68},{5,69},{6,70},{7,71},{8,72},{9,... | collective-permute-start | bytes 196616 | tf_op jit(solution)/shard_map/ppermute | solution.py:21
  7.0 8.8 %collective-permute-start.1 = (bf16[256,128]{1,0:T(8,128)(2,1)S(1)}, bf16[256,128]{1,0:T(8,128)(2,1)S(1)}, u32[]{:S(2)}, u32[]{:S(2)}) collective-permute-start(bf16[256,128]{1,0:T(8,128)(2,1)S(1)} %constant_dynamic-slice_fusion.2.refs_0_), channel_id=1, source_target_pairs={{0,128},{1,129},{2,130},{3,131},{4,132},{5,133},{6,134},{7,135},{8... | collective-permute-start | bytes 196616 | tf_op jit(solution)/shard_map/ppermute | solution.py:21
  12.1 5.5 %collective-permute-start.2 = (bf16[256,128]{1,0:T(8,128)(2,1)S(1)}, bf16[256,128]{1,0:T(8,128)(2,1)S(1)}, u32[]{:S(2)}, u32[]{:S(2)}) collective-permute-start(bf16[256,128]{1,0:T(8,128)(2,1)S(1)} %constant_dynamic-slice_fusion.2.refs_0_), channel_id=1, source_target_pairs={{0,192},{1,193},{2,194},{3,195},{4,196},{5,197},{6,198},{7,199},{8... | collective-permute-start | bytes 196616 | tf_op jit(solution)/shard_map/ppermute | solution.py:21
  17.7 8.0 %collective-permute-start.3 = (bf16[1024,128]{1,0:T(8,128)(2,1)S(1)}, bf16[1024,128]{1,0:T(8,128)(2,1)S(1)}, u32[]{:S(2)}, u32[]{:S(2)}) collective-permute-start(bf16[1024,128]{1,0:T(8,128)(2,1)S(1)} %shard_map.157.refs_0_), channel_id=1, source_target_pairs={{0,16},{1,17},{2,18},{3,19},{4,20},{5,21},{6,22},{7,23},{8,24},{9,... | collective-permute-start | bytes 786440 | tf_op jit(solution)/shard_map/ppermute | solution.py:21
  19.0 13.0 %collective-permute-start.4 = (bf16[1024,128]{1,0:T(8,128)(2,1)S(1)}, bf16[1024,128]{1,0:T(8,128)(2,1)S(1)}, u32[]{:S(2)}, u32[]{:S(2)}) collective-permute-start(bf16[1024,128]{1,0:T(8,128)(2,1)S(1)} %shard_map.157.refs_0_), channel_id=1, source_target_pairs={{0,32},{1,33},{2,34},{3,35},{4,36},{5,37},{6,38},{7,39},{8,40},{9,... | collective-permute-start | bytes 786440 | tf_op jit(solution)/shard_map/ppermute | solution.py:21
  21.4 13.4 %collective-permute-start.5 = (bf16[1024,128]{1,0:T(8,128)(2,1)S(1)}, bf16[1024,128]{1,0:T(8,128)(2,1)S(1)}, u32[]{:S(2)}, u32[]{:S(2)}) collective-permute-start(bf16[1024,128]{1,0:T(8,128)(2,1)S(1)} %shard_map.157.refs_0_), channel_id=1, source_target_pairs={{0,48},{1,49},{2,50},{3,51},{4,52},{5,53},{6,54},{7,55},{8,56},{9,... | collective-permute-start | bytes 786440 | tf_op jit(solution)/shard_map/ppermute | solution.py:21
  22.4 2.2 %copy-start = (bf16[256,8192]{1,0:T(8,128)(2,1)S(1)}, bf16[256,8192]{1,0:T(8,128)(2,1)}, u32[]{:S(2)}) copy-start(bf16[256,8192]{1,0:T(8,128)(2,1)} %refs_1_.2) | copy-start | bytes 12582916
  25.7 11.6 %copy-start.1 = (f32[32,3584]{1,0:T(8,128)S(1)}, f32[32,3584]{1,0:T(8,128)}, u32[]{:S(2)}) copy-start(f32[32,3584]{1,0:T(8,128)} %refs_1_.3) | copy-start | bytes 1376260
  25.7 11.5 %copy-start.2 = (f32[32,3584]{1,0:T(8,128)S(1)}, f32[32,3584]{1,0:T(8,128)}, u32[]{:S(2)}) copy-start(f32[32,3584]{1,0:T(8,128)} %refs_2_.1) | copy-start | bytes 1376260
  34.9 4.6 %collective-permute-start.7 = (bf16[4096,128]{1,0:T(8,128)(2,1)S(1)}, bf16[4096,128]{1,0:T(8,128)(2,1)S(1)}, u32[]{:S(2)}, u32[]{:S(2)}) collective-permute-start(bf16[4096,128]{1,0:T(8,128)(2,1)S(1)} %shard_map.159), channel_id=1, source_target_pairs={{0,8},{1,9},{2,10},{3,11},{4,12},{5,13},{6,14},{7,15},{8,0},{9,1},... | collective-permute-start | bytes 3145736 | tf_op jit(solution)/shard_map/ppermute | solution.py:21
  37.2 11.0 %collective-permute-start.13 = (bf16[256,1024]{1,0:T(8,128)(2,1)S(1)}, bf16[256,1024]{1,0:T(8,128)(2,1)S(1)}, u32[]{:S(2)}, u32[]{:S(2)}) collective-permute-start(bf16[256,1024]{1,0:T(8,128)(2,1)S(1)} %copy-done.3), channel_id=1, source_target_pairs={{0,8},{1,9},{2,10},{3,11},{4,12},{5,13},{6,14},{7,15},{8,0},{9,1},... | collective-permute-start | bytes 1572872 | tf_op jit(solution)/shard_map/ppermute | solution.py:21
  37.3 10.8 %collective-permute-start.12 = (f32[64,1792]{1,0:T(8,128)S(1)}, f32[64,1792]{1,0:T(8,128)S(1)}, u32[]{:S(2)}, u32[]{:S(2)}) collective-permute-start(f32[64,1792]{1,0:T(8,128)S(1)} %get-tuple-element.40), channel_id=1, source_target_pairs={{0,8},{1,9},{2,10},{3,11},{4,12},{5,13},{6,14},{7,15},{8,0},{9,1},... | collective-permute-start | bytes 1376264 | tf_op jit(solution)/shard_map/ppermute | solution.py:21
  40.3 15.3 %copy-start.5 = (s32[16]{0:T(128)S(1)}, s32[16]{0:T(128)}, u32[]{:S(2)}) copy-start(s32[16]{0:T(128)} %get-tuple-element.91) | copy-start | bytes 196
  41.2 3.2 %collective-permute-start.8 = (bf16[128,256]{1,0:T(8,128)(2,1)S(1)}, bf16[128,256]{1,0:T(8,128)(2,1)S(1)}, u32[]{:S(2)}, u32[]{:S(2)}) collective-permute-start(bf16[128,256]{1,0:T(8,128)(2,1)S(1)} %fusion.13.refs_0_), channel_id=1, source_target_pairs={{0,1},{1,0},{2,3},{3,2},{4,5},{5,4},{6,7},{7,6},{8,9},{9,8},{10,11... | collective-permute-start | bytes 196616 | tf_op jit(solution)/shard_map/ppermute | solution.py:21
  44.4 5.4 %collective-permute-start.10 = (bf16[256,256]{1,0:T(8,128)(2,1)S(1)}, bf16[256,256]{1,0:T(8,128)(2,1)S(1)}, u32[]{:S(2)}, u32[]{:S(2)}) collective-permute-start(bf16[256,256]{1,0:T(8,128)(2,1)S(1)} %shard_map.160.refs_0_), channel_id=1, source_target_pairs={{0,4},{1,5},{2,6},{3,7},{4,0},{5,1},{6,2},{7,3},{8,12},{9,13},{10,... | collective-permute-start | bytes 393224 | tf_op jit(solution)/shard_map/ppermute | solution.py:21
  47.4 5.8 %collective-permute-start.11 = (bf16[256,256]{1,0:T(8,128)(2,1)S(1)}, bf16[256,256]{1,0:T(8,128)(2,1)S(1)}, u32[]{:S(2)}, u32[]{:S(2)}) collective-permute-start(bf16[256,256]{1,0:T(8,128)(2,1)S(1)} %shard_map.160.refs_0_), channel_id=1, source_target_pairs={{0,6},{1,7},{2,4},{3,5},{4,2},{5,3},{6,0},{7,1},{8,14},{9,15},{10,... | collective-permute-start | bytes 393224 | tf_op jit(solution)/shard_map/ppermute | solution.py:21
  48.1 5.1 %collective-permute-start.9 = (bf16[256,256]{1,0:T(8,128)(2,1)S(1)}, bf16[256,256]{1,0:T(8,128)(2,1)S(1)}, u32[]{:S(2)}, u32[]{:S(2)}) collective-permute-start(bf16[256,256]{1,0:T(8,128)(2,1)S(1)} %shard_map.160.refs_0_), channel_id=1, source_target_pairs={{0,2},{1,3},{2,0},{3,1},{4,6},{5,7},{6,4},{7,5},{8,10},{9,11},{10,... | collective-permute-start | bytes 393224 | tf_op jit(solution)/shard_map/ppermute | solution.py:21
  53.3 3.9 %collective-permute-start.14 = (bf16[1024,256]{1,0:T(8,128)(2,1)S(1)}, bf16[1024,256]{1,0:T(8,128)(2,1)S(1)}, u32[]{:S(2)}, u32[]{:S(2)}) collective-permute-start(bf16[1024,256]{1,0:T(8,128)(2,1)S(1)} %shard_map.162.refs_1_), channel_id=1, source_target_pairs={{0,8},{1,9},{2,10},{3,11},{4,12},{5,13},{6,14},{7,15},{8,0},{9,1},... | collective-permute-start | bytes 1572872 | tf_op jit(solution)/shard_map/ppermute | solution.py:21
  58.5 17.9 %collective-permute-start.15 = (bf16[512,1280]{1,0:T(8,128)(2,1)S(1)}, bf16[512,1280]{1,0:T(8,128)(2,1)S(1)}, u32[]{:S(2)}, u32[]{:S(2)}) collective-permute-start(bf16[512,1280]{1,0:T(8,128)(2,1)S(1)} %shard_map.164.refs_4_), channel_id=1, source_target_pairs={{0,16},{1,17},{2,18},{3,19},{4,20},{5,21},{6,22},{7,23},{8,56},{9,... | collective-permute-start | bytes 3932168 | tf_op jit(solution)/shard_map/ppermute | solution.py:21
  60.1 16.0 %collective-permute-start.16 = (bf16[512,512]{1,0:T(8,128)(2,1)S(1)}, bf16[512,512]{1,0:T(8,128)(2,1)S(1)}, u32[]{:S(2)}, u32[]{:S(2)}) collective-permute-start(bf16[512,512]{1,0:T(8,128)(2,1)S(1)} %shard_map.165), channel_id=1, source_target_pairs={{0,64},{1,65},{2,66},{3,67},{4,68},{5,69},{6,70},{7,71},{8,200},{9... | collective-permute-start | bytes 1572872 | tf_op jit(solution)/shard_map/ppermute | solution.py:21
  76.9 9.8 %collective-permute-start.17 = (bf16[256,1280]{1,0:T(8,128)(2,1)S(1)}, bf16[256,1280]{1,0:T(8,128)(2,1)S(1)}, u32[]{:S(2)}, u32[]{:S(2)}) collective-permute-start(bf16[256,1280]{1,0:T(8,128)(2,1)S(1)} %get-tuple-element.45), channel_id=1, source_target_pairs={{0,48},{1,49},{2,50},{3,51},{4,52},{5,53},{6,54},{7,55},{8,24},{9,... | collective-permute-start | bytes 1966088 | tf_op jit(solution)/shard_map/ppermute | solution.py:21
  77.0 9.4 %collective-permute-start.18 = (bf16[256,512]{1,0:T(8,128)(2,1)S(1)}, bf16[256,512]{1,0:T(8,128)(2,1)S(1)}, u32[]{:S(2)}, u32[]{:S(2)}) collective-permute-start(bf16[256,512]{1,0:T(8,128)(2,1)S(1)} %get-tuple-element.46), channel_id=1, source_target_pairs={{0,192},{1,193},{2,194},{3,195},{4,196},{5,197},{6,198},{7,199},{8... | collective-permute-start | bytes 786440 | tf_op jit(solution)/shard_map/ppermute | solution.py:21
  78.4 4.9 %collective-permute-start.19 = (f32[8,128]{1,0:T(8,128)S(1)}, f32[8,128]{1,0:T(8,128)S(1)}, u32[]{:S(2)}, u32[]{:S(2)}) collective-permute-start(f32[8,128]{1,0:T(8,128)S(1)} %get-tuple-element.47), channel_id=1, source_target_pairs={{0,8},{1,9},{2,10},{3,11},{4,12},{5,13},{6,14},{7,15},{8,0},{9,1},... | collective-permute-start | bytes 12296 | tf_op jit(solution)/shard_map/ppermute | solution.py:21
  86.9 11.8 %collective-permute-start.20 = (bf16[128,1280]{1,0:T(8,128)(2,1)S(1)}, bf16[128,1280]{1,0:T(8,128)(2,1)S(1)}, u32[]{:S(2)}, u32[]{:S(2)}) collective-permute-start(bf16[128,1280]{1,0:T(8,128)(2,1)S(1)} %get-tuple-element.50), channel_id=1, source_target_pairs={{0,64},{1,65},{2,66},{3,67},{4,68},{5,69},{6,70},{7,71},{8,200},{9... | collective-permute-start | bytes 983048 | tf_op jit(solution)/shard_map/ppermute | solution.py:21
  91.4 5.3 %collective-permute-start.21 = (bf16[128,512]{1,0:T(8,128)(2,1)S(1)}, bf16[128,512]{1,0:T(8,128)(2,1)S(1)}, u32[]{:S(2)}, u32[]{:S(2)}) collective-permute-start(bf16[128,512]{1,0:T(8,128)(2,1)S(1)} %get-tuple-element.51), channel_id=1, source_target_pairs={{0,16},{1,17},{2,18},{3,19},{4,20},{5,21},{6,22},{7,23},{8,56},{9,... | collective-permute-start | bytes 393224 | tf_op jit(solution)/shard_map/ppermute | solution.py:21
  93.2 1.3 collective-permute-start.22
  98.8 10.9 %collective-permute-start.23 = (bf16[64,1280]{1,0:T(8,128)(2,1)S(1)}, bf16[64,1280]{1,0:T(8,128)(2,1)S(1)}, u32[]{:S(2)}, u32[]{:S(2)}) collective-permute-start(bf16[64,1280]{1,0:T(8,128)(2,1)S(1)} %get-tuple-element.55), channel_id=1, source_target_pairs={{0,192},{1,193},{2,194},{3,195},{4,196},{5,197},{6,198},{7,199},{8... | collective-permute-start | bytes 491528 | tf_op jit(solution)/shard_map/ppermute | solution.py:21
  100.6 9.0 %collective-permute-start.24 = (bf16[64,512]{1,0:T(8,128)(2,1)S(1)}, bf16[64,512]{1,0:T(8,128)(2,1)S(1)}, u32[]{:S(2)}, u32[]{:S(2)}) collective-permute-start(bf16[64,512]{1,0:T(8,128)(2,1)S(1)} %get-tuple-element.56), channel_id=1, source_target_pairs={{0,48},{1,49},{2,50},{3,51},{4,52},{5,53},{6,54},{7,55},{8,24},{9,... | collective-permute-start | bytes 196616 | tf_op jit(solution)/shard_map/ppermute | solution.py:21
  101.2 8.4 %collective-permute-start.25 = (f32[8,128]{1,0:T(8,128)S(1)}, f32[8,128]{1,0:T(8,128)S(1)}, u32[]{:S(2)}, u32[]{:S(2)}) collective-permute-start(f32[8,128]{1,0:T(8,128)S(1)} %get-tuple-element.60), channel_id=1, source_target_pairs={{0,8},{1,9},{2,10},{3,11},{4,12},{5,13},{6,14},{7,15},{8,0},{9,1},... | collective-permute-start | bytes 12296 | tf_op jit(solution)/shard_map/ppermute | solution.py:21
  110.1 7.8 %collective-permute-start.26 = (f32[64,1792]{1,0:T(8,128)S(1)}, f32[64,1792]{1,0:T(8,128)S(1)}, u32[]{:S(2)}, u32[]{:S(2)}) collective-permute-start(f32[64,1792]{1,0:T(8,128)S(1)} %shard_map.171), channel_id=1, source_target_pairs={{0,8},{1,9},{2,10},{3,11},{4,12},{5,13},{6,14},{7,15},{8,0},{9,1},... | collective-permute-start | bytes 1376264 | tf_op jit(solution)/shard_map/ppermute | solution.py:21
  111.7 6.3 %collective-permute-start.27 = (bf16[64,1280]{1,0:T(8,128)(2,1)S(1)}, bf16[64,1280]{1,0:T(8,128)(2,1)S(1)}, u32[]{:S(2)}, u32[]{:S(2)}) collective-permute-start(bf16[64,1280]{1,0:T(8,128)(2,1)S(1)} %get-tuple-element.65.refs_0_), channel_id=1, source_target_pairs={{0,192},{1,193},{2,194},{3,195},{4,196},{5,197},{6,198},{7,199},{8... | collective-permute-start | bytes 491528 | tf_op jit(solution)/shard_map/ppermute | solution.py:21
  112.0 3.1 %collective-permute-start.28 = (bf16[64,512]{1,0:T(8,128)(2,1)S(1)}, bf16[64,512]{1,0:T(8,128)(2,1)S(1)}, u32[]{:S(2)}, u32[]{:S(2)}) collective-permute-start(bf16[64,512]{1,0:T(8,128)(2,1)S(1)} %get-tuple-element.66.refs_2_), channel_id=1, source_target_pairs={{0,48},{1,49},{2,50},{3,51},{4,52},{5,53},{6,54},{7,55},{8,24},{9,... | collective-permute-start | bytes 196616 | tf_op jit(solution)/shard_map/ppermute | solution.py:21
  118.0 9.4 %collective-permute-start.29 = (bf16[128,1280]{1,0:T(8,128)(2,1)S(1)}, bf16[128,1280]{1,0:T(8,128)(2,1)S(1)}, u32[]{:S(2)}, u32[]{:S(2)}) collective-permute-start(bf16[128,1280]{1,0:T(8,128)(2,1)S(1)} %get-tuple-element.67.refs_0_), channel_id=1, source_target_pairs={{0,64},{1,65},{2,66},{3,67},{4,68},{5,69},{6,70},{7,71},{8,200},{9... | collective-permute-start | bytes 983048 | tf_op jit(solution)/shard_map/ppermute | solution.py:21
  119.7 5.2 %collective-permute-start.30 = (bf16[128,512]{1,0:T(8,128)(2,1)S(1)}, bf16[128,512]{1,0:T(8,128)(2,1)S(1)}, u32[]{:S(2)}, u32[]{:S(2)}) collective-permute-start(bf16[128,512]{1,0:T(8,128)(2,1)S(1)} %get-tuple-element.68.refs_2_), channel_id=1, source_target_pairs={{0,16},{1,17},{2,18},{3,19},{4,20},{5,21},{6,22},{7,23},{8,56},{9,... | collective-permute-start | bytes 393224 | tf_op jit(solution)/shard_map/ppermute | solution.py:21
  121.6 1.7 collective-permute-start.31
  127.5 11.0 %collective-permute-start.32 = (bf16[256,1280]{1,0:T(8,128)(2,1)S(1)}, bf16[256,1280]{1,0:T(8,128)(2,1)S(1)}, u32[]{:S(2)}, u32[]{:S(2)}) collective-permute-start(bf16[256,1280]{1,0:T(8,128)(2,1)S(1)} %get-tuple-element.71.refs_0_), channel_id=1, source_target_pairs={{0,48},{1,49},{2,50},{3,51},{4,52},{5,53},{6,54},{7,55},{8,24},{9,... | collective-permute-start | bytes 1966088 | tf_op jit(solution)/shard_map/ppermute | solution.py:21
  129.2 9.3 %collective-permute-start.33 = (bf16[256,512]{1,0:T(8,128)(2,1)S(1)}, bf16[256,512]{1,0:T(8,128)(2,1)S(1)}, u32[]{:S(2)}, u32[]{:S(2)}) collective-permute-start(bf16[256,512]{1,0:T(8,128)(2,1)S(1)} %get-tuple-element.72.refs_2_), channel_id=1, source_target_pairs={{0,192},{1,193},{2,194},{3,195},{4,196},{5,197},{6,198},{7,199},{8... | collective-permute-start | bytes 786440 | tf_op jit(solution)/shard_map/ppermute | solution.py:21
  130.3 5.9 %collective-permute-start.34 = (f32[8,128]{1,0:T(8,128)S(1)}, f32[8,128]{1,0:T(8,128)S(1)}, u32[]{:S(2)}, u32[]{:S(2)}) collective-permute-start(f32[8,128]{1,0:T(8,128)S(1)} %get-tuple-element.73), channel_id=1, source_target_pairs={{0,8},{1,9},{2,10},{3,11},{4,12},{5,13},{6,14},{7,15},{8,0},{9,1},... | collective-permute-start | bytes 12296 | tf_op jit(solution)/shard_map/ppermute | solution.py:21
  138.6 19.9 %collective-permute-start.35 = (bf16[512,1280]{1,0:T(8,128)(2,1)S(1)}, bf16[512,1280]{1,0:T(8,128)(2,1)S(1)}, u32[]{:S(2)}, u32[]{:S(2)}) collective-permute-start(bf16[512,1280]{1,0:T(8,128)(2,1)S(1)} %get-tuple-element.74.refs_2_), channel_id=1, source_target_pairs={{0,16},{1,17},{2,18},{3,19},{4,20},{5,21},{6,22},{7,23},{8,56},{9,... | collective-permute-start | bytes 3932168 | tf_op jit(solution)/shard_map/ppermute | solution.py:21
  142.7 15.9 %collective-permute-start.36 = (bf16[512,512]{1,0:T(8,128)(2,1)S(1)}, bf16[512,512]{1,0:T(8,128)(2,1)S(1)}, u32[]{:S(2)}, u32[]{:S(2)}) collective-permute-start(bf16[512,512]{1,0:T(8,128)(2,1)S(1)} %get-tuple-element.75.refs_3_), channel_id=1, source_target_pairs={{0,64},{1,65},{2,66},{3,67},{4,68},{5,69},{6,70},{7,71},{8,200},{9... | collective-permute-start | bytes 1572872 | tf_op jit(solution)/shard_map/ppermute | solution.py:21
  143.2 3.1 %collective-permute-start.37 = (f32[8,128]{1,0:T(8,128)S(1)}, f32[8,128]{1,0:T(8,128)S(1)}, u32[]{:S(2)}, u32[]{:S(2)}) collective-permute-start(f32[8,128]{1,0:T(8,128)S(1)} %get-tuple-element.76), channel_id=1, source_target_pairs={{0,8},{1,9},{2,10},{3,11},{4,12},{5,13},{6,14},{7,15},{8,0},{9,1},... | collective-permute-start | bytes 12296 | tf_op jit(solution)/shard_map/ppermute | solution.py:21
  159.2 5.3 %collective-permute-start.38 = (bf16[256,1792]{1,0:T(8,128)(2,1)S(1)}, bf16[256,1792]{1,0:T(8,128)(2,1)S(1)}, u32[]{:S(2)}, u32[]{:S(2)}) collective-permute-start(bf16[256,1792]{1,0:T(8,128)(2,1)S(1)} %shard_map.178), channel_id=1, source_target_pairs={{0,8},{1,9},{2,10},{3,11},{4,12},{5,13},{6,14},{7,15},{8,0},{9,1},... | collective-permute-start | bytes 2752520 | tf_op jit(solution)/shard_map/ppermute | solution.py:21
  (1 other events, 1.9 us)
